TPU v7x, 256 devices: a whole 4x4x8 slice. The times are simulated.
256 devices in a mesh: sample: 16 (over x_lo, y, core), seq: 16 (over z, x_hi).
Axes of the slice: x: 4 (x_hi: 2, x_lo: 2; x = x_hi * 2 + x_lo), y: 4, z: 8, core: 2. Of those that a mesh axis runs over, the one named last changes fastest.
Arguments:
- atom_feats: bfloat16 [32, 16384, 128], P('sample', 'seq'), may hold values from -6 to 6
- atom_token: int32 [16384], P('seq'), may hold values from 0 to 2047, as said below
- single_cond: bfloat16 [32, 2048, 384], P('sample', 'seq'), may hold values from -6 to 6
- pair_rep: bfloat16 [2048, 2048, 128], P('seq', 'sample'), may hold values from -6 to 6
- w_atom: bfloat16 [128, 768], replicated, may hold values from -0.5 to 0.5
- w_ada_gate: bfloat16 [384, 768], replicated, may hold values from -0.3125 to 0.3125
- w_ada_shift: bfloat16 [384, 768], replicated, may hold values from -0.3125 to 0.3125
- w_query: bfloat16 [768, 768], replicated, may hold values from -1 to 1
- w_key: bfloat16 [768, 768], replicated, may hold values from -32 to 32
- w_value: bfloat16 [768, 768], replicated, may hold values from -0.21875 to 0.21875
- w_pair: bfloat16 [128, 16], replicated, may hold values from -1 to 1
- w_out: bfloat16 [768, 768], replicated, may hold values from -0.875 to 0.875
- w_outgate: bfloat16 [384, 768], replicated, may hold values from -0.3125 to 0.3125
- outgate_bias: bfloat16 [768], replicated, may hold values from -6 to 6
Outputs:
- update: bfloat16 [32, 2048, 768], P('sample', 'seq')
Inputs may be any that keep to these rules, and one draw needn't show every extreme that they name: `atom_token`: sorted; every token has at least one atom; the atoms of one index p of seq belong to tokens of index p of seq and of index p + 1.
All inputs are finite; a program needn't handle non-finite values.
Results may differ from a plain program's by a relative error of at most 0.012.
The roundings to bfloat16 on the way count: a program that leaves them out, or rounds other values in their place, can miss the bound.
Values may be sent and summed in bfloat16 or wider, within the bound.
No kernel may reach another device: no remote copies, remote signals or barrier semaphores. Data moves between devices by JAX's collectives and lax.ppermute only.
A program may use at most 128 MiB of HBM per device.

v0:
```python
import math

import jax
import jax.numpy as jnp
from jax import lax
from jax.sharding import PartitionSpec as P


def from_behind(value, axis, steps):
    count = lax.axis_size(axis)
    initial, last = (max(0, -steps), min(count, count - steps))
    return lax.ppermute(value, axis, [(source, source + steps) for source in range(initial, last)])


def layer_norm(inputs):
    average = jnp.mean(inputs, axis=-1, keepdims=True)
    centered = inputs - average
    variance = jnp.mean(centered * centered, axis=-1, keepdims=True)
    return centered * lax.rsqrt(variance + 1e-05)


def per_device(
    atom_feats,
    atom_token,
    single_cond,
    pair_rep,
    w_atom,
    w_ada_gate,
    w_ada_shift,
    w_query,
    w_key,
    w_value,
    w_pair,
    w_out,
    w_outgate,
    outgate_bias,
):
    samp_local = atom_feats.shape[0]
    atom_local = atom_feats.shape[1]
    tok_local = single_cond.shape[1]
    model_width = w_query.shape[1]
    head_count = w_pair.shape[1]
    head_size = model_width // head_count
    seq_count = lax.axis_size("seq")
    seq_place = lax.axis_index("seq")
    total_tokens = tok_local * seq_count
    normed_pair = layer_norm(pair_rep.astype(jnp.float32)).astype(jnp.bfloat16)
    bias_local = jnp.einsum(
        "ijc,ch->hij", normed_pair, w_pair, preferred_element_type=jnp.float32
    ).astype(jnp.bfloat16)
    pair_bias = lax.all_gather(bias_local, "sample", axis=2, tiled=True)
    hidden = jax.nn.relu(
        jnp.einsum("sac,cd->sad", atom_feats, w_atom, preferred_element_type=jnp.float32)
    ).astype(jnp.bfloat16)
    relative = atom_token - seq_place * tok_local
    slot_ids = lax.broadcasted_iota(jnp.int32, (2 * tok_local, atom_local), 0)
    member = slot_ids == relative[None, :]
    partial_value = jnp.einsum(
        "ta,sad->std", member.astype(jnp.bfloat16), hidden, preferred_element_type=jnp.float32
    )
    counts = jnp.sum(member.astype(jnp.float32), axis=1)[None, :]
    rounded = partial_value.astype(jnp.bfloat16)
    count_rounded = counts.astype(jnp.bfloat16)
    below_part, below_count = from_behind(
        (rounded[:, tok_local:], count_rounded[:, tok_local:]), "seq", 1
    )
    summed = rounded[:, :tok_local].astype(jnp.float32) + below_part.astype(jnp.float32)
    token_counts = counts[:, :tok_local] + below_count.astype(jnp.float32)
    tokens = summed / token_counts[:, :, None]
    cond = layer_norm(single_cond.astype(jnp.float32)).astype(jnp.bfloat16)
    gate_ada = jax.nn.sigmoid(
        jnp.einsum("stc,cd->std", cond, w_ada_gate, preferred_element_type=jnp.float32)
    )
    shift_ada = jnp.einsum("stc,cd->std", cond, w_ada_shift, preferred_element_type=jnp.float32)
    normed = (gate_ada * layer_norm(tokens) + shift_ada).astype(jnp.bfloat16)
    queries = jnp.einsum("std,de->ste", normed, w_query, preferred_element_type=jnp.float32).astype(
        jnp.bfloat16
    )
    key_part = jnp.einsum("std,de->ste", normed, w_key, preferred_element_type=jnp.float32).astype(
        jnp.bfloat16
    )
    value_part = jnp.einsum(
        "std,de->ste", normed, w_value, preferred_element_type=jnp.float32
    ).astype(jnp.bfloat16)
    local_pair = jnp.stack([key_part, value_part], axis=0)
    keys_all, values_all = (
        lax.all_gather(local_pair[0], "seq", axis=1, tiled=True),
        lax.all_gather(local_pair[1], "seq", axis=1, tiled=True),
    )
    scaling = 1.0 / math.sqrt(head_size)
    bias_float = pair_bias.astype(jnp.float32)
    outputs = []
    for sample_index in range(samp_local):
        query_heads = queries[sample_index].reshape(tok_local, head_count, head_size)
        key_heads = keys_all[sample_index].reshape(total_tokens, head_count, head_size)
        value_heads = values_all[sample_index].reshape(total_tokens, head_count, head_size)
        scores = (
            jnp.einsum("qhd,khd->hqk", query_heads, key_heads, preferred_element_type=jnp.float32)
            * scaling
            + bias_float
        )
        largest = jnp.max(scores, axis=-1, keepdims=True)
        exponent = jnp.exp(scores - largest)
        weights = (exponent / jnp.sum(exponent, axis=-1, keepdims=True)).astype(jnp.bfloat16)
        attended = jnp.einsum(
            "hqk,khd->qhd", weights, value_heads, preferred_element_type=jnp.float32
        ).astype(jnp.bfloat16)
        outputs.append(attended.reshape(tok_local, model_width))
    attended_all = jnp.stack(outputs, axis=0)
    out_gate = jax.nn.sigmoid(
        jnp.einsum("std,de->ste", cond, w_outgate, preferred_element_type=jnp.float32)
        + outgate_bias.astype(jnp.float32)
    )
    mixed_out = jnp.einsum("std,de->ste", attended_all, w_out, preferred_element_type=jnp.float32)
    return (out_gate * mixed_out).astype(jnp.bfloat16)


def solution(mesh):
    return jax.shard_map(
        per_device,
        mesh=mesh,
        in_specs=(
            P("sample", "seq", None),
            P("seq"),
            P("sample", "seq", None),
            P("seq", "sample", None),
            P(),
            P(),
            P(),
            P(),
            P(),
            P(),
            P(),
            P(),
            P(),
            P(),
        ),
        out_specs=P("sample", "seq", None),
        check_vma=False,
    )
```

profile of v0, /device:TPU:1, one launch (start us, length us, event | category | flops | bytes accessed | tf_op | source)
XLA Modules:
  0.0 380.4 jit_solution(15206672385938164830)
XLA Ops:
  6.5 0.8 broadcast_subtract_fusion
  7.5 5.5 %collective-permute-start.1 = (bf16[1,128]{1,0:T(2,128)(2,1)S(1)}, bf16[1,128]{1,0:T(2,128)(2,1)S(1)}, u32[]{:S(2)}, u32[]{:S(2)}) collective-permute-start(bf16[1,128]{1,0:T(2,128)(2,1)S(1)} %slice.61), channel_id=1, source_target_pairs={{0,1},{1,2},{2,3},{3,4},{4,5},{5,6},{6,7},{7,8},{8,9},{9,10},{10,1... | collective-permute-start | bytes 776 | tf_op jit(solution)/shard_map/ppermute | solution.py:12
  13.0 2.9 fusion.33
  16.0 3.5 collective-permute-start
  19.9 1.7 fusion.29
  21.5 5.4 %collective-permute-done = bf16[2,128,768]{2,1,0:T(8,128)(2,1)S(1)} collective-permute-done((bf16[2,128,768]{2,1,0:T(8,128)(2,1)S(1)}, bf16[2,128,768]{2,1,0:T(8,128)(2,1)S(1)}, u32[]{:S(2)}, u32[]{:S(2)}) %collective-permute-start) | collective-permute-done | bytes 393248 | tf_op jit(solution)/shard_map/ppermute | solution.py:12
  26.9 0.2 fusion.74
  27.2 0.3 multiply_reduce_fusion
  27.5 1.6 fusion.35
  29.1 1.2 convolution_convert_fusion.2
  30.4 1.3 convolution_convert_fusion
  31.7 0.2 all-gather.8.cloned.1.call-start
  31.9 3.5 convert_reduce_fusion
  35.5 4.8 %fusion.6 = f32[128,128]{1,0:T(8,128)S(1)} fusion(bf16[128,128,128]{2,1,0:T(8,128)(2,1)S(1)} %copy-done.1, f32[128,128]{1,0:T(8,128)S(1)} %broadcast_multiply_fusion), kind=kLoop, calls=%fused_computation.14 | loop fusion | flops 8372224 | bytes 4325376 | tf_op jit(solution)/shard_map/reduce_sum | solution.py:18
  40.3 5.8 %fusion.12 = bf16[128,128,16]{1,2,0:T(8,128)(2,1)S(1)} fusion(bf16[128,128,128]{2,1,0:T(8,128)(2,1)S(1)} %copy-done.1, f32[128,128]{1,0:T(8,128)S(1)} %add_rsqrt_fusion, f32[128,128]{1,0:T(8,128)S(1)} %broadcast_multiply_fusion, bf16[128,16]{0,1:T(8,128)(2,1)S(1)} %copy-done.8), kind=kOutput, calls=%fused_computation.21 | convolution fusion | flops 75497472 | bytes 4853760 | tf_op jit(solution)/shard_map/ijc,ch->hij/dot_general | solution.py:48
  46.1 0.9 copy.39
  47.1 0.5 convolution_convert_fusion.1
  48.0 103.3 %all-gather.4.cloned.1.call-done = bf16[2,2048,768]{2,1,0:T(8,128)(2,1)} async-done(((bf16[2,128,768]{2,1,0:T(8,128)(2,1)}), bf16[2,2048,768]{2,1,0:T(8,128)(2,1)}) %all-gather.4.cloned.1.call-update) | async-done | bytes 6291472 | tf_op jit(solution)/shard_map/all_gather | solution.py:88
  151.3 5.9 %fusion.76 = (bf16[1,2048,768]{2,1,0:T(8,128)(2,1)}, bf16[1,2048,768]{2,1,0:T(8,128)(2,1)}) fusion(bf16[2,2048,768]{2,1,0:T(8,128)(2,1)} %all-gather.4.cloned.1.call-done), kind=kLoop, calls=%fused_computation.96 | loop fusion | bytes 12582912 | tf_op jit(solution)/shard_map/slice | solution.py:96
  157.2 4.7 %copy.30 = bf16[1,2048,768]{1,2,0:T(8,128)(2,1)} copy(bf16[1,2048,768]{2,1,0:T(8,128)(2,1)} %get-tuple-element.8) | data formatting | bytes 6291456 | tf_op jit(solution)/shard_map/slice | solution.py:96
  162.0 104.9 %all-gather.6.cloned.1.call-done = bf16[2,2048,768]{2,1,0:T(8,128)(2,1)} async-done(((bf16[2,128,768]{2,1,0:T(8,128)(2,1)}), bf16[2,2048,768]{2,1,0:T(8,128)(2,1)}) %all-gather.6.cloned.1.call-update) | async-done | bytes 6291472 | tf_op jit(solution)/shard_map/all_gather | solution.py:87
  266.8 5.9 %fusion.75 = (bf16[1,2048,768]{2,1,0:T(8,128)(2,1)}, bf16[1,2048,768]{2,1,0:T(8,128)(2,1)}) fusion(bf16[2,2048,768]{2,1,0:T(8,128)(2,1)} %all-gather.6.cloned.1.call-done), kind=kLoop, calls=%fused_computation.95 | loop fusion | bytes 12582912 | tf_op jit(solution)/shard_map/slice | solution.py:95
  272.8 4.7 %copy.32 = bf16[1,2048,768]{1,2,0:T(8,128)(2,1)} copy(bf16[1,2048,768]{2,1,0:T(8,128)(2,1)} %get-tuple-element.6) | data formatting | bytes 6291456 | tf_op jit(solution)/shard_map/slice | solution.py:95
  277.5 4.7 %copy.26 = bf16[1,2048,768]{1,2,0:T(8,128)(2,1)} copy(bf16[1,2048,768]{2,1,0:T(8,128)(2,1)} %get-tuple-element.7) | data formatting | bytes 6291456 | tf_op jit(solution)/shard_map/slice | solution.py:96
  282.2 4.7 %copy.28 = bf16[1,2048,768]{1,2,0:T(8,128)(2,1)} copy(bf16[1,2048,768]{2,1,0:T(8,128)(2,1)} %get-tuple-element.5) | data formatting | bytes 6291456 | tf_op jit(solution)/shard_map/slice | solution.py:95
  286.9 45.2 %all-gather.8.cloned.1.call-done = bf16[16,128,2048]{2,1,0:T(8,128)(2,1)} async-done(((bf16[16,128,128]{2,1,0:T(8,128)(2,1)}), bf16[16,128,2048]{2,1,0:T(8,128)(2,1)}) %all-gather.8.cloned.1.call-update) | async-done | bytes 8388624 | tf_op jit(solution)/shard_map/all_gather | solution.py:51
  332.0 8.4 %fusion.78 = f32[16,128]{1,0:T(8,128)S(1)} fusion(bf16[16,128,2048]{2,1,0:T(8,128)(2,1)} %all-gather.8.cloned.1.call-done, bf16[128,16,48]{0,2,1:T(8,128)(2,1)S(1)} %bitcast.74, bf16[2048,16,48]{0,2,1:T(8,128)(2,1)} %bitcast.69), kind=kOutput, calls=%fused_computation.98 | convolution fusion | flops 423626752 | bytes 11739136 | tf_op jit(solution)/shard_map/sub | solution.py:103
  340.5 10.9 %fusion.41 = bf16[16,48,128]{2,1,0:T(8,128)(2,1)S(1)} fusion(bf16[2048,16,48]{0,2,1:T(8,128)(2,1)} %bitcast.65, f32[16,128]{1,0:T(8,128)S(1)} %fusion.78, bf16[16,128,2048]{2,1,0:T(8,128)(2,1)} %all-gather.8.cloned.1.call-done, bf16[128,16,48]{0,2,1:T(8,128)(2,1)S(1)} %bitcast.75, bf16[2048,16,48]{0,2,1:T(8,128)(2,1)} %bitcast.70), kind=kOutput, calls=%fused_computation.52 | convolution fusion | flops 830574592 | bytes 15081472 | tf_op jit(solution)/shard_map/hqk,khd->qhd/dot_general | solution.py:105
  351.5 8.5 %fusion.79 = f32[16,128]{1,0:T(8,128)S(1)} fusion(bf16[16,128,2048]{2,1,0:T(8,128)(2,1)} %all-gather.8.cloned.1.call-done, bf16[128,16,48]{0,2,1:T(8,128)(2,1)S(1)} %bitcast.72, bf16[2048,16,48]{0,2,1:T(8,128)(2,1)} %bitcast.67), kind=kOutput, calls=%fused_computation.99 | convolution fusion | flops 423626752 | bytes 11739136 | tf_op jit(solution)/shard_map/sub | solution.py:103
  360.0 10.9 %fusion.42 = bf16[16,48,128]{2,1,0:T(8,128)(2,1)S(1)} fusion(bf16[2048,16,48]{0,2,1:T(8,128)(2,1)} %bitcast.66, f32[16,128]{1,0:T(8,128)S(1)} %fusion.79, bf16[16,128,2048]{2,1,0:T(8,128)(2,1)} %all-gather.8.cloned.1.call-done, bf16[128,16,48]{0,2,1:T(8,128)(2,1)S(1)} %bitcast.73, bf16[2048,16,48]{0,2,1:T(8,128)(2,1)} %bitcast.68), kind=kOutput, calls=%fused_computation.53 | convolution fusion | flops 830574592 | bytes 15081472 | tf_op jit(solution)/shard_map/hqk,khd->qhd/dot_general | solution.py:105
  371.1 0.5 fusion.36
  371.6 2.3 fusion.34
  (42 shorter events, 1.4 us)
Async XLA Ops:
  6.5 22.5 %copy-start = (bf16[768,768]{1,0:T(8,128)(2,1)S(1)}, bf16[768,768]{1,0:T(8,128)(2,1)}, u32[]{:S(2)}) copy-start(bf16[768,768]{1,0:T(8,128)(2,1)} %param.23) | copy-start | bytes 3538948
  6.5 13.0 %copy-start.5 = (bf16[2,128,384]{2,1,0:T(8,128)(2,1)S(1)}, bf16[2,128,384]{2,1,0:T(8,128)(2,1)}, u32[]{:S(2)}) copy-start(bf16[2,128,384]{2,1,0:T(8,128)(2,1)} %param.16) | copy-start | bytes 589828
  6.5 144.8 %all-gather.4.cloned.1.call-start = ((), (), s32[]{:S(2)}) async-start(), calls=%async_computation | async-start | bytes 6684672 | tf_op jit(solution)/shard_map/all_gather | solution.py:88
  7.5 14.0 %collective-permute-start.1 = (bf16[1,128]{1,0:T(2,128)(2,1)S(1)}, bf16[1,128]{1,0:T(2,128)(2,1)S(1)}, u32[]{:S(2)}, u32[]{:S(2)}) collective-permute-start(bf16[1,128]{1,0:T(2,128)(2,1)S(1)} %slice.61), channel_id=1, source_target_pairs={{0,1},{1,2},{2,3},{3,4},{4,5},{5,6},{6,7},{7,8},{8,9},{9,10},{10,1... | collective-permute-start | bytes 776 | tf_op jit(solution)/shard_map/ppermute | solution.py:12
  16.0 10.9 %collective-permute-start = (bf16[2,128,768]{2,1,0:T(8,128)(2,1)S(1)}, bf16[2,128,768]{2,1,0:T(8,128)(2,1)S(1)}, u32[]{:S(2)}, u32[]{:S(2)}) collective-permute-start(bf16[2,128,768]{2,1,0:T(8,128)(2,1)S(1)} %slice.41), channel_id=1, source_target_pairs={{0,1},{1,2},{2,3},{3,4},{4,5},{5,6},{6,7},{7,8},{8,9},{9,10},{10,1... | collective-permute-start | bytes 1179656 | tf_op jit(solution)/shard_map/ppermute | solution.py:12
  19.8 10.5 %copy-start.3 = (bf16[768,768]{1,0:T(8,128)(2,1)S(1)}, bf16[768,768]{1,0:T(8,128)(2,1)}, u32[]{:S(2)}) copy-start(bf16[768,768]{1,0:T(8,128)(2,1)} %param.22) | copy-start | bytes 3538948
  30.3 10.0 %copy-start.8 = (bf16[128,16]{0,1:T(8,128)(2,1)S(1)}, bf16[128,16]{0,1:T(8,128)(2,1)}, u32[]{:S(2)}) copy-start(bf16[128,16]{0,1:T(8,128)(2,1)} %param.24) | copy-start | bytes 12292
  30.3 236.5 %all-gather.6.cloned.1.call-start = ((), (), s32[]{:S(2)}) async-start(), calls=%async_computation.1 | async-start | bytes 6684672 | tf_op jit(solution)/shard_map/all_gather | solution.py:87
  31.7 300.4 %all-gather.8.cloned.1.call-start = ((), (), s32[]{:S(2)}) async-start(), calls=%async_computation.2 | async-start | bytes 8912896 | tf_op jit(solution)/shard_map/all_gather | solution.py:51
  31.9 3.5 copy-start.1
  35.5 11.6 %copy-start.7 = (bf16[768]{0:T(1024)(128)(2,1)S(1)}, bf16[768]{0:T(1024)(128)(2,1)}, u32[]{:S(2)}) copy-start(bf16[768]{0:T(1024)(128)(2,1)} %param.27) | copy-start | bytes 4612
  35.5 11.6 %copy-start.4 = (bf16[768,768]{1,0:T(8,128)(2,1)S(1)}, bf16[768,768]{1,0:T(8,128)(2,1)}, u32[]{:S(2)}) copy-start(bf16[768,768]{1,0:T(8,128)(2,1)} %param.21) | copy-start | bytes 3538948
  360.0 11.1 %copy-start.2 = (bf16[768,768]{1,0:T(8,128)(2,1)S(1)}, bf16[768,768]{1,0:T(8,128)(2,1)}, u32[]{:S(2)}) copy-start(bf16[768,768]{1,0:T(8,128)(2,1)} %param.25) | copy-start | bytes 3538948
  360.0 11.6 %copy-start.6 = (bf16[2,128,384]{2,1,0:T(8,128)(2,1)S(1)}, bf16[2,128,384]{2,1,0:T(8,128)(2,1)}, u32[]{:S(2)}) copy-start(bf16[2,128,384]{2,1,0:T(8,128)(2,1)} %param.16) | copy-start | bytes 589828
Sparse Core Ops, SparseCore 0:
  30.5 120.8 all-gather.3
  153.9 112.8 all-gather.5
  268.6 63.3 all-gather.7
where the time goes:
time: 381 us; the launch traced here: 380 us
  waiting for transfers between devices  259 us (68%)
  matrix products  56.5 us (15%)
  local copies, waits for them, and re-layouts  32.3 us (8%)
  between operations  13.4 us (4%)
  other arithmetic  10.1 us (3%)
  starting transfers between devices  9.26 us (2%)
    all_gather x1, waiting for transfers between devices, per_device(): lax.all_gather(local_pair[0], 'seq', axis=1, tiled=True)  105 us
    all_gather x1, waiting for transfers between devices, per_device(): lax.all_gather(local_pair[1], 'seq', axis=1, tiled=True)  103 us
    all_gather x1, waiting for transfers between devices, per_device(): pair_bias = lax.all_gather(bias_local, 'sample', axis=2, tiled=True)  45.2 us
    dot_general x2, matrix products, per_device(): jnp.einsum('hqk,khd->qhd', weights, value_heads, preferred_element_type=j...  21.8 us
    sub x2, matrix products, per_device(): exponent = jnp.exp(scores - largest)  16.9 us
    slice x3, local copies, waits for them, and re-layouts, per_device(): values_all[sample_index].reshape(total_tokens, head_count, head_size)  15.4 us
    slice x3, local copies, waits for them, and re-layouts, per_device(): keys_all[sample_index].reshape(total_tokens, head_count, head_size)  15.3 us
    ppermute x2, starting transfers between devices, from_behind(): lax.ppermute(value, axis, [(source, source + steps) for source in range(i...  8.99 us
  transfers between devices with their start and end apart: 5, of which 4 were waited for; matrix products, arithmetic and copies ran while one was open for 14% of the time, Pallas kernels for 0%

commit v1 on v0

v1 whole, which is shorter than its diff:
```python
import math

import jax
import jax.numpy as jnp
from jax import lax
from jax.experimental import pallas as pl
from jax.experimental.pallas import tpu as pltpu
from jax.sharding import PartitionSpec as P

F32 = jnp.float32
BF16 = jnp.bfloat16
LOG2E = 1.4426950408889634
ROWS = 256


def from_behind(value, axis, steps):
    count = lax.axis_size(axis)
    initial, last = (max(0, -steps), min(count, count - steps))
    return lax.ppermute(value, axis, [(source, source + steps) for source in range(initial, last)])


def layer_norm(inputs):
    average = jnp.mean(inputs, axis=-1, keepdims=True)
    centered = inputs - average
    variance = jnp.mean(centered * centered, axis=-1, keepdims=True)
    return centered * lax.rsqrt(variance + 1e-05)


def swap_core(value):
    return lax.ppermute(value, "sample", [(i, i ^ 1) for i in range(16)])


def swap_x(value):
    return lax.ppermute(value, "sample", [(i, i ^ 8) for i in range(16)])


def shift_y(value, steps):
    return lax.ppermute(
        value, "sample", [(i, (i & 9) | ((((i >> 1) + steps) & 3) << 1)) for i in range(16)]
    )


def attention_kernel(order_ref, kv_ref, *refs):
    pieces, (out_ref, q_scr, k_scr, v_scr, b_scr) = refs[:16], refs[16:]
    step = pl.program_id(0)
    blocks = kv_ref.shape[0]
    size = kv_ref.shape[1] // 3
    tok = kv_ref.shape[2] // 2
    scale = LOG2E / math.sqrt(size)

    @pl.when(step == 0)
    def _():
        for sample in range(2):
            lanes = slice(sample * tok, (sample + 1) * tok)
            for place in range(blocks):
                block = order_ref[place]
                q_scr[sample, place * tok : (place + 1) * tok, :] = (
                    kv_ref[place, :size, lanes].astype(F32).T.astype(BF16)
                )
                k_scr[sample, :, place * tok : (place + 1) * tok] = kv_ref[block, size : 2 * size, lanes]
                values = kv_ref[block, 2 * size :, lanes].astype(F32)
                padded = jnp.concatenate([values, jnp.ones((tok - size, tok), F32)], axis=0)
                v_scr[sample, place * tok : (place + 1) * tok, :] = padded.T.astype(BF16)

    for place in range(blocks):
        b_scr[:, place * tok : (place + 1) * tok] = pieces[place][...].astype(F32) * LOG2E

    row = pl.multiple_of(step * ROWS, ROWS)
    for sample in range(2):
        scores = jnp.dot(q_scr[sample, pl.ds(row, ROWS), :], k_scr[sample], preferred_element_type=F32)
        scores = scores * scale + b_scr[...]
        largest = jnp.max(scores, axis=-1, keepdims=True)
        weights = jnp.exp2(scores - largest).astype(BF16)
        mixed = jnp.dot(weights, v_scr[sample], preferred_element_type=F32)
        mixed = (mixed / mixed[:, size : size + 1]).T
        for part in range(ROWS // tok):
            out_ref[part, :, sample * tok : (sample + 1) * tok] = mixed[
                :size, part * tok : (part + 1) * tok
            ].astype(BF16)


def attention(order, kv, pieces):
    blocks, rows3, width = kv.shape
    size = rows3 // 3
    tok = width // 2
    total = blocks * tok
    return pl.pallas_call(
        attention_kernel,
        grid=(total // ROWS,),
        in_specs=[
            pl.BlockSpec(memory_space=pltpu.SMEM),
            pl.BlockSpec((blocks, rows3, width), lambda i: (0, 0, 0)),
        ]
        + [pl.BlockSpec((ROWS, tok), lambda i: (i, 0))] * blocks,
        out_specs=pl.BlockSpec((ROWS // tok, size, width), lambda i: (i, 0, 0)),
        out_shape=jax.ShapeDtypeStruct((blocks, size, width), BF16),
        scratch_shapes=[
            pltpu.VMEM((2, total, size), BF16),
            pltpu.VMEM((2, size, total), BF16),
            pltpu.VMEM((2, total, tok), BF16),
            pltpu.VMEM((ROWS, total), F32),
        ],
        compiler_params=pltpu.CompilerParams(vmem_limit_bytes=50 * 1024 * 1024),
        cost_estimate=pl.CostEstimate(
            flops=8 * total * total * 64, bytes_accessed=12 * 1024 * 1024, transcendentals=2 * total * total
        ),
    )(order, kv, *pieces)


def per_device(
    atom_feats,
    atom_token,
    single_cond,
    pair_rep,
    w_atom,
    w_ada_gate,
    w_ada_shift,
    w_query,
    w_key,
    w_value,
    w_pair,
    w_out,
    w_outgate,
    outgate_bias,
):
    samp_local = atom_feats.shape[0]
    atom_local = atom_feats.shape[1]
    tok_local = single_cond.shape[1]
    model_width = w_query.shape[1]
    head_count = w_pair.shape[1]
    head_size = model_width // head_count
    seq_place = lax.axis_index("seq")
    sample_place = lax.axis_index("sample")

    normed_pair = layer_norm(pair_rep.astype(F32)).astype(BF16)
    bias_local = jnp.einsum("ijc,ch->hij", normed_pair, w_pair, preferred_element_type=F32).astype(BF16)
    bias_own = lax.all_to_all(bias_local, "seq", 0, 0, tiled=True).reshape(-1, tok_local)

    hidden = jax.nn.relu(
        jnp.einsum("sac,cd->sad", atom_feats, w_atom, preferred_element_type=F32)
    ).astype(BF16)
    relative = atom_token - seq_place * tok_local
    slot_ids = lax.broadcasted_iota(jnp.int32, (2 * tok_local, atom_local), 0)
    member = slot_ids == relative[None, :]
    partial_value = jnp.einsum("ta,sad->std", member.astype(BF16), hidden, preferred_element_type=F32)
    counts = jnp.sum(member.astype(F32), axis=1)[None, :]
    rounded = partial_value.astype(BF16)
    count_sent = counts
    below_part, below_count = from_behind(
        (rounded[:, tok_local:], count_sent[:, tok_local:]), "seq", 1
    )
    summed = rounded[:, :tok_local].astype(F32) + below_part.astype(F32)
    token_counts = counts[:, :tok_local] + below_count
    tokens = summed / token_counts[:, :, None]
    cond = layer_norm(single_cond.astype(F32)).astype(BF16)
    gate_ada = jax.nn.sigmoid(jnp.einsum("stc,cd->std", cond, w_ada_gate, preferred_element_type=F32))
    shift_ada = jnp.einsum("stc,cd->std", cond, w_ada_shift, preferred_element_type=F32)
    normed = (gate_ada * layer_norm(tokens) + shift_ada).astype(BF16)
    flat = normed.reshape(samp_local * tok_local, model_width)

    def heads_of(weight):
        out = jnp.dot(flat, weight, preferred_element_type=F32).astype(BF16)
        return out.T.reshape(head_count, head_size, samp_local * tok_local)

    sent = jnp.concatenate([heads_of(w_query), heads_of(w_key), heads_of(w_value)], axis=1)
    kv = lax.all_to_all(sent, "seq", 0, 0, tiled=True)

    half = bias_own.shape[0] // 2
    mine = bias_own
    across = swap_x(mine)

    def ring(piece):
        up, down = shift_y(piece, 1), shift_y(piece, -1)
        far = jnp.concatenate([shift_y(up[:half], 1), shift_y(down[half:], -1)], axis=0)
        return [piece, up, down, far]

    pieces = ring(mine) + ring(across)
    pieces = pieces + [swap_core(piece) for piece in pieces]
    x_lo, y, core = sample_place // 8, sample_place // 2 % 4, sample_place % 2
    order = jnp.stack(
        [
            (x_lo ^ dx) * 8 + ((y + dy) % 4) * 2 + (core ^ dc)
            for dc in (0, 1)
            for dx in (0, 1)
            for dy in (0, 3, 1, 2)
        ]
    ).astype(jnp.int32)

    attended = attention(order, kv, pieces)
    attended = lax.all_to_all(attended, "seq", 0, 0, tiled=True).reshape(model_width, -1)
    out_gate = jax.nn.sigmoid(
        jnp.einsum("std,de->ste", cond, w_outgate, preferred_element_type=F32)
        + outgate_bias.astype(F32)
    )
    mixed_out = jnp.einsum("dt,de->te", attended, w_out, preferred_element_type=F32)
    return (out_gate * mixed_out.reshape(out_gate.shape)).astype(BF16)


def solution(mesh):
    return jax.shard_map(
        per_device,
        mesh=mesh,
        in_specs=(
            P("sample", "seq", None),
            P("seq"),
            P("sample", "seq", None),
            P("seq", "sample", None),
            P(),
            P(),
            P(),
            P(),
            P(),
            P(),
            P(),
            P(),
            P(),
            P(),
        ),
        out_specs=P("sample", "seq", None),
        check_vma=False,
    )
```

time: 381 us -> 159 us (0.42)
  waiting for transfers between devices: 259 us -> 41.6 us
  starting transfers between devices: 9.26 us -> 58.5 us
  matrix products: 56.5 us -> 20.1 us
  local copies, waits for them, and re-layouts: 32.3 us -> 8.23 us
  Pallas kernels: 0 us -> 18.3 us
  between operations: 13.4 us -> 0.37 us
    all_gather x3 -> x0, waiting for transfers between devices: 253 us -> none  [the longest x1 105 us: per_device(): lax.all_gather(local_pair[0], 'seq', axis=1, tiled=True)]
    slice x10 -> x5, local copies, waits for them, and re-layouts: 31.1 us -> 1.03 us  [the longest x2 0.98 us: ring(): down[half:]]
    ppermute x0 -> x17, starting transfers between devices: none -> 26.1 us  [the longest x8 14.6 us: swap_core(): return lax.ppermute(value, 'sample', [(i, i ^ 1) for i in range(16)])]
    all_to_all x0 -> x3, waiting for transfers between devices: none -> 23.3 us  [the longest x1 15.1 us: per_device(): lax.all_to_all(attended, 'seq', 0, 0, tiled=True).reshape(model_width, -1)]
    all_to_all x0 -> x3, starting transfers between devices: none -> 23.1 us  [the longest x1 9.83 us: per_device(): lax.all_to_all(bias_local, 'seq', 0, 0, tiled=True).reshape(-1, tok_local)]
    dot_general x11 -> x9, matrix products: 39.6 us -> 20.1 us  [the longest x1 5.84 us: per_device(): jnp.einsum('ijc,ch->hij', normed_pair, w_pair, preferred_element_type=F32)]
    ppermute x0 -> x17, waiting for transfers between devices: none -> 18.3 us  [the longest x1 9.79 us: swap_x(): return lax.ppermute(value, 'sample', [(i, i ^ 8) for i in range(16)])]
    pallas_call x0 -> x1, Pallas kernels: none -> 18.3 us  [attention(): pl.pallas_call(attention_kernel, grid=(total // ROWS,), in_specs=[pl.Bloc...]
  transfers between devices with their start and end apart: 5 -> 22, of which waited for: 4 -> 7; matrix products, arithmetic and copies ran while one was open for 14% -> 20% of each run, Pallas kernels for 0% -> 0%
where the time goes in v1:
time: 159 us; the launch traced here: 158 us
  starting transfers between devices  58.5 us (37%)
  waiting for transfers between devices  41.6 us (26%)
  matrix products  20.1 us (13%)
  Pallas kernels  18.3 us (12%)
  other arithmetic  11.1 us (7%)
  local copies, waits for them, and re-layouts  8.23 us (5%)
    pallas_call x1, Pallas kernels, attention(): pl.pallas_call(attention_kernel, grid=(total // ROWS,), in_specs=[pl.Bloc...  18.3 us
    all_to_all x1, waiting for transfers between devices, per_device(): lax.all_to_all(attended, 'seq', 0, 0, tiled=True).reshape(model_width, -1)  15.1 us
    ppermute x8, starting transfers between devices, swap_core(): return lax.ppermute(value, 'sample', [(i, i ^ 1) for i in range(16)])  14.6 us
    ppermute x8, starting transfers between devices, shift_y(): lax.ppermute(value, 'sample', [(i, i & 9 | ((i >> 1) + steps & 3) << 1) f...  11.1 us
    all_to_all x1, starting transfers between devices, per_device(): lax.all_to_all(bias_local, 'seq', 0, 0, tiled=True).reshape(-1, tok_local)  9.83 us
    ppermute x1, waiting for transfers between devices, swap_x(): return lax.ppermute(value, 'sample', [(i, i ^ 8) for i in range(16)])  9.79 us
    ppermute x2, starting transfers between devices, from_behind(): lax.ppermute(value, axis, [(source, source + steps) for source in range(i...  9.25 us
    all_to_all x1, starting transfers between devices, per_device(): lax.all_to_all(attended, 'seq', 0, 0, tiled=True).reshape(model_width, -1)  8.86 us
  transfers between devices with their start and end apart: 22, of which 7 were waited for; matrix products, arithmetic and copies ran while one was open for 20% of the time, Pallas kernels for 0%

profile of v1, /device:TPU:1, one launch (start us, length us, event | category | flops | bytes accessed | tf_op | source)
XLA Modules:
  0.0 158.2 jit_solution(6607605815641270145)
XLA Ops:
  1.0 5.5 %collective-permute-start.1 = (f32[1,128]{1,0:T(1,128)S(1)}, f32[1,128]{1,0:T(1,128)S(1)}, u32[]{:S(2)}, u32[]{:S(2)}) collective-permute-start(f32[1,128]{1,0:T(1,128)S(1)} %slice.35), channel_id=1, source_target_pairs={{0,1},{1,2},{2,3},{3,4},{4,5},{5,6},{6,7},{7,8},{8,9},{9,10},{10,1... | collective-permute-start | bytes 1544 | tf_op jit(solution)/shard_map/ppermute | solution.py:19
  6.5 4.1 %fusion.24 = bf16[2,256,768]{2,1,0:T(8,128)(2,1)S(1)} fusion(bf16[2,1024,128]{2,1,0:T(8,128)(2,1)} %param.14, s32[1024]{0:T(1024)S(1)} %broadcast_subtract_fusion, bf16[128,768]{1,0:T(8,128)(2,1)} %param.18), kind=kOutput, calls=%fused_computation.26 | convolution fusion | flops 1211760640 | bytes 1511424 | tf_op jit(solution)/shard_map/ta,sad->std/dot_general | solution.py:145
  10.7 3.8 %collective-permute-start = (bf16[2,128,768]{2,1,0:T(8,128)(2,1)S(1)}, bf16[2,128,768]{2,1,0:T(8,128)(2,1)S(1)}, u32[]{:S(2)}, u32[]{:S(2)}) collective-permute-start(bf16[2,128,768]{2,1,0:T(8,128)(2,1)S(1)} %slice.33), channel_id=1, source_target_pairs={{0,1},{1,2},{2,3},{3,4},{4,5},{5,6},{6,7},{7,8},{8,9},{9,10},{10,1... | collective-permute-start | bytes 1179656 | tf_op jit(solution)/shard_map/ppermute | solution.py:19
  14.4 3.4 %convert_reduce_fusion = f32[128,128]{1,0:T(8,128)S(1)} fusion(bf16[128,128,128]{2,1,0:T(8,128)(2,1)} %param.17), kind=kLoop, calls=%fused_computation.1 | loop fusion | flops 4177920 | bytes 4259840 | tf_op jit(solution)/shard_map/reduce_sum | solution.py:23
  17.8 4.8 %fusion.2 = f32[128,128]{1,0:T(8,128)S(1)} fusion(bf16[128,128,128]{2,1,0:T(8,128)(2,1)S(1)} %copy-done.3, f32[128,128]{1,0:T(8,128)S(1)} %broadcast_multiply_fusion), kind=kLoop, calls=%fused_computation.4 | loop fusion | flops 8372224 | bytes 4325376 | tf_op jit(solution)/shard_map/reduce_sum | solution.py:25
  22.7 5.8 %fusion.27 = bf16[16,128,128]{2,0,1:T(8,128)(2,1)S(1)} fusion(bf16[128,128,128]{2,1,0:T(8,128)(2,1)S(1)} %copy-done.3, f32[128,128]{1,0:T(8,128)S(1)} %add_rsqrt_fusion, f32[128,128]{1,0:T(8,128)S(1)} %broadcast_multiply_fusion, bf16[128,16]{0,1:T(8,128)(2,1)S(1)} %copy-done.10), kind=kOutput, calls=%fused_computation.32 | convolution fusion | flops 75759616 | bytes 4853760 | tf_op jit(solution)/shard_map/ijc,ch->hij/dot_general | solution.py:136
  29.4 9.8 %all-to-all-start.1 = ((bf16[16,128,128]{2,1,0:T(8,128)(2,1)}), bf16[16,128,128]{2,1,0:T(8,128)(2,1)S(1)}, u32[]{:S(2)}, u32[]{:S(2)}) async-start(bf16[16,128,128]{2,1,0:T(8,128)(2,1)} %copy.23), calls=%async_computation.1 | async-start | bytes 1048576 | tf_op jit(solution)/shard_map/all_to_all | solution.py:137
  39.6 1.6 %fusion.20 = f32[2,128,768]{2,1,0:T(8,128)S(1)} fusion(bf16[384,768]{1,0:T(8,128)(2,1)} %param.19, bf16[2,128,384]{2,1,0:T(8,128)(2,1)S(1)} %copy-done.4, f32[2,128]{1,0:T(2,128)S(1)} %add_rsqrt_fusion.2, f32[2,128]{1,0:T(2,128)S(1)} %broadcast_multiply_fusion.2), kind=kOutput, calls=%fused_computation.22 | convolution fusion | flops 151977984 | bytes 1574912 | tf_op jit(solution)/shard_map/stc,cd->std/dot_general | solution.py:156
  43.0 1.7 %fusion.31 = bf16[768,256]{0,1:T(8,128)(2,1)S(1)} fusion(bf16[256,768]{1,0:T(8,128)(2,1)S(1)} %bitcast.74, bf16[768,768]{1,0:T(8,128)(2,1)} %param.22), kind=kOutput, calls=%fused_computation.34 | convolution fusion | flops 302186496 | bytes 1966080 | tf_op jit(solution)/shard_map/dot_general | solution.py:162
  44.9 1.7 %fusion.32 = bf16[768,256]{0,1:T(8,128)(2,1)S(1)} fusion(bf16[256,768]{1,0:T(8,128)(2,1)S(1)} %bitcast.75, bf16[768,768]{1,0:T(8,128)(2,1)} %param.23), kind=kOutput, calls=%fused_computation.35 | convolution fusion | flops 302186496 | bytes 1966080 | tf_op jit(solution)/shard_map/dot_general | solution.py:162
  46.8 1.1 pad_maximum_fusion
  47.9 8.1 %all-to-all-done.1 = bf16[16,128,128]{2,1,0:T(8,128)(2,1)S(1)} async-done(((bf16[16,128,128]{2,1,0:T(8,128)(2,1)}), bf16[16,128,128]{2,1,0:T(8,128)(2,1)S(1)}, u32[]{:S(2)}, u32[]{:S(2)}) %all-to-all-start.1) | async-done | bytes 524320 | tf_op jit(solution)/shard_map/all_to_all | solution.py:137
  56.0 4.4 %all-to-all-start = ((bf16[16,144,256]{2,1,0:T(8,128)(2,1)}), bf16[16,144,256]{2,1,0:T(8,128)(2,1)}, u32[]{:S(2)}, u32[]{:S(2)}) async-start(bf16[16,144,256]{2,1,0:T(8,128)(2,1)} %pad_maximum_fusion), calls=%async_computation | async-start | bytes 2359296 | tf_op jit(solution)/shard_map/all_to_all | solution.py:166
  60.9 1.3 collective-permute-start.2
  62.2 1.4 collective-permute-start.3
  63.6 9.8 %collective-permute-done.6.refs_4_ = bf16[2048,128]{1,0:T(8,128)(2,1)S(1)} collective-permute-done((bf16[2048,128]{1,0:T(8,128)(2,1)S(1)}, bf16[2048,128]{1,0:T(8,128)(2,1)S(1)}, u32[]{:S(2)}, u32[]{:S(2)}) %collective-permute-start.6) | collective-permute-done | bytes 524320 | tf_op jit(solution)/shard_map/ppermute | solution.py:34
  73.4 1.3 collective-permute-start.7
  74.7 1.4 collective-permute-start.8
  76.3 2.7 %collective-permute-start.5 = (bf16[1024,128]{1,0:T(8,128)(2,1)S(1)}, bf16[1024,128]{1,0:T(8,128)(2,1)S(1)}, u32[]{:S(2)}, u32[]{:S(2)}) collective-permute-start(bf16[1024,128]{1,0:T(8,128)(2,1)S(1)} %slice.37), channel_id=1, source_target_pairs={{0,96},{16,112},{32,0},{48,16},{64,32},{80,48},{96,64},{112,80},{1... | collective-permute-start | bytes 786440 | tf_op jit(solution)/shard_map/ppermute | solution.py:38
  79.0 6.4 %collective-permute-start.11 = (bf16[2048,128]{1,0:T(8,128)(2,1)S(1)}, bf16[2048,128]{1,0:T(8,128)(2,1)S(1)}, u32[]{:S(2)}, u32[]{:S(2)}) collective-permute-start(bf16[2048,128]{1,0:T(8,128)(2,1)S(1)} %bitcast.71), channel_id=1, source_target_pairs={{0,16},{16,0},{32,48},{48,32},{64,80},{80,64},{96,112},{112,96},{1... | collective-permute-start | bytes 1572872 | tf_op jit(solution)/shard_map/ppermute | solution.py:30
  85.4 3.2 %collective-permute-done.4 = bf16[1024,128]{1,0:T(8,128)(2,1)S(1)} collective-permute-done((bf16[1024,128]{1,0:T(8,128)(2,1)S(1)}, bf16[1024,128]{1,0:T(8,128)(2,1)S(1)}, u32[]{:S(2)}, u32[]{:S(2)}) %collective-permute-start.4) | collective-permute-done | bytes 262176 | tf_op jit(solution)/shard_map/ppermute | solution.py:38
  88.6 6.1 %collective-permute-start.15 = (bf16[2048,128]{1,0:T(8,128)(2,1)S(1)}, bf16[2048,128]{1,0:T(8,128)(2,1)S(1)}, u32[]{:S(2)}, u32[]{:S(2)}) collective-permute-start(bf16[2048,128]{1,0:T(8,128)(2,1)S(1)} %collective-permute-done.6.refs_4_), channel_id=1, source_target_pairs={{0,16},{16,0},{32,48},{48,32},{64,80},{80,64},{96,112},{112,96},{1... | collective-permute-start | bytes 1572872 | tf_op jit(solution)/shard_map/ppermute | solution.py:30
  95.8 2.7 %collective-permute-start.10 = (bf16[1024,128]{1,0:T(8,128)(2,1)S(1)}, bf16[1024,128]{1,0:T(8,128)(2,1)S(1)}, u32[]{:S(2)}, u32[]{:S(2)}) collective-permute-start(bf16[1024,128]{1,0:T(8,128)(2,1)S(1)} %slice.39), channel_id=1, source_target_pairs={{0,96},{16,112},{32,0},{48,16},{64,32},{80,48},{96,64},{112,80},{1... | collective-permute-start | bytes 786440 | tf_op jit(solution)/shard_map/ppermute | solution.py:38
  99.9 3.4 %collective-permute-done.9 = bf16[1024,128]{1,0:T(8,128)(2,1)S(1)} collective-permute-done((bf16[1024,128]{1,0:T(8,128)(2,1)S(1)}, bf16[1024,128]{1,0:T(8,128)(2,1)S(1)}, u32[]{:S(2)}, u32[]{:S(2)}) %collective-permute-start.9) | collective-permute-done | bytes 262176 | tf_op jit(solution)/shard_map/ppermute | solution.py:38
  103.3 1.4 collective-permute-start.13
  109.3 1.2 collective-permute-done.18.refs_15_
  110.5 1.0 copy-done.2
  111.6 18.3 %shard_map.136 = bf16[16,48,256]{2,1,0:T(8,128)(2,1)} custom-call(s32[16]{0:T(128)S(1)} %stack.67.order_ref, bf16[16,144,256]{2,1,0:T(8,128)(2,1)} %all-to-all-done.kv_ref, bf16[2048,128]{1,0:T(8,128)(2,1)S(1)} %bitcast.72, bf16[2048,128]{1,0:T(8,128)(2,1)S(1)} %collective-permute-done.2.refs_1_, bf16[2048,128]{1,0:T(8,128)(2,1)S(1)} %collective-permute-done.3.refs_2_, ...), custom_call_target="tpu_custom_call" | custom-call | flops 2147483648 | bytes 12582912 | tf_op jit(solution)/shard_map/pallas_call | solution.py:87
  129.9 8.9 %all-to-all-start.2 = ((bf16[16,48,256]{2,1,0:T(8,128)(2,1)}), bf16[16,48,256]{2,1,0:T(8,128)(2,1)S(1)}, u32[]{:S(2)}, u32[]{:S(2)}) async-start(bf16[16,48,256]{2,1,0:T(8,128)(2,1)} %shard_map.136), calls=%async_computation.2 | async-start | bytes 786432 | tf_op jit(solution)/shard_map/all_to_all | solution.py:190
  138.8 15.1 %all-to-all-done.2 = bf16[16,48,256]{2,1,0:T(8,128)(2,1)S(1)} async-done(((bf16[16,48,256]{2,1,0:T(8,128)(2,1)}), bf16[16,48,256]{2,1,0:T(8,128)(2,1)S(1)}, u32[]{:S(2)}, u32[]{:S(2)}) %all-to-all-start.2) | async-done | bytes 393248 | tf_op jit(solution)/shard_map/all_to_all | solution.py:190
  154.1 1.7 %fusion.33 = f32[2,128,768]{2,1,0:T(8,128)S(1)} fusion(bf16[2,128,768]{2,1,0:T(8,128)(2,1)S(1)} %bitcast.80, bf16[768,768]{1,0:T(8,128)(2,1)} %param.25), kind=kOutput, calls=%fused_computation.37 | convolution fusion | flops 301989888 | bytes 2359296 | tf_op jit(solution)/shard_map/dt,de->te/dot_general | solution.py:195
  155.8 2.3 %fusion.25 = bf16[2,128,768]{2,1,0:T(8,128)(2,1)} fusion(f32[2,128,768]{2,1,0:T(8,128)S(1)} %fusion.33, bf16[384,768]{1,0:T(8,128)(2,1)} %param.26, f32[768]{0:T(1024)S(1)} %convert_element_type.69, bf16[2,128,384]{2,1,0:T(8,128)(2,1)S(1)} %copy-done.4, f32[2,128]{1,0:T(2,128)S(1)} %add_rsqrt_fusion.2, f32[2,128]{1,0:T(2,128)S(1)} %broadcast_multiply_fusion.2), kind=kOutput, calls=%fused_computation.27 | convolution fusion | flops 152567808 | bytes 1971200 | tf_op jit(solution)/shard_map/std,de->ste/dot_general | solution.py:192
  (77 shorter events, 12.2 us)
Async XLA Ops:
  0.0 42.3 %copy-start = (bf16[768,768]{1,0:T(8,128)(2,1)S(1)}, bf16[768,768]{1,0:T(8,128)(2,1)}, u32[]{:S(2)}) copy-start(bf16[768,768]{1,0:T(8,128)(2,1)} %param.21) | copy-start | bytes 3538948
  1.0 40.3 %collective-permute-start.1 = (f32[1,128]{1,0:T(1,128)S(1)}, f32[1,128]{1,0:T(1,128)S(1)}, u32[]{:S(2)}, u32[]{:S(2)}) collective-permute-start(f32[1,128]{1,0:T(1,128)S(1)} %slice.35), channel_id=1, source_target_pairs={{0,1},{1,2},{2,3},{3,4},{4,5},{5,6},{6,7},{7,8},{8,9},{9,10},{10,1... | collective-permute-start | bytes 1544 | tf_op jit(solution)/shard_map/ppermute | solution.py:19
  10.6 7.2 %copy-start.3 = (bf16[128,128,128]{2,1,0:T(8,128)(2,1)S(1)}, bf16[128,128,128]{2,1,0:T(8,128)(2,1)}, u32[]{:S(2)}) copy-start(bf16[128,128,128]{2,1,0:T(8,128)(2,1)} %param.17) | copy-start | bytes 12582916
  10.7 30.6 %collective-permute-start = (bf16[2,128,768]{2,1,0:T(8,128)(2,1)S(1)}, bf16[2,128,768]{2,1,0:T(8,128)(2,1)S(1)}, u32[]{:S(2)}, u32[]{:S(2)}) collective-permute-start(bf16[2,128,768]{2,1,0:T(8,128)(2,1)S(1)} %slice.33), channel_id=1, source_target_pairs={{0,1},{1,2},{2,3},{3,4},{4,5},{5,6},{6,7},{7,8},{8,9},{9,10},{10,1... | collective-permute-start | bytes 1179656 | tf_op jit(solution)/shard_map/ppermute | solution.py:19
  17.8 4.8 %copy-start.10 = (bf16[128,16]{0,1:T(8,128)(2,1)S(1)}, bf16[128,16]{0,1:T(8,128)(2,1)}, u32[]{:S(2)}) copy-start(bf16[128,16]{0,1:T(8,128)(2,1)} %param.24) | copy-start | bytes 12292
  22.7 16.6 %copy-start.4 = (bf16[2,128,384]{2,1,0:T(8,128)(2,1)S(1)}, bf16[2,128,384]{2,1,0:T(8,128)(2,1)}, u32[]{:S(2)}) copy-start(bf16[2,128,384]{2,1,0:T(8,128)(2,1)} %param.16) | copy-start | bytes 589828
  29.4 26.6 %all-to-all-start.1 = ((bf16[16,128,128]{2,1,0:T(8,128)(2,1)}), bf16[16,128,128]{2,1,0:T(8,128)(2,1)S(1)}, u32[]{:S(2)}, u32[]{:S(2)}) async-start(bf16[16,128,128]{2,1,0:T(8,128)(2,1)} %copy.23), calls=%async_computation.1 | async-start | bytes 1048576 | tf_op jit(solution)/shard_map/all_to_all | solution.py:137
  39.6 2.2 %copy-start.6 = (bf16[384,768]{1,0:T(8,128)(2,1)S(1)}, bf16[384,768]{1,0:T(8,128)(2,1)}, u32[]{:S(2)}) copy-start(bf16[384,768]{1,0:T(8,128)(2,1)} %param.20) | copy-start | bytes 1769476
  56.0 53.3 %all-to-all-start = ((bf16[16,144,256]{2,1,0:T(8,128)(2,1)}), bf16[16,144,256]{2,1,0:T(8,128)(2,1)}, u32[]{:S(2)}, u32[]{:S(2)}) async-start(bf16[16,144,256]{2,1,0:T(8,128)(2,1)} %pad_maximum_fusion), calls=%async_computation | async-start | bytes 2359296 | tf_op jit(solution)/shard_map/all_to_all | solution.py:166
  60.5 12.9 %collective-permute-start.6 = (bf16[2048,128]{1,0:T(8,128)(2,1)S(1)}, bf16[2048,128]{1,0:T(8,128)(2,1)S(1)}, u32[]{:S(2)}, u32[]{:S(2)}) collective-permute-start(bf16[2048,128]{1,0:T(8,128)(2,1)S(1)} %bitcast.68), channel_id=1, source_target_pairs={{0,128},{16,144},{32,160},{48,176},{64,192},{80,208},{96,224},{112... | collective-permute-start | bytes 1572872 | tf_op jit(solution)/shard_map/ppermute | solution.py:34
  60.9 15.3 %collective-permute-start.2 = (bf16[2048,128]{1,0:T(8,128)(2,1)S(1)}, bf16[2048,128]{1,0:T(8,128)(2,1)S(1)}, u32[]{:S(2)}, u32[]{:S(2)}) collective-permute-start(bf16[2048,128]{1,0:T(8,128)(2,1)S(1)} %bitcast.69), channel_id=1, source_target_pairs={{0,32},{16,48},{32,64},{48,80},{64,96},{80,112},{96,0},{112,16},{1... | collective-permute-start | bytes 1572872 | tf_op jit(solution)/shard_map/ppermute | solution.py:38
  62.2 14.1 %collective-permute-start.3 = (bf16[2048,128]{1,0:T(8,128)(2,1)S(1)}, bf16[2048,128]{1,0:T(8,128)(2,1)S(1)}, u32[]{:S(2)}, u32[]{:S(2)}) collective-permute-start(bf16[2048,128]{1,0:T(8,128)(2,1)S(1)} %bitcast.70), channel_id=1, source_target_pairs={{0,96},{16,112},{32,0},{48,16},{64,32},{80,48},{96,64},{112,80},{1... | collective-permute-start | bytes 1572872 | tf_op jit(solution)/shard_map/ppermute | solution.py:38
  73.4 33.4 %copy-start.1 = (bf16[2048,128]{1,0:T(8,128)(2,1)}, bf16[2048,128]{1,0:T(8,128)(2,1)S(1)}, u32[]{:S(2)}) copy-start(bf16[2048,128]{1,0:T(8,128)(2,1)S(1)} %collective-permute-done.6.refs_4_) | copy-start | bytes 1572868
  73.4 21.2 %collective-permute-start.7 = (bf16[2048,128]{1,0:T(8,128)(2,1)S(1)}, bf16[2048,128]{1,0:T(8,128)(2,1)S(1)}, u32[]{:S(2)}, u32[]{:S(2)}) collective-permute-start(bf16[2048,128]{1,0:T(8,128)(2,1)S(1)} %collective-permute-done.6.refs_4_), channel_id=1, source_target_pairs={{0,32},{16,48},{32,64},{48,80},{64,96},{80,112},{96,0},{112,16},{1... | collective-permute-start | bytes 1572872 | tf_op jit(solution)/shard_map/ppermute | solution.py:38
  74.7 19.9 %collective-permute-start.8 = (bf16[2048,128]{1,0:T(8,128)(2,1)S(1)}, bf16[2048,128]{1,0:T(8,128)(2,1)}, u32[]{:S(2)}, u32[]{:S(2)}) collective-permute-start(bf16[2048,128]{1,0:T(8,128)(2,1)S(1)} %collective-permute-done.6.refs_4_), channel_id=1, source_target_pairs={{0,96},{16,112},{32,0},{48,16},{64,32},{80,48},{96,64},{112,80},{1... | collective-permute-start | bytes 1572872 | tf_op jit(solution)/shard_map/ppermute | solution.py:38
  76.2 12.4 %collective-permute-start.4 = (bf16[1024,128]{1,0:T(8,128)(2,1)S(1)}, bf16[1024,128]{1,0:T(8,128)(2,1)S(1)}, u32[]{:S(2)}, u32[]{:S(2)}) collective-permute-start(bf16[1024,128]{1,0:T(8,128)(2,1)S(1)} %slice.36), channel_id=1, source_target_pairs={{0,32},{16,48},{32,64},{48,80},{64,96},{80,112},{96,0},{112,16},{1... | collective-permute-start | bytes 786440 | tf_op jit(solution)/shard_map/ppermute | solution.py:38
  76.3 19.5 %collective-permute-start.5 = (bf16[1024,128]{1,0:T(8,128)(2,1)S(1)}, bf16[1024,128]{1,0:T(8,128)(2,1)S(1)}, u32[]{:S(2)}, u32[]{:S(2)}) collective-permute-start(bf16[1024,128]{1,0:T(8,128)(2,1)S(1)} %slice.37), channel_id=1, source_target_pairs={{0,96},{16,112},{32,0},{48,16},{64,32},{80,48},{96,64},{112,80},{1... | collective-permute-start | bytes 786440 | tf_op jit(solution)/shard_map/ppermute | solution.py:38
  79.0 27.1 %collective-permute-start.11 = (bf16[2048,128]{1,0:T(8,128)(2,1)S(1)}, bf16[2048,128]{1,0:T(8,128)(2,1)S(1)}, u32[]{:S(2)}, u32[]{:S(2)}) collective-permute-start(bf16[2048,128]{1,0:T(8,128)(2,1)S(1)} %bitcast.71), channel_id=1, source_target_pairs={{0,16},{16,0},{32,48},{48,32},{64,80},{80,64},{96,112},{112,96},{1... | collective-permute-start | bytes 1572872 | tf_op jit(solution)/shard_map/ppermute | solution.py:30
  88.6 18.1 %collective-permute-start.15 = (bf16[2048,128]{1,0:T(8,128)(2,1)S(1)}, bf16[2048,128]{1,0:T(8,128)(2,1)S(1)}, u32[]{:S(2)}, u32[]{:S(2)}) collective-permute-start(bf16[2048,128]{1,0:T(8,128)(2,1)S(1)} %collective-permute-done.6.refs_4_), channel_id=1, source_target_pairs={{0,16},{16,0},{32,48},{48,32},{64,80},{80,64},{96,112},{112,96},{1... | collective-permute-start | bytes 1572872 | tf_op jit(solution)/shard_map/ppermute | solution.py:30
  94.6 12.1 %collective-permute-start.12 = (bf16[2048,128]{1,0:T(8,128)(2,1)S(1)}, bf16[2048,128]{1,0:T(8,128)(2,1)S(1)}, u32[]{:S(2)}, u32[]{:S(2)}) collective-permute-start(bf16[2048,128]{1,0:T(8,128)(2,1)S(1)} %collective-permute-done.2.refs_1_), channel_id=1, source_target_pairs={{0,16},{16,0},{32,48},{48,32},{64,80},{80,64},{96,112},{112,96},{1... | collective-permute-start | bytes 1572872 | tf_op jit(solution)/shard_map/ppermute | solution.py:30
  94.7 8.6 %collective-permute-start.9 = (bf16[1024,128]{1,0:T(8,128)(2,1)S(1)}, bf16[1024,128]{1,0:T(8,128)(2,1)S(1)}, u32[]{:S(2)}, u32[]{:S(2)}) collective-permute-start(bf16[1024,128]{1,0:T(8,128)(2,1)S(1)} %slice.38), channel_id=1, source_target_pairs={{0,32},{16,48},{32,64},{48,80},{64,96},{80,112},{96,0},{112,16},{1... | collective-permute-start | bytes 786440 | tf_op jit(solution)/shard_map/ppermute | solution.py:38
  95.8 9.6 %collective-permute-start.10 = (bf16[1024,128]{1,0:T(8,128)(2,1)S(1)}, bf16[1024,128]{1,0:T(8,128)(2,1)S(1)}, u32[]{:S(2)}, u32[]{:S(2)}) collective-permute-start(bf16[1024,128]{1,0:T(8,128)(2,1)S(1)} %slice.39), channel_id=1, source_target_pairs={{0,96},{16,112},{32,0},{48,16},{64,32},{80,48},{96,64},{112,80},{1... | collective-permute-start | bytes 786440 | tf_op jit(solution)/shard_map/ppermute | solution.py:38
  103.3 5.2 %collective-permute-start.13 = (bf16[2048,128]{1,0:T(8,128)(2,1)S(1)}, bf16[2048,128]{1,0:T(8,128)(2,1)}, u32[]{:S(2)}, u32[]{:S(2)}) collective-permute-start(bf16[2048,128]{1,0:T(8,128)(2,1)S(1)} %collective-permute-done.3.refs_2_), channel_id=1, source_target_pairs={{0,16},{16,0},{32,48},{48,32},{64,80},{80,64},{96,112},{112,96},{1... | collective-permute-start | bytes 1572872 | tf_op jit(solution)/shard_map/ppermute | solution.py:30
  105.4 3.2 %collective-permute-start.14 = (bf16[2048,128]{1,0:T(8,128)(2,1)}, bf16[2048,128]{1,0:T(8,128)(2,1)}, u32[]{:S(2)}, u32[]{:S(2)}) collective-permute-start(bf16[2048,128]{1,0:T(8,128)(2,1)} %constant_dynamic-update-slice_fusion.refs_3_), channel_id=1, source_target_pairs={{0,16},{16,0},{32,48},{48,32},{64,80},{80,64},{96,112},{112,96},{1... | collective-permute-start | bytes 1572872 | tf_op jit(solution)/shard_map/ppermute | solution.py:30
  106.2 0.8 copy-start.7
  106.2 2.4 %collective-permute-start.16 = (bf16[2048,128]{1,0:T(8,128)(2,1)S(1)}, bf16[2048,128]{1,0:T(8,128)(2,1)}, u32[]{:S(2)}, u32[]{:S(2)}) collective-permute-start(bf16[2048,128]{1,0:T(8,128)(2,1)S(1)} %collective-permute-done.7.refs_5_), channel_id=1, source_target_pairs={{0,16},{16,0},{32,48},{48,32},{64,80},{80,64},{96,112},{112,96},{1... | collective-permute-start | bytes 1572872 | tf_op jit(solution)/shard_map/ppermute | solution.py:30
  106.7 0.8 copy-start.8
  106.7 2.6 %collective-permute-start.17 = (bf16[2048,128]{1,0:T(8,128)(2,1)}, bf16[2048,128]{1,0:T(8,128)(2,1)}, u32[]{:S(2)}, u32[]{:S(2)}) collective-permute-start(bf16[2048,128]{1,0:T(8,128)(2,1)} %collective-permute-done.8.refs_6_), channel_id=1, source_target_pairs={{0,16},{16,0},{32,48},{48,32},{64,80},{80,64},{96,112},{112,96},{1... | collective-permute-start | bytes 1572872 | tf_op jit(solution)/shard_map/ppermute | solution.py:30
  108.3 2.3 %collective-permute-start.18 = (bf16[2048,128]{1,0:T(8,128)(2,1)}, bf16[2048,128]{1,0:T(8,128)(2,1)}, u32[]{:S(2)}, u32[]{:S(2)}) collective-permute-start(bf16[2048,128]{1,0:T(8,128)(2,1)} %constant_dynamic-update-slice_fusion.2.refs_7_), channel_id=1, source_target_pairs={{0,16},{16,0},{32,48},{48,32},{64,80},{80,64},{96,112},{112,96},{1... | collective-permute-start | bytes 1572872 | tf_op jit(solution)/shard_map/ppermute | solution.py:30
  108.5 30.3 %copy-start.5 = (bf16[768]{0:T(1024)(128)(2,1)S(1)}, bf16[768]{0:T(1024)(128)(2,1)}, u32[]{:S(2)}) copy-start(bf16[768]{0:T(1024)(128)(2,1)} %param.27) | copy-start | bytes 4612
  110.5 1.0 copy-start.2
  129.9 24.0 %all-to-all-start.2 = ((bf16[16,48,256]{2,1,0:T(8,128)(2,1)}), bf16[16,48,256]{2,1,0:T(8,128)(2,1)S(1)}, u32[]{:S(2)}, u32[]{:S(2)}) async-start(bf16[16,48,256]{2,1,0:T(8,128)(2,1)} %shard_map.136), calls=%async_computation.2 | async-start | bytes 786432 | tf_op jit(solution)/shard_map/all_to_all | solution.py:190
  (1 other events, 0.8 us)

commit v2 on v1

v2 whole, which is shorter than its diff:
```python
import math

import jax
import jax.numpy as jnp
from jax import lax
from jax.experimental import pallas as pl
from jax.experimental.pallas import tpu as pltpu
from jax.sharding import PartitionSpec as P

F32 = jnp.float32
BF16 = jnp.bfloat16
LOG2E = 1.4426950408889634
ROWS = 256


def from_behind(value, axis, steps):
    count = lax.axis_size(axis)
    initial, last = (max(0, -steps), min(count, count - steps))
    return lax.ppermute(value, axis, [(source, source + steps) for source in range(initial, last)])


def layer_norm(inputs):
    average = jnp.mean(inputs, axis=-1, keepdims=True)
    centered = inputs - average
    variance = jnp.mean(centered * centered, axis=-1, keepdims=True)
    return centered * lax.rsqrt(variance + 1e-05)


def swap_core(value):
    return lax.ppermute(value, "sample", [(i, i ^ 1) for i in range(16)])


def swap_x(value):
    return lax.ppermute(value, "sample", [(i, i ^ 8) for i in range(16)])


def shift_y(value, steps):
    return lax.ppermute(
        value, "sample", [(i, (i & 9) | ((((i >> 1) + steps) & 3) << 1)) for i in range(16)]
    )


def pair_kernel(pair_ref, weight_ref, out_ref, sum_weights, square_weights, mean_weights, bias_scr):
    step = pl.program_id(0)
    groups, eight, keys, depth = pair_ref.shape
    heads = weight_ref.shape[0]
    width = heads * eight

    @pl.when(step == 0)
    def _():
        lane = lax.broadcasted_iota(jnp.int32, (heads, width), 1)
        row = lax.broadcasted_iota(jnp.int32, (heads, width), 0)
        spread = (lane // eight == row).astype(BF16)
        repeated = lax.dot_general(
            weight_ref[...], spread, (((0,), (0,)), ((), ())), preferred_element_type=F32
        )
        mean_weights[...] = jnp.broadcast_to(
            jnp.sum(repeated, axis=0, keepdims=True) * (1.0 / depth), mean_weights.shape
        )
        place = lax.broadcasted_iota(jnp.int32, (depth, width), 1) % eight
        for i in range(eight):
            own = place == i
            ones = jnp.where(own, 1.0, 0.0).astype(BF16)
            sum_weights[i * depth : (i + 1) * depth, :width] = jnp.where(own, repeated, 0.0).astype(BF16)
            sum_weights[i * depth : (i + 1) * depth, width:] = ones
            square_weights[2 * i * depth : (2 * i + 1) * depth, :] = ones
            square_weights[(2 * i + 1) * depth : (2 * i + 2) * depth, :] = ones

    rows = [pair_ref[:, i].reshape(groups * keys, depth) for i in range(eight)]
    sums = jnp.dot(jnp.concatenate(rows, axis=1), sum_weights[...], preferred_element_type=F32)
    parts = []
    for value in rows:
        wide = value.astype(F32)
        square = wide * wide
        high = square.astype(BF16)
        parts += [high, (square - high.astype(F32)).astype(BF16)]
    squares = jnp.dot(jnp.concatenate(parts, axis=1), square_weights[...], preferred_element_type=F32)
    total = sums[:, width:]
    mean = total * (1.0 / depth)
    variance = squares * (1.0 / depth) - mean * mean
    bias = (sums[:, :width] - total * mean_weights[0:1]) * lax.rsqrt(variance + 1e-05)
    for group in range(groups):
        turned = bias[group * keys : (group + 1) * keys].T
        for head in range(heads):
            bias_scr[head, pl.ds((step * groups + group) * eight, eight), :] = turned[
                head * eight : (head + 1) * eight
            ]

    @pl.when(step == pl.num_programs(0) - 1)
    def _():
        for head in range(heads):
            out_ref[head] = bias_scr[head].T.astype(BF16)


def pair_bias_local(pair_rep, w_pair, groups=8):
    queries, keys, depth = pair_rep.shape
    heads = w_pair.shape[1]
    eight = 8
    width = heads * eight
    return pl.pallas_call(
        pair_kernel,
        grid=(queries // (eight * groups),),
        in_specs=[
            pl.BlockSpec((groups, eight, keys, depth), lambda i: (i, 0, 0, 0)),
            pl.BlockSpec((heads, depth), lambda i: (0, 0)),
        ],
        out_specs=pl.BlockSpec((heads, keys, queries), lambda i: (0, 0, 0)),
        out_shape=jax.ShapeDtypeStruct((heads, keys, queries), BF16),
        scratch_shapes=[
            pltpu.VMEM((eight * depth, 2 * width), BF16),
            pltpu.VMEM((2 * eight * depth, width), BF16),
            pltpu.VMEM((8, width), F32),
            pltpu.VMEM((heads, queries, keys), F32),
        ],
        compiler_params=pltpu.CompilerParams(vmem_limit_bytes=40 * 1024 * 1024),
        cost_estimate=pl.CostEstimate(
            flops=2 * queries * keys * depth * 256, bytes_accessed=5 * 1024 * 1024, transcendentals=queries * keys
        ),
    )(pair_rep.reshape(queries // eight, eight, keys, depth), w_pair.T)


def attention_kernel(order_ref, kv_ref, *refs):
    count = len(refs) - 11
    pieces = refs[:count]
    out_ref, q_scr, k_scr, v_scr, b_scr, s_even, s_odd, m_even, m_odd, sems, kv_scr = refs[count:]
    scores_scr, top_scr = (s_even, s_odd), (m_even, m_odd)
    blocks, size, width = out_ref.shape
    tok = width // 2
    total = blocks * tok
    per_step = ROWS // tok
    steps = blocks // per_step
    chunk = 2 * tok
    scale = LOG2E / math.sqrt(size)

    def copies(step):
        found = []
        for place in range(blocks):
            five, kind = place // 4 * 5, place % 4
            start = step * per_step
            if kind == 3:
                found.append((pieces[five + 3 + start * 2 // blocks], start % (blocks // 2)))
            else:
                found.append((pieces[five + kind], start))
        return [
            pltpu.make_async_copy(
                piece.at[pl.ds(start, per_step)],
                b_scr.at[place, pl.ds(step * per_step, per_step)],
                sems.at[step, place],
            )
            for place, (piece, start) in enumerate(found)
        ]

    kv_copy = pltpu.make_async_copy(kv_ref, kv_scr, sems.at[steps, 0])
    kv_copy.start()
    for step in range(steps):
        for copy in copies(step):
            copy.start()
    kv_copy.wait()

    for sample in range(2):
        lanes = slice(sample * tok, (sample + 1) * tok)
        for place in range(blocks):
            block = order_ref[place]
            span = slice(place * tok, (place + 1) * tok)
            query = kv_scr[place, :size, lanes].astype(F32) * scale
            high = query.astype(BF16)
            q_scr[sample, :size, span] = high
            q_scr[sample, size:, span] = (query - high.astype(F32)).astype(BF16)
            key = kv_scr[block, size : 2 * size, lanes].astype(F32)
            k_scr[sample, span, :] = jnp.concatenate([key, key], axis=0).T.astype(BF16)
            v_scr[sample, :size, span] = kv_scr[block, 2 * size :, lanes]
            v_scr[sample, size:, span] = jnp.ones((v_scr.shape[1] - size, tok), BF16)

    def score(step, slot):
        held = {}

        def part(c):
            if c == 0:
                for place in range(blocks):
                    pltpu.make_async_copy(
                        pieces[0].at[pl.ds(0, per_step)],
                        b_scr.at[place, pl.ds(step * per_step, per_step)],
                        sems.at[step, place],
                    ).wait()
                column = step * ROWS if isinstance(step, int) else pl.multiple_of(step * ROWS, ROWS)
                held["q"] = [q_scr[sample, :, pl.ds(column, ROWS)] for sample in range(2)]
            span = slice(c * chunk, (c + 1) * chunk)
            bias = jnp.concatenate(
                [
                    jnp.concatenate([b_scr[place, step * per_step + t] for t in range(per_step)], axis=1)
                    for place in range(c * chunk // tok, (c + 1) * chunk // tok)
                ],
                axis=0,
            )
            bias = bias.astype(F32) * LOG2E
            for sample in range(2):
                scores = (
                    jnp.dot(k_scr[sample, span, :], held["q"][sample], preferred_element_type=F32) + bias
                )
                scores_scr[slot][sample, span, :] = scores
                top = scores.reshape(chunk // 8, 8, ROWS)
                while top.shape[0] > 4:
                    half = top.shape[0] // 2
                    top = jnp.maximum(top[:half], top[half:])
                held[sample] = top if c == 0 else jnp.maximum(held[sample], top)
                if c == total // chunk - 1:
                    top_scr[slot][sample] = jnp.max(held[sample], axis=0)

        return [lambda c=c: part(c) for c in range(total // chunk)]

    def weigh(step, slot):
        held = {}

        def part(c):
            span = slice(c * chunk, (c + 1) * chunk)
            for sample in range(2):
                if c == 0:
                    held[sample] = jnp.max(top_scr[slot][sample], axis=0, keepdims=True)
                weights = jnp.exp2(scores_scr[slot][sample, span, :] - held[sample]).astype(BF16)
                mixed = jnp.dot(v_scr[sample, :, span], weights, preferred_element_type=F32)
                mixed = mixed if c == 0 else held[sample, 0] + mixed
                held[sample, 0] = mixed
                if c == total // chunk - 1:
                    result = (mixed[:size] / mixed[size : size + 1]).astype(BF16)
                    for t in range(per_step):
                        out_ref[step * per_step + t, :, sample * tok : (sample + 1) * tok] = result[
                            :, t * tok : (t + 1) * tok
                        ]

        return [lambda c=c: part(c) for c in range(total // chunk)]

    def run(*lists):
        for together in zip(*lists):
            for work in together:
                work()

    run(score(0, 0))

    def body(pair, _):
        run(score(2 * pair + 1, 1), weigh(2 * pair, 0))
        run(score(2 * pair + 2, 0), weigh(2 * pair + 1, 1))
        return 0

    lax.fori_loop(0, steps // 2 - 1, body, 0)
    run(score(steps - 1, 1), weigh(steps - 2, 0))
    run(weigh(steps - 1, 1))


def attention(order, kv, pieces):
    blocks, rows3, width = kv.shape
    size = rows3 // 3
    tok = width // 2
    total = blocks * tok
    any_place = pl.BlockSpec(memory_space=pl.ANY)
    return pl.pallas_call(
        attention_kernel,
        in_specs=[pl.BlockSpec(memory_space=pltpu.SMEM), any_place] + [any_place] * len(pieces),
        out_specs=pl.BlockSpec(memory_space=pltpu.VMEM),
        out_shape=jax.ShapeDtypeStruct((blocks, size, width), BF16),
        scratch_shapes=[
            pltpu.VMEM((2, 2 * size, total), BF16),
            pltpu.VMEM((2, total, 2 * size), BF16),
            pltpu.VMEM((2, 64, total), BF16),
            pltpu.VMEM((blocks, blocks, tok, tok), BF16),
            pltpu.VMEM((2, total, ROWS), F32),
            pltpu.VMEM((2, total, ROWS), F32),
            pltpu.VMEM((2, 8, ROWS), F32),
            pltpu.VMEM((2, 8, ROWS), F32),
            pltpu.SemaphoreType.DMA((total // ROWS + 1, blocks)),
            pltpu.VMEM(kv.shape, BF16),
        ],
        compiler_params=pltpu.CompilerParams(vmem_limit_bytes=60 * 1024 * 1024),
        cost_estimate=pl.CostEstimate(
            flops=8 * total * total * 64, bytes_accessed=12 * 1024 * 1024, transcendentals=2 * total * total
        ),
    )(order, kv, *pieces)


def finish_kernel(attended_ref, weight_ref, gate_ref, out_ref):
    mixed = lax.dot_general(
        attended_ref[...], weight_ref[...], (((0,), (0,)), ((), ())), preferred_element_type=F32
    )
    out_ref[...] = (gate_ref[...] * mixed).astype(BF16)


def per_device(
    atom_feats,
    atom_token,
    single_cond,
    pair_rep,
    w_atom,
    w_ada_gate,
    w_ada_shift,
    w_query,
    w_key,
    w_value,
    w_pair,
    w_out,
    w_outgate,
    outgate_bias,
):
    samp_local = atom_feats.shape[0]
    atom_local = atom_feats.shape[1]
    tok_local = single_cond.shape[1]
    model_width = w_query.shape[1]
    head_count = w_pair.shape[1]
    head_size = model_width // head_count
    seq_place = lax.axis_index("seq")
    sample_place = lax.axis_index("sample")

    bias_local = pair_bias_local(pair_rep, w_pair)
    mine = lax.all_to_all(bias_local, "seq", 0, 0, tiled=True)

    hidden = jax.nn.relu(
        jnp.einsum("sac,cd->sad", atom_feats, w_atom, preferred_element_type=F32)
    ).astype(BF16)
    relative = atom_token - seq_place * tok_local
    slot_ids = lax.broadcasted_iota(jnp.int32, (2 * tok_local, atom_local), 0)
    member = slot_ids == relative[None, :]
    partial_value = jnp.einsum("ta,sad->std", member.astype(BF16), hidden, preferred_element_type=F32)
    counts = jnp.sum(member.astype(F32), axis=1)[None, :]
    rounded = partial_value.astype(BF16)
    below_part, below_count = from_behind(
        (rounded[:, tok_local:], counts[:, tok_local:]), "seq", 1
    )
    summed = rounded[:, :tok_local].astype(F32) + below_part.astype(F32)
    token_counts = counts[:, :tok_local] + below_count
    tokens = summed / token_counts[:, :, None]
    cond = layer_norm(single_cond.astype(F32)).astype(BF16)
    out_gate = jax.nn.sigmoid(
        jnp.einsum("std,de->ste", cond, w_outgate, preferred_element_type=F32)
        + outgate_bias.astype(F32)
    ).reshape(samp_local * tok_local, model_width)
    gate_ada = jax.nn.sigmoid(jnp.einsum("stc,cd->std", cond, w_ada_gate, preferred_element_type=F32))
    shift_ada = jnp.einsum("stc,cd->std", cond, w_ada_shift, preferred_element_type=F32)
    normed = (gate_ada * layer_norm(tokens) + shift_ada).astype(BF16)
    flat = normed.reshape(samp_local * tok_local, model_width)

    def heads_of(weight):
        out = jnp.dot(flat, weight, preferred_element_type=F32).astype(BF16)
        return out.T.reshape(head_count, head_size, samp_local * tok_local)

    sent = jnp.concatenate([heads_of(w_query), heads_of(w_key), heads_of(w_value)], axis=1)
    kv = lax.all_to_all(sent, "seq", 0, 0, tiled=True)

    half = mine.shape[0] // 2
    across = swap_x(mine)
    up, down = shift_y(mine, 1), shift_y(mine, -1)
    far = [shift_y(up[:half], 1), shift_y(down[half:], -1)]
    across_up, across_down = shift_y(across, 1), shift_y(across, -1)
    across_far = [swap_x(part) for part in far]
    pieces = [mine, up, down, *far, across, across_up, across_down, *across_far]
    pieces = pieces + [swap_core(piece) for piece in pieces]
    x_lo, y, core = sample_place // 8, sample_place // 2 % 4, sample_place % 2
    order = jnp.stack(
        [
            (x_lo ^ dx) * 8 + ((y + dy) % 4) * 2 + (core ^ dc)
            for dc in (0, 1)
            for dx in (0, 1)
            for dy in (0, 3, 1, 2)
        ]
    ).astype(jnp.int32)

    attended = attention(order, kv, pieces)
    attended = lax.all_to_all(attended, "seq", 0, 0, tiled=True).reshape(model_width, -1)
    out = pl.pallas_call(
        finish_kernel,
        out_shape=jax.ShapeDtypeStruct((samp_local * tok_local, model_width), BF16),
        compiler_params=pltpu.CompilerParams(vmem_limit_bytes=40 * 1024 * 1024),
    )(attended, w_out, out_gate)
    return out.reshape(samp_local, tok_local, model_width)


def solution(mesh):
    return jax.shard_map(
        per_device,
        mesh=mesh,
        in_specs=(
            P("sample", "seq", None),
            P("seq"),
            P("sample", "seq", None),
            P("seq", "sample", None),
            P(),
            P(),
            P(),
            P(),
            P(),
            P(),
            P(),
            P(),
            P(),
            P(),
        ),
        out_specs=P("sample", "seq", None),
        check_vma=False,
    )
```

time: 159 us -> 139 us (0.87)
  matrix products: 20.1 us -> 11.8 us
  other arithmetic: 11.1 us -> 2.94 us
  starting transfers between devices: 58.5 us -> 54.3 us
  local copies, waits for them, and re-layouts: 8.23 us -> 6.37 us
    dot_general x2 -> x0, matrix products: 7.59 us -> none  [the longest x1 5.84 us: per_device(): jnp.einsum('ijc,ch->hij', normed_pair, w_pair, preferred_element_type=F32)]
    reduce_sum x3 -> x2, other arithmetic: 5.25 us -> 0.48 us  [layer_norm(): variance = jnp.mean(centered * centered, axis=-1, keepdims=True)]
    ppermute x8 -> x6, waiting for transfers between devices: 6.58 us -> 10.6 us  [shift_y(): lax.ppermute(value, 'sample', [(i, i & 9 | ((i >> 1) + steps & 3) << 1) f...]
    reduce_sum x3 -> x2, other arithmetic: 3.7 us -> 0.34 us  [layer_norm(): average = jnp.mean(inputs, axis=-1, keepdims=True)]
    ppermute x8 -> x10, starting transfers between devices: 14.6 us -> 11.8 us  [swap_core(): return lax.ppermute(value, 'sample', [(i, i ^ 1) for i in range(16)])]
    ppermute x8 -> x6, starting transfers between devices: 11.1 us -> 8.55 us  [shift_y(): lax.ppermute(value, 'sample', [(i, i & 9 | ((i >> 1) + steps & 3) << 1) f...]
    all_to_all x1, waiting for transfers between devices: 15.1 us -> 13.2 us  [per_device(): lax.all_to_all(attended, 'seq', 0, 0, tiled=True).reshape(model_width, -1)]
    pallas_call x1 -> x3, Pallas kernels: 18.3 us -> 19.8 us  [the longest x1 13.6 us: attention(): pl.pallas_call(attention_kernel, in_specs=[pl.BlockSpec(memory_space=pltp...]
  transfers between devices with their start and end apart: 22 -> 24, of which waited for: 7 -> 9; matrix products, arithmetic and copies ran while one was open for 20% -> 11% of each run, Pallas kernels for 0% -> 4%
where the time goes in v2:
time: 139 us; the launch traced here: 138 us
  starting transfers between devices  54.3 us (39%)
  waiting for transfers between devices  42.5 us (31%)
  Pallas kernels  19.8 us (14%)
  matrix products  11.8 us (8%)
  local copies, waits for them, and re-layouts  6.37 us (5%)
  other arithmetic  2.94 us (2%)
    pallas_call x1, Pallas kernels, attention(): pl.pallas_call(attention_kernel, in_specs=[pl.BlockSpec(memory_space=pltp...  13.6 us
    all_to_all x1, waiting for transfers between devices, per_device(): lax.all_to_all(attended, 'seq', 0, 0, tiled=True).reshape(model_width, -1)  13.2 us
    ppermute x10, starting transfers between devices, swap_core(): return lax.ppermute(value, 'sample', [(i, i ^ 1) for i in range(16)])  11.8 us
    ppermute x6, waiting for transfers between devices, shift_y(): lax.ppermute(value, 'sample', [(i, i & 9 | ((i >> 1) + steps & 3) << 1) f...  10.6 us
    all_to_all x1, starting transfers between devices, per_device(): mine = lax.all_to_all(bias_local, 'seq', 0, 0, tiled=True)  10 us
    ppermute x2, starting transfers between devices, from_behind(): lax.ppermute(value, axis, [(source, source + steps) for source in range(i...  8.99 us
    all_to_all x1, starting transfers between devices, per_device(): lax.all_to_all(attended, 'seq', 0, 0, tiled=True).reshape(model_width, -1)  8.69 us
    ppermute x6, starting transfers between devices, shift_y(): lax.ppermute(value, 'sample', [(i, i & 9 | ((i >> 1) + steps & 3) << 1) f...  8.55 us
  transfers between devices with their start and end apart: 24, of which 9 were waited for; matrix products, arithmetic and copies ran while one was open for 11% of the time, Pallas kernels for 4%

profile of v2, /device:TPU:1, one launch (start us, length us, event | category | flops | bytes accessed | tf_op | source)
XLA Modules:
  0.0 138.0 jit_solution(14683558403990785384)
XLA Ops:
  1.0 5.5 %collective-permute-start.1 = (f32[1,128]{1,0:T(1,128)S(1)}, f32[1,128]{1,0:T(1,128)S(1)}, u32[]{:S(2)}, u32[]{:S(2)}) collective-permute-start(f32[1,128]{1,0:T(1,128)S(1)} %slice.27), channel_id=1, source_target_pairs={{0,1},{1,2},{2,3},{3,4},{4,5},{5,6},{6,7},{7,8},{8,9},{9,10},{10,1... | collective-permute-start | bytes 1544 | tf_op jit(solution)/shard_map/ppermute | solution.py:19
  6.5 4.1 %fusion.12 = bf16[2,256,768]{2,1,0:T(8,128)(2,1)S(1)} fusion(bf16[2,1024,128]{2,1,0:T(8,128)(2,1)} %param.14, s32[1024]{0:T(1024)S(1)} %broadcast_subtract_fusion, bf16[128,768]{1,0:T(8,128)(2,1)} %param.18), kind=kOutput, calls=%fused_computation.15 | convolution fusion | flops 1211760640 | bytes 1511424 | tf_op jit(solution)/shard_map/ta,sad->std/dot_general | solution.py:320
  10.7 3.5 %collective-permute-start = (bf16[2,128,768]{2,1,0:T(8,128)(2,1)S(1)}, bf16[2,128,768]{2,1,0:T(8,128)(2,1)S(1)}, u32[]{:S(2)}, u32[]{:S(2)}) collective-permute-start(bf16[2,128,768]{2,1,0:T(8,128)(2,1)S(1)} %slice.25), channel_id=1, source_target_pairs={{0,1},{1,2},{2,3},{3,4},{4,5},{5,6},{6,7},{7,8},{8,9},{9,10},{10,1... | collective-permute-start | bytes 1179656 | tf_op jit(solution)/shard_map/ppermute | solution.py:19
  14.2 2.2 %copy-done.1 = bf16[128,128,128]{2,1,0:T(8,128)(2,1)S(1)} copy-done((bf16[128,128,128]{2,1,0:T(8,128)(2,1)S(1)}, bf16[128,128,128]{2,1,0:T(8,128)(2,1)}, u32[]{:S(2)}) %copy-start.1) | copy-done | bytes 4194328
  16.4 5.0 %shard_map.136 = bf16[16,128,128]{2,1,0:T(8,128)(2,1)} custom-call(bf16[16,8,128,128]{3,2,1,0:T(8,128)(2,1)S(1)} %bitcast.59, bf16[16,128]{1,0:T(8,128)(2,1)S(1)} %bitcast.62), custom_call_target="tpu_custom_call" | custom-call | flops 1073741824 | bytes 5242880 | tf_op jit(solution)/shard_map/pallas_call | solution.py:100
  21.3 10.0 %all-to-all-start.1 = ((bf16[16,128,128]{2,1,0:T(8,128)(2,1)}), bf16[16,128,128]{2,1,0:T(8,128)(2,1)}, u32[]{:S(2)}, u32[]{:S(2)}) async-start(bf16[16,128,128]{2,1,0:T(8,128)(2,1)} %shard_map.136), calls=%async_computation.1 | async-start | bytes 1048576 | tf_op jit(solution)/shard_map/all_to_all | solution.py:312
  31.7 1.6 %fusion.9 = f32[2,128,768]{2,1,0:T(8,128)S(1)} fusion(bf16[384,768]{1,0:T(8,128)(2,1)} %param.19, bf16[2,128,384]{2,1,0:T(8,128)(2,1)S(1)} %copy-done.5, f32[2,128]{1,0:T(2,128)S(1)} %add_rsqrt_fusion.1, f32[2,128]{1,0:T(2,128)S(1)} %broadcast_multiply_fusion.1), kind=kOutput, calls=%fused_computation.12 | convolution fusion | flops 151977984 | bytes 1574912 | tf_op jit(solution)/shard_map/stc,cd->std/dot_general | solution.py:334
  35.4 1.7 %fusion.15 = bf16[768,256]{0,1:T(8,128)(2,1)S(1)} fusion(bf16[256,768]{1,0:T(8,128)(2,1)S(1)} %bitcast.64, bf16[768,768]{1,0:T(8,128)(2,1)} %param.22), kind=kOutput, calls=%fused_computation.21 | convolution fusion | flops 302186496 | bytes 1966080 | tf_op jit(solution)/shard_map/dot_general | solution.py:340
  37.4 1.7 %fusion.16 = bf16[768,256]{0,1:T(8,128)(2,1)S(1)} fusion(bf16[256,768]{1,0:T(8,128)(2,1)S(1)} %bitcast.65, bf16[768,768]{1,0:T(8,128)(2,1)} %param.23), kind=kOutput, calls=%fused_computation.22 | convolution fusion | flops 302186496 | bytes 1966080 | tf_op jit(solution)/shard_map/dot_general | solution.py:340
  39.3 1.1 pad_maximum_fusion
  40.4 7.8 %all-to-all-done.1.refs_0_ = bf16[16,128,128]{2,1,0:T(8,128)(2,1)} async-done(((bf16[16,128,128]{2,1,0:T(8,128)(2,1)}), bf16[16,128,128]{2,1,0:T(8,128)(2,1)}, u32[]{:S(2)}, u32[]{:S(2)}) %all-to-all-start.1) | async-done | bytes 524320 | tf_op jit(solution)/shard_map/all_to_all | solution.py:312
  48.2 4.4 %all-to-all-start = ((bf16[16,144,256]{2,1,0:T(8,128)(2,1)}), bf16[16,144,256]{2,1,0:T(8,128)(2,1)S(1)}, u32[]{:S(2)}, u32[]{:S(2)}) async-start(bf16[16,144,256]{2,1,0:T(8,128)(2,1)} %pad_maximum_fusion), calls=%async_computation | async-start | bytes 2359296 | tf_op jit(solution)/shard_map/all_to_all | solution.py:344
  52.6 1.4 collective-permute-start.2
  54.0 1.5 %collective-permute-start.3 = (bf16[16,128,128]{2,1,0:T(8,128)(2,1)}, bf16[16,128,128]{2,1,0:T(8,128)(2,1)S(1)}, u32[]{:S(2)}, u32[]{:S(2)}) collective-permute-start(bf16[16,128,128]{2,1,0:T(8,128)(2,1)} %all-to-all-done.1.refs_0_), channel_id=1, source_target_pairs={{0,96},{16,112},{32,0},{48,16},{64,32},{80,48},{96,64},{112,80},{1... | collective-permute-start | bytes 1572872 | tf_op jit(solution)/shard_map/ppermute | solution.py:38
  55.8 2.9 %collective-permute-start.11 = (bf16[16,128,128]{2,1,0:T(8,128)(2,1)}, bf16[16,128,128]{2,1,0:T(8,128)(2,1)S(1)}, u32[]{:S(2)}, u32[]{:S(2)}) collective-permute-start(bf16[16,128,128]{2,1,0:T(8,128)(2,1)} %all-to-all-done.1.refs_0_), channel_id=1, source_target_pairs={{0,16},{16,0},{32,48},{48,32},{64,80},{80,64},{96,112},{112,96},{1... | collective-permute-start | bytes 1572872 | tf_op jit(solution)/shard_map/ppermute | solution.py:30
  58.7 6.6 %collective-permute-done.2.refs_1_ = bf16[16,128,128]{2,1,0:T(8,128)(2,1)S(1)} collective-permute-done((bf16[16,128,128]{2,1,0:T(8,128)(2,1)}, bf16[16,128,128]{2,1,0:T(8,128)(2,1)S(1)}, u32[]{:S(2)}, u32[]{:S(2)}) %collective-permute-start.2) | collective-permute-done | bytes 524320 | tf_op jit(solution)/shard_map/ppermute | solution.py:38
  65.7 2.7 %collective-permute-start.5 = (bf16[8,128,128]{2,1,0:T(8,128)(2,1)S(1)}, bf16[8,128,128]{2,1,0:T(8,128)(2,1)S(1)}, u32[]{:S(2)}, u32[]{:S(2)}) collective-permute-start(bf16[8,128,128]{2,1,0:T(8,128)(2,1)S(1)} %slice.29), channel_id=1, source_target_pairs={{0,96},{16,112},{32,0},{48,16},{64,32},{80,48},{96,64},{112,80},{1... | collective-permute-start | bytes 786440 | tf_op jit(solution)/shard_map/ppermute | solution.py:38
  68.4 3.9 %collective-permute-done.4.refs_3_ = bf16[8,128,128]{2,1,0:T(8,128)(2,1)S(1)} collective-permute-done((bf16[8,128,128]{2,1,0:T(8,128)(2,1)S(1)}, bf16[8,128,128]{2,1,0:T(8,128)(2,1)S(1)}, u32[]{:S(2)}, u32[]{:S(2)}) %collective-permute-start.4) | collective-permute-done | bytes 262176 | tf_op jit(solution)/shard_map/ppermute | solution.py:38
  72.8 1.1 collective-permute-start.10
  73.9 4.5 %collective-permute-start.14 = (bf16[8,128,128]{2,1,0:T(8,128)(2,1)S(1)}, bf16[8,128,128]{2,1,0:T(8,128)(2,1)}, u32[]{:S(2)}, u32[]{:S(2)}) collective-permute-start(bf16[8,128,128]{2,1,0:T(8,128)(2,1)S(1)} %collective-permute-done.4.refs_3_), channel_id=1, source_target_pairs={{0,16},{16,0},{32,48},{48,32},{64,80},{80,64},{96,112},{112,96},{1... | collective-permute-start | bytes 786440 | tf_op jit(solution)/shard_map/ppermute | solution.py:30
  78.4 2.7 %collective-permute-start.8 = (bf16[16,128,128]{2,1,0:T(8,128)(2,1)S(1)}, bf16[16,128,128]{2,1,0:T(8,128)(2,1)}, u32[]{:S(2)}, u32[]{:S(2)}) collective-permute-start(bf16[16,128,128]{2,1,0:T(8,128)(2,1)S(1)} %collective-permute-done.6.refs_5_), channel_id=1, source_target_pairs={{0,96},{16,112},{32,0},{48,16},{64,32},{80,48},{96,64},{112,80},{1... | collective-permute-start | bytes 1572872 | tf_op jit(solution)/shard_map/ppermute | solution.py:38
  81.1 4.9 %collective-permute-done.9.refs_8_ = bf16[8,128,128]{2,1,0:T(8,128)(2,1)} collective-permute-done((bf16[8,128,128]{2,1,0:T(8,128)(2,1)S(1)}, bf16[8,128,128]{2,1,0:T(8,128)(2,1)}, u32[]{:S(2)}, u32[]{:S(2)}) %collective-permute-start.9) | collective-permute-done | bytes 262176 | tf_op jit(solution)/shard_map/ppermute | solution.py:34
  86.0 2.0 %collective-permute-start.16 = (bf16[16,128,128]{2,1,0:T(8,128)(2,1)S(1)}, bf16[16,128,128]{2,1,0:T(8,128)(2,1)S(1)}, u32[]{:S(2)}, u32[]{:S(2)}) collective-permute-start(bf16[16,128,128]{2,1,0:T(8,128)(2,1)S(1)} %collective-permute-done.6.refs_5_), channel_id=1, source_target_pairs={{0,16},{16,0},{32,48},{48,32},{64,80},{80,64},{96,112},{112,96},{1... | collective-permute-start | bytes 1572872 | tf_op jit(solution)/shard_map/ppermute | solution.py:30
  88.0 3.6 %collective-permute-done.10.refs_9_ = bf16[8,128,128]{2,1,0:T(8,128)(2,1)} collective-permute-done((bf16[8,128,128]{2,1,0:T(8,128)(2,1)S(1)}, bf16[8,128,128]{2,1,0:T(8,128)(2,1)}, u32[]{:S(2)}, u32[]{:S(2)}) %collective-permute-start.10) | collective-permute-done | bytes 262176 | tf_op jit(solution)/shard_map/ppermute | solution.py:34
  91.6 1.2 collective-permute-start.15
  92.8 1.2 collective-permute-done.15.refs_14_
  98.5 1.0 copy-done.4
  99.5 13.6 %shard_map.137 = bf16[16,48,256]{2,1,0:T(8,128)(2,1)} custom-call(s32[16]{0:T(128)} %stack.67.order_ref, bf16[16,144,256]{2,1,0:T(8,128)(2,1)} %copy-done.4, bf16[16,128,128]{2,1,0:T(8,128)(2,1)} %all-to-all-done.1.refs_0_, bf16[16,128,128]{2,1,0:T(8,128)(2,1)} %copy-done.6, bf16[16,128,128]{2,1,0:T(8,128)(2,1)} %copy-done.7, ...), custom_call_target="tpu_custom_call" | custom-call | flops 2147483648 | bytes 12582912 | tf_op jit(solution)/shard_map/pallas_call | solution.py:255
  113.1 8.7 %all-to-all-start.2 = ((bf16[16,48,256]{2,1,0:T(8,128)(2,1)}), bf16[16,48,256]{2,1,0:T(8,128)(2,1)S(1)}, u32[]{:S(2)}, u32[]{:S(2)}) async-start(bf16[16,48,256]{2,1,0:T(8,128)(2,1)} %shard_map.137), calls=%async_computation.2 | async-start | bytes 786432 | tf_op jit(solution)/shard_map/all_to_all | solution.py:365
  121.8 1.7 %fusion.11 = f32[2,128,768]{2,1,0:T(8,128)S(1)} fusion(bf16[384,768]{1,0:T(8,128)(2,1)} %param.26, f32[768]{0:T(1024)S(1)} %convert_element_type.67, bf16[2,128,384]{2,1,0:T(8,128)(2,1)} %param.16, f32[2,128]{1,0:T(2,128)S(1)} %add_rsqrt_fusion.1, f32[2,128]{1,0:T(2,128)S(1)} %broadcast_multiply_fusion.1), kind=kOutput, calls=%fused_computation.14 | convolution fusion | flops 152174592 | bytes 1577984 | tf_op jit(solution)/shard_map/std,de->ste/dot_general | solution.py:331
  123.6 13.2 %all-to-all-done.2 = bf16[16,48,256]{2,1,0:T(8,128)(2,1)S(1)} async-done(((bf16[16,48,256]{2,1,0:T(8,128)(2,1)}), bf16[16,48,256]{2,1,0:T(8,128)(2,1)S(1)}, u32[]{:S(2)}, u32[]{:S(2)}) %all-to-all-start.2) | async-done | bytes 393248 | tf_op jit(solution)/shard_map/all_to_all | solution.py:365
  136.8 1.3 shard_map.138
  (81 shorter events, 9.3 us)
Async XLA Ops:
  0.0 34.8 %copy-start = (bf16[768,768]{1,0:T(8,128)(2,1)S(1)}, bf16[768,768]{1,0:T(8,128)(2,1)}, u32[]{:S(2)}) copy-start(bf16[768,768]{1,0:T(8,128)(2,1)} %param.21) | copy-start | bytes 3538948
  1.0 32.3 %collective-permute-start.1 = (f32[1,128]{1,0:T(1,128)S(1)}, f32[1,128]{1,0:T(1,128)S(1)}, u32[]{:S(2)}, u32[]{:S(2)}) collective-permute-start(f32[1,128]{1,0:T(1,128)S(1)} %slice.27), channel_id=1, source_target_pairs={{0,1},{1,2},{2,3},{3,4},{4,5},{5,6},{6,7},{7,8},{8,9},{9,10},{10,1... | collective-permute-start | bytes 1544 | tf_op jit(solution)/shard_map/ppermute | solution.py:19
  10.7 22.7 %collective-permute-start = (bf16[2,128,768]{2,1,0:T(8,128)(2,1)S(1)}, bf16[2,128,768]{2,1,0:T(8,128)(2,1)S(1)}, u32[]{:S(2)}, u32[]{:S(2)}) collective-permute-start(bf16[2,128,768]{2,1,0:T(8,128)(2,1)S(1)} %slice.25), channel_id=1, source_target_pairs={{0,1},{1,2},{2,3},{3,4},{4,5},{5,6},{6,7},{7,8},{8,9},{9,10},{10,1... | collective-permute-start | bytes 1179656 | tf_op jit(solution)/shard_map/ppermute | solution.py:19
  21.3 26.8 %all-to-all-start.1 = ((bf16[16,128,128]{2,1,0:T(8,128)(2,1)}), bf16[16,128,128]{2,1,0:T(8,128)(2,1)}, u32[]{:S(2)}, u32[]{:S(2)}) async-start(bf16[16,128,128]{2,1,0:T(8,128)(2,1)} %shard_map.136), calls=%async_computation.1 | async-start | bytes 1048576 | tf_op jit(solution)/shard_map/all_to_all | solution.py:312
  48.2 50.3 %all-to-all-start = ((bf16[16,144,256]{2,1,0:T(8,128)(2,1)}), bf16[16,144,256]{2,1,0:T(8,128)(2,1)S(1)}, u32[]{:S(2)}, u32[]{:S(2)}) async-start(bf16[16,144,256]{2,1,0:T(8,128)(2,1)} %pad_maximum_fusion), calls=%async_computation | async-start | bytes 2359296 | tf_op jit(solution)/shard_map/all_to_all | solution.py:344
  52.6 12.8 %collective-permute-start.2 = (bf16[16,128,128]{2,1,0:T(8,128)(2,1)}, bf16[16,128,128]{2,1,0:T(8,128)(2,1)S(1)}, u32[]{:S(2)}, u32[]{:S(2)}) collective-permute-start(bf16[16,128,128]{2,1,0:T(8,128)(2,1)} %all-to-all-done.1.refs_0_), channel_id=1, source_target_pairs={{0,32},{16,48},{32,64},{48,80},{64,96},{80,112},{96,0},{112,16},{1... | collective-permute-start | bytes 1572872 | tf_op jit(solution)/shard_map/ppermute | solution.py:38
  54.0 11.7 %collective-permute-start.3 = (bf16[16,128,128]{2,1,0:T(8,128)(2,1)}, bf16[16,128,128]{2,1,0:T(8,128)(2,1)S(1)}, u32[]{:S(2)}, u32[]{:S(2)}) collective-permute-start(bf16[16,128,128]{2,1,0:T(8,128)(2,1)} %all-to-all-done.1.refs_0_), channel_id=1, source_target_pairs={{0,96},{16,112},{32,0},{48,16},{64,32},{80,48},{96,64},{112,80},{1... | collective-permute-start | bytes 1572872 | tf_op jit(solution)/shard_map/ppermute | solution.py:38
  55.5 22.9 %collective-permute-start.6 = (bf16[16,128,128]{2,1,0:T(8,128)(2,1)}, bf16[16,128,128]{2,1,0:T(8,128)(2,1)S(1)}, u32[]{:S(2)}, u32[]{:S(2)}) collective-permute-start(bf16[16,128,128]{2,1,0:T(8,128)(2,1)} %all-to-all-done.1.refs_0_), channel_id=1, source_target_pairs={{0,128},{16,144},{32,160},{48,176},{64,192},{80,208},{96,224},{112... | collective-permute-start | bytes 1572872 | tf_op jit(solution)/shard_map/ppermute | solution.py:34
  55.8 22.6 %collective-permute-start.11 = (bf16[16,128,128]{2,1,0:T(8,128)(2,1)}, bf16[16,128,128]{2,1,0:T(8,128)(2,1)S(1)}, u32[]{:S(2)}, u32[]{:S(2)}) collective-permute-start(bf16[16,128,128]{2,1,0:T(8,128)(2,1)} %all-to-all-done.1.refs_0_), channel_id=1, source_target_pairs={{0,16},{16,0},{32,48},{48,32},{64,80},{80,64},{96,112},{112,96},{1... | collective-permute-start | bytes 1572872 | tf_op jit(solution)/shard_map/ppermute | solution.py:30
  65.4 33.1 %copy-start.6 = (bf16[16,128,128]{2,1,0:T(8,128)(2,1)}, bf16[16,128,128]{2,1,0:T(8,128)(2,1)S(1)}, u32[]{:S(2)}) copy-start(bf16[16,128,128]{2,1,0:T(8,128)(2,1)S(1)} %collective-permute-done.2.refs_1_) | copy-start | bytes 1572868
  65.4 7.0 %collective-permute-start.4 = (bf16[8,128,128]{2,1,0:T(8,128)(2,1)S(1)}, bf16[8,128,128]{2,1,0:T(8,128)(2,1)S(1)}, u32[]{:S(2)}, u32[]{:S(2)}) collective-permute-start(bf16[8,128,128]{2,1,0:T(8,128)(2,1)S(1)} %slice.28), channel_id=1, source_target_pairs={{0,32},{16,48},{32,64},{48,80},{64,96},{80,112},{96,0},{112,16},{1... | collective-permute-start | bytes 786440 | tf_op jit(solution)/shard_map/ppermute | solution.py:38
  65.7 32.8 %copy-start.7 = (bf16[16,128,128]{2,1,0:T(8,128)(2,1)}, bf16[16,128,128]{2,1,0:T(8,128)(2,1)S(1)}, u32[]{:S(2)}) copy-start(bf16[16,128,128]{2,1,0:T(8,128)(2,1)S(1)} %collective-permute-done.3.refs_2_) | copy-start | bytes 1572868
  65.7 7.0 %collective-permute-start.5 = (bf16[8,128,128]{2,1,0:T(8,128)(2,1)S(1)}, bf16[8,128,128]{2,1,0:T(8,128)(2,1)S(1)}, u32[]{:S(2)}, u32[]{:S(2)}) collective-permute-start(bf16[8,128,128]{2,1,0:T(8,128)(2,1)S(1)} %slice.29), channel_id=1, source_target_pairs={{0,96},{16,112},{32,0},{48,16},{64,32},{80,48},{96,64},{112,80},{1... | collective-permute-start | bytes 786440 | tf_op jit(solution)/shard_map/ppermute | solution.py:38
  72.4 22.6 %copy-start.14 = (bf16[8,128,128]{2,1,0:T(8,128)(2,1)}, bf16[8,128,128]{2,1,0:T(8,128)(2,1)S(1)}, u32[]{:S(2)}) copy-start(bf16[8,128,128]{2,1,0:T(8,128)(2,1)S(1)} %collective-permute-done.4.refs_3_) | copy-start | bytes 786436
  72.4 13.6 %collective-permute-start.9 = (bf16[8,128,128]{2,1,0:T(8,128)(2,1)S(1)}, bf16[8,128,128]{2,1,0:T(8,128)(2,1)}, u32[]{:S(2)}, u32[]{:S(2)}) collective-permute-start(bf16[8,128,128]{2,1,0:T(8,128)(2,1)S(1)} %collective-permute-done.4.refs_3_), channel_id=1, source_target_pairs={{0,128},{16,144},{32,160},{48,176},{64,192},{80,208},{96,224},{112... | collective-permute-start | bytes 786440 | tf_op jit(solution)/shard_map/ppermute | solution.py:34
  72.7 22.2 %copy-start.15 = (bf16[8,128,128]{2,1,0:T(8,128)(2,1)}, bf16[8,128,128]{2,1,0:T(8,128)(2,1)S(1)}, u32[]{:S(2)}) copy-start(bf16[8,128,128]{2,1,0:T(8,128)(2,1)S(1)} %collective-permute-done.5.refs_4_) | copy-start | bytes 786436
  72.8 18.8 %collective-permute-start.10 = (bf16[8,128,128]{2,1,0:T(8,128)(2,1)S(1)}, bf16[8,128,128]{2,1,0:T(8,128)(2,1)}, u32[]{:S(2)}, u32[]{:S(2)}) collective-permute-start(bf16[8,128,128]{2,1,0:T(8,128)(2,1)S(1)} %collective-permute-done.5.refs_4_), channel_id=1, source_target_pairs={{0,128},{16,144},{32,160},{48,176},{64,192},{80,208},{96,224},{112... | collective-permute-start | bytes 786440 | tf_op jit(solution)/shard_map/ppermute | solution.py:34
  73.9 18.9 %collective-permute-start.14 = (bf16[8,128,128]{2,1,0:T(8,128)(2,1)S(1)}, bf16[8,128,128]{2,1,0:T(8,128)(2,1)}, u32[]{:S(2)}, u32[]{:S(2)}) collective-permute-start(bf16[8,128,128]{2,1,0:T(8,128)(2,1)S(1)} %collective-permute-done.4.refs_3_), channel_id=1, source_target_pairs={{0,16},{16,0},{32,48},{48,32},{64,80},{80,64},{96,112},{112,96},{1... | collective-permute-start | bytes 786440 | tf_op jit(solution)/shard_map/ppermute | solution.py:30
  78.4 16.6 %copy-start.10 = (bf16[16,128,128]{2,1,0:T(8,128)(2,1)}, bf16[16,128,128]{2,1,0:T(8,128)(2,1)S(1)}, u32[]{:S(2)}) copy-start(bf16[16,128,128]{2,1,0:T(8,128)(2,1)S(1)} %collective-permute-done.6.refs_5_) | copy-start | bytes 1572868
  78.4 15.9 %collective-permute-start.7 = (bf16[16,128,128]{2,1,0:T(8,128)(2,1)S(1)}, bf16[16,128,128]{2,1,0:T(8,128)(2,1)}, u32[]{:S(2)}, u32[]{:S(2)}) collective-permute-start(bf16[16,128,128]{2,1,0:T(8,128)(2,1)S(1)} %collective-permute-done.6.refs_5_), channel_id=1, source_target_pairs={{0,32},{16,48},{32,64},{48,80},{64,96},{80,112},{96,0},{112,16},{1... | collective-permute-start | bytes 1572872 | tf_op jit(solution)/shard_map/ppermute | solution.py:38
  78.4 16.6 %copy-start.11 = (bf16[16,128,128]{2,1,0:T(8,128)(2,1)}, bf16[16,128,128]{2,1,0:T(8,128)(2,1)S(1)}, u32[]{:S(2)}) copy-start(bf16[16,128,128]{2,1,0:T(8,128)(2,1)S(1)} %collective-permute-done.11.refs_10_) | copy-start | bytes 1572868
  78.4 16.1 %collective-permute-start.8 = (bf16[16,128,128]{2,1,0:T(8,128)(2,1)S(1)}, bf16[16,128,128]{2,1,0:T(8,128)(2,1)}, u32[]{:S(2)}, u32[]{:S(2)}) collective-permute-start(bf16[16,128,128]{2,1,0:T(8,128)(2,1)S(1)} %collective-permute-done.6.refs_5_), channel_id=1, source_target_pairs={{0,96},{16,112},{32,0},{48,16},{64,32},{80,48},{96,64},{112,80},{1... | collective-permute-start | bytes 1572872 | tf_op jit(solution)/shard_map/ppermute | solution.py:38
  86.0 8.9 %collective-permute-start.16 = (bf16[16,128,128]{2,1,0:T(8,128)(2,1)S(1)}, bf16[16,128,128]{2,1,0:T(8,128)(2,1)S(1)}, u32[]{:S(2)}, u32[]{:S(2)}) collective-permute-start(bf16[16,128,128]{2,1,0:T(8,128)(2,1)S(1)} %collective-permute-done.6.refs_5_), channel_id=1, source_target_pairs={{0,16},{16,0},{32,48},{48,32},{64,80},{80,64},{96,112},{112,96},{1... | collective-permute-start | bytes 1572872 | tf_op jit(solution)/shard_map/ppermute | solution.py:30
  91.6 2.4 %collective-permute-start.15 = (bf16[8,128,128]{2,1,0:T(8,128)(2,1)S(1)}, bf16[8,128,128]{2,1,0:T(8,128)(2,1)S(1)}, u32[]{:S(2)}, u32[]{:S(2)}) collective-permute-start(bf16[8,128,128]{2,1,0:T(8,128)(2,1)S(1)} %collective-permute-done.5.refs_4_), channel_id=1, source_target_pairs={{0,16},{16,0},{32,48},{48,32},{64,80},{80,64},{96,112},{112,96},{1... | collective-permute-start | bytes 786440 | tf_op jit(solution)/shard_map/ppermute | solution.py:30
  92.8 2.2 %collective-permute-start.12 = (bf16[16,128,128]{2,1,0:T(8,128)(2,1)S(1)}, bf16[16,128,128]{2,1,0:T(8,128)(2,1)S(1)}, u32[]{:S(2)}, u32[]{:S(2)}) collective-permute-start(bf16[16,128,128]{2,1,0:T(8,128)(2,1)S(1)} %collective-permute-done.2.refs_1_), channel_id=1, source_target_pairs={{0,16},{16,0},{32,48},{48,32},{64,80},{80,64},{96,112},{112,96},{1... | collective-permute-start | bytes 1572872 | tf_op jit(solution)/shard_map/ppermute | solution.py:30
  93.9 3.3 %collective-permute-start.13 = (bf16[16,128,128]{2,1,0:T(8,128)(2,1)S(1)}, bf16[16,128,128]{2,1,0:T(8,128)(2,1)}, u32[]{:S(2)}, u32[]{:S(2)}) collective-permute-start(bf16[16,128,128]{2,1,0:T(8,128)(2,1)S(1)} %collective-permute-done.3.refs_2_), channel_id=1, source_target_pairs={{0,16},{16,0},{32,48},{48,32},{64,80},{80,64},{96,112},{112,96},{1... | collective-permute-start | bytes 1572872 | tf_op jit(solution)/shard_map/ppermute | solution.py:30
  94.3 4.1 %collective-permute-start.17 = (bf16[16,128,128]{2,1,0:T(8,128)(2,1)}, bf16[16,128,128]{2,1,0:T(8,128)(2,1)}, u32[]{:S(2)}, u32[]{:S(2)}) collective-permute-start(bf16[16,128,128]{2,1,0:T(8,128)(2,1)} %collective-permute-done.7.refs_6_), channel_id=1, source_target_pairs={{0,16},{16,0},{32,48},{48,32},{64,80},{80,64},{96,112},{112,96},{1... | collective-permute-start | bytes 1572872 | tf_op jit(solution)/shard_map/ppermute | solution.py:30
  94.5 4.0 %collective-permute-start.18 = (bf16[16,128,128]{2,1,0:T(8,128)(2,1)}, bf16[16,128,128]{2,1,0:T(8,128)(2,1)}, u32[]{:S(2)}, u32[]{:S(2)}) collective-permute-start(bf16[16,128,128]{2,1,0:T(8,128)(2,1)} %collective-permute-done.8.refs_7_), channel_id=1, source_target_pairs={{0,16},{16,0},{32,48},{48,32},{64,80},{80,64},{96,112},{112,96},{1... | collective-permute-start | bytes 1572872 | tf_op jit(solution)/shard_map/ppermute | solution.py:30
  94.8 3.2 %collective-permute-start.19 = (bf16[8,128,128]{2,1,0:T(8,128)(2,1)}, bf16[8,128,128]{2,1,0:T(8,128)(2,1)}, u32[]{:S(2)}, u32[]{:S(2)}) collective-permute-start(bf16[8,128,128]{2,1,0:T(8,128)(2,1)} %collective-permute-done.9.refs_8_), channel_id=1, source_target_pairs={{0,16},{16,0},{32,48},{48,32},{64,80},{80,64},{96,112},{112,96},{1... | collective-permute-start | bytes 786440 | tf_op jit(solution)/shard_map/ppermute | solution.py:30
  96.5 2.0 %collective-permute-start.20 = (bf16[8,128,128]{2,1,0:T(8,128)(2,1)}, bf16[8,128,128]{2,1,0:T(8,128)(2,1)}, u32[]{:S(2)}, u32[]{:S(2)}) collective-permute-start(bf16[8,128,128]{2,1,0:T(8,128)(2,1)} %collective-permute-done.10.refs_9_), channel_id=1, source_target_pairs={{0,16},{16,0},{32,48},{48,32},{64,80},{80,64},{96,112},{112,96},{1... | collective-permute-start | bytes 786440 | tf_op jit(solution)/shard_map/ppermute | solution.py:30
  97.2 24.6 %copy-start.8 = (bf16[768]{0:T(1024)(128)(2,1)S(1)}, bf16[768]{0:T(1024)(128)(2,1)}, u32[]{:S(2)}) copy-start(bf16[768]{0:T(1024)(128)(2,1)} %param.27) | copy-start | bytes 4612
  113.1 23.7 %all-to-all-start.2 = ((bf16[16,48,256]{2,1,0:T(8,128)(2,1)}), bf16[16,48,256]{2,1,0:T(8,128)(2,1)S(1)}, u32[]{:S(2)}, u32[]{:S(2)}) async-start(bf16[16,48,256]{2,1,0:T(8,128)(2,1)} %shard_map.137), calls=%async_computation.2 | async-start | bytes 786432 | tf_op jit(solution)/shard_map/all_to_all | solution.py:365
  (9 other events, 45.1 us)

commit v3 on v2

--- a/solution.py
+++ b/solution.py
@@ -40,7 +40,7 @@
     )
 
 
-def pair_kernel(pair_ref, weight_ref, out_ref, sum_weights, square_weights, mean_weights, bias_scr):
+def pair_kernel(pair_ref, weight_ref, out_ref, wide_weights, bias_scr):
     step = pl.program_id(0)
     groups, eight, keys, depth = pair_ref.shape
     heads = weight_ref.shape[0]
@@ -54,31 +54,19 @@
         repeated = lax.dot_general(
             weight_ref[...], spread, (((0,), (0,)), ((), ())), preferred_element_type=F32
         )
-        mean_weights[...] = jnp.broadcast_to(
-            jnp.sum(repeated, axis=0, keepdims=True) * (1.0 / depth), mean_weights.shape
-        )
         place = lax.broadcasted_iota(jnp.int32, (depth, width), 1) % eight
         for i in range(eight):
-            own = place == i
-            ones = jnp.where(own, 1.0, 0.0).astype(BF16)
-            sum_weights[i * depth : (i + 1) * depth, :width] = jnp.where(own, repeated, 0.0).astype(BF16)
-            sum_weights[i * depth : (i + 1) * depth, width:] = ones
-            square_weights[2 * i * depth : (2 * i + 1) * depth, :] = ones
-            square_weights[(2 * i + 1) * depth : (2 * i + 2) * depth, :] = ones
-
-    rows = [pair_ref[:, i].reshape(groups * keys, depth) for i in range(eight)]
-    sums = jnp.dot(jnp.concatenate(rows, axis=1), sum_weights[...], preferred_element_type=F32)
-    parts = []
-    for value in rows:
-        wide = value.astype(F32)
-        square = wide * wide
-        high = square.astype(BF16)
-        parts += [high, (square - high.astype(F32)).astype(BF16)]
-    squares = jnp.dot(jnp.concatenate(parts, axis=1), square_weights[...], preferred_element_type=F32)
-    total = sums[:, width:]
-    mean = total * (1.0 / depth)
-    variance = squares * (1.0 / depth) - mean * mean
-    bias = (sums[:, :width] - total * mean_weights[0:1]) * lax.rsqrt(variance + 1e-05)
+            wide_weights[i * depth : (i + 1) * depth, :] = jnp.where(place == i, repeated, 0.0).astype(BF16)
+
+    ones = jnp.ones((depth, depth), BF16)
+    normed = []
+    for i in range(eight):
+        value = pair_ref[:, i].reshape(groups * keys, depth)
+        mean = jnp.dot(value, ones, preferred_element_type=F32) * (1.0 / depth)
+        centered = value.astype(F32) - mean
+        variance = jnp.mean(centered * centered, axis=-1, keepdims=True)
+        normed.append((centered * lax.rsqrt(variance + 1e-05)).astype(BF16))
+    bias = jnp.dot(jnp.concatenate(normed, axis=1), wide_weights[...], preferred_element_type=F32)
     for group in range(groups):
         turned = bias[group * keys : (group + 1) * keys].T
         for head in range(heads):
@@ -96,7 +84,6 @@
     queries, keys, depth = pair_rep.shape
     heads = w_pair.shape[1]
     eight = 8
-    width = heads * eight
     return pl.pallas_call(
         pair_kernel,
         grid=(queries // (eight * groups),),
@@ -107,16 +94,57 @@
         out_specs=pl.BlockSpec((heads, keys, queries), lambda i: (0, 0, 0)),
         out_shape=jax.ShapeDtypeStruct((heads, keys, queries), BF16),
         scratch_shapes=[
-            pltpu.VMEM((eight * depth, 2 * width), BF16),
-            pltpu.VMEM((2 * eight * depth, width), BF16),
-            pltpu.VMEM((8, width), F32),
+            pltpu.VMEM((eight * depth, heads * eight), BF16),
             pltpu.VMEM((heads, queries, keys), F32),
         ],
-        compiler_params=pltpu.CompilerParams(vmem_limit_bytes=40 * 1024 * 1024),
+        compiler_params=pltpu.CompilerParams(vmem_limit_bytes=60 * 1024 * 1024),
         cost_estimate=pl.CostEstimate(
             flops=2 * queries * keys * depth * 256, bytes_accessed=5 * 1024 * 1024, transcendentals=queries * keys
         ),
     )(pair_rep.reshape(queries // eight, eight, keys, depth), w_pair.T)
+
+
+def atom_kernel(feats_ref, relative_ref, weight_ref, own_ref, count_ref, sent_ref):
+    samples, atoms, _ = feats_ref.shape
+    tok, width = count_ref.shape[0], weight_ref.shape[1]
+    slots = lax.broadcasted_iota(jnp.int32, (2 * tok, atoms), 0)
+    member = jnp.where(slots == relative_ref[...], 1.0, 0.0)
+    counts = jnp.sum(member, axis=1, keepdims=True)
+    member = member.astype(BF16)
+    count_ref[...] = jnp.broadcast_to(counts[:tok], count_ref.shape)
+    above = jnp.broadcast_to(counts[tok:], count_ref.shape)
+    high = jnp.floor(above * (1.0 / 256.0)) * 256.0
+    lane = lax.broadcasted_iota(jnp.int32, count_ref.shape, 1)
+    tail = jnp.where(lane == 0, high, jnp.where(lane == 1, above - high, 0.0)).astype(BF16)
+    for sample in range(samples):
+        hidden = jnp.dot(feats_ref[sample], weight_ref[...], preferred_element_type=F32)
+        hidden = jnp.maximum(hidden, 0.0).astype(BF16)
+        partial = jnp.dot(member, hidden, preferred_element_type=F32).astype(BF16)
+        own_ref[sample] = partial[:tok]
+        sent_ref[sample, :, :width] = partial[tok:]
+        sent_ref[sample, :, width:] = tail
+
+
+def token_kernel(own_ref, count_ref, came_ref, gate_ref, shift_ref, wq_ref, wk_ref, wv_ref, out_ref):
+    samples, tok, width = own_ref.shape
+    heads, size = out_ref.shape[0], out_ref.shape[1] // 3
+    parts = []
+    for sample in range(samples):
+        tail = came_ref[sample, :, width:].astype(F32)
+        count = count_ref[:, 0:1] + tail[:, 0:1] + tail[:, 1:2]
+        summed = own_ref[sample].astype(F32) + came_ref[sample, :, :width].astype(F32)
+        tokens = summed / count
+        average = jnp.mean(tokens, axis=-1, keepdims=True)
+        centered = tokens - average
+        variance = jnp.mean(centered * centered, axis=-1, keepdims=True)
+        normed = centered * lax.rsqrt(variance + 1e-05)
+        parts.append((gate_ref[sample] * normed + shift_ref[sample]).astype(BF16))
+    normed = jnp.concatenate(parts, axis=0)
+    for kind, weight_ref in enumerate((wq_ref, wk_ref, wv_ref)):
+        result = jnp.dot(normed, weight_ref[...], preferred_element_type=F32)
+        turned = result.T.astype(BF16)
+        for head in range(heads):
+            out_ref[head, kind * size : (kind + 1) * size, :] = turned[head * size : (head + 1) * size]
 
 
 def attention_kernel(order_ref, kv_ref, *refs):
@@ -135,12 +163,11 @@
     def copies(step):
         found = []
         for place in range(blocks):
-            five, kind = place // 4 * 5, place % 4
-            start = step * per_step
-            if kind == 3:
-                found.append((pieces[five + 3 + start * 2 // blocks], start % (blocks // 2)))
+            first, start = place + place // 8, step * per_step
+            if place % 8 == 7:
+                found.append((pieces[first + start * 2 // blocks], start % (blocks // 2)))
             else:
-                found.append((pieces[five + kind], start))
+                found.append((pieces[first], start))
         return [
             pltpu.make_async_copy(
                 piece.at[pl.ds(start, per_step)],
@@ -269,7 +296,7 @@
             pltpu.SemaphoreType.DMA((total // ROWS + 1, blocks)),
             pltpu.VMEM(kv.shape, BF16),
         ],
-        compiler_params=pltpu.CompilerParams(vmem_limit_bytes=60 * 1024 * 1024),
+        compiler_params=pltpu.CompilerParams(vmem_limit_bytes=36 * 1024 * 1024),
         cost_estimate=pl.CostEstimate(
             flops=8 * total * total * 64, bytes_accessed=12 * 1024 * 1024, transcendentals=2 * total * total
         ),
@@ -309,23 +336,21 @@
     sample_place = lax.axis_index("sample")
 
     bias_local = pair_bias_local(pair_rep, w_pair)
+    bias_local, atom_feats = lax.optimization_barrier((bias_local, atom_feats))
     mine = lax.all_to_all(bias_local, "seq", 0, 0, tiled=True)
 
-    hidden = jax.nn.relu(
-        jnp.einsum("sac,cd->sad", atom_feats, w_atom, preferred_element_type=F32)
-    ).astype(BF16)
-    relative = atom_token - seq_place * tok_local
-    slot_ids = lax.broadcasted_iota(jnp.int32, (2 * tok_local, atom_local), 0)
-    member = slot_ids == relative[None, :]
-    partial_value = jnp.einsum("ta,sad->std", member.astype(BF16), hidden, preferred_element_type=F32)
-    counts = jnp.sum(member.astype(F32), axis=1)[None, :]
-    rounded = partial_value.astype(BF16)
-    below_part, below_count = from_behind(
-        (rounded[:, tok_local:], counts[:, tok_local:]), "seq", 1
-    )
-    summed = rounded[:, :tok_local].astype(F32) + below_part.astype(F32)
-    token_counts = counts[:, :tok_local] + below_count
-    tokens = summed / token_counts[:, :, None]
+    relative = (atom_token - seq_place * tok_local)[None, :]
+    own, counts, sent = pl.pallas_call(
+        atom_kernel,
+        out_shape=(
+            jax.ShapeDtypeStruct((samp_local, tok_local, model_width), BF16),
+            jax.ShapeDtypeStruct((tok_local, 128), F32),
+            jax.ShapeDtypeStruct((samp_local, tok_local, model_width + 128), BF16),
+        ),
+        compiler_params=pltpu.CompilerParams(vmem_limit_bytes=40 * 1024 * 1024),
+        cost_estimate=pl.CostEstimate(flops=4 * 10**9, bytes_accessed=3 * 1024 * 1024, transcendentals=0),
+    )(atom_feats, relative, w_atom)
+    came = from_behind(sent, "seq", 1)
     cond = layer_norm(single_cond.astype(F32)).astype(BF16)
     out_gate = jax.nn.sigmoid(
         jnp.einsum("std,de->ste", cond, w_outgate, preferred_element_type=F32)
@@ -333,23 +358,19 @@
     ).reshape(samp_local * tok_local, model_width)
     gate_ada = jax.nn.sigmoid(jnp.einsum("stc,cd->std", cond, w_ada_gate, preferred_element_type=F32))
     shift_ada = jnp.einsum("stc,cd->std", cond, w_ada_shift, preferred_element_type=F32)
-    normed = (gate_ada * layer_norm(tokens) + shift_ada).astype(BF16)
-    flat = normed.reshape(samp_local * tok_local, model_width)
-
-    def heads_of(weight):
-        out = jnp.dot(flat, weight, preferred_element_type=F32).astype(BF16)
-        return out.T.reshape(head_count, head_size, samp_local * tok_local)
-
-    sent = jnp.concatenate([heads_of(w_query), heads_of(w_key), heads_of(w_value)], axis=1)
-    kv = lax.all_to_all(sent, "seq", 0, 0, tiled=True)
+    heads_sent = pl.pallas_call(
+        token_kernel,
+        out_shape=jax.ShapeDtypeStruct((head_count, 3 * head_size, samp_local * tok_local), BF16),
+        compiler_params=pltpu.CompilerParams(vmem_limit_bytes=40 * 1024 * 1024),
+        cost_estimate=pl.CostEstimate(flops=3 * 10**9, bytes_accessed=6 * 1024 * 1024, transcendentals=0),
+    )(own, counts, came, gate_ada, shift_ada, w_query, w_key, w_value)
+    kv = lax.all_to_all(heads_sent, "seq", 0, 0, tiled=True)
 
     half = mine.shape[0] // 2
-    across = swap_x(mine)
-    up, down = shift_y(mine, 1), shift_y(mine, -1)
-    far = [shift_y(up[:half], 1), shift_y(down[half:], -1)]
-    across_up, across_down = shift_y(across, 1), shift_y(across, -1)
-    across_far = [swap_x(part) for part in far]
-    pieces = [mine, up, down, *far, across, across_up, across_down, *across_far]
+    across, up, down = swap_x(mine), shift_y(mine, 1), shift_y(mine, -1)
+    far, across_up, across_down = shift_y(up, 1), swap_x(up), shift_y(across, -1)
+    across_far = [shift_y(across_up[:half], 1), shift_y(across_down[half:], -1)]
+    pieces = [mine, up, down, far, across, across_up, across_down, *across_far]
     pieces = pieces + [swap_core(piece) for piece in pieces]
     x_lo, y, core = sample_place // 8, sample_place // 2 % 4, sample_place % 2
     order = jnp.stack(

time: 139 us -> 157 us (1.13)
  Pallas kernels: 19.8 us -> 32 us
  matrix products: 11.8 us -> 2.56 us
  local copies, waits for them, and re-layouts: 6.37 us -> 13 us
  waiting for transfers between devices: 42.5 us -> 48.6 us
  starting transfers between devices: 54.3 us -> 59.5 us
  other arithmetic: 2.94 us -> 0.33 us
    dot_general x4 -> x0, matrix products: 8.1 us -> none  [the longest x1 4.12 us: per_device(): jnp.einsum('ta,sad->std', member.astype(BF16), hidden, preferred_element_...]
    unnamed x34 -> x50, local copies, waits for them, and re-layouts: 5.18 us -> 12.9 us
    all_to_all x1, starting transfers between devices: 8.69 us -> 15.1 us  [per_device(): lax.all_to_all(attended, 'seq', 0, 0, tiled=True).reshape(model_width, -1)]
    pallas_call x1, Pallas kernels: 13.6 us -> 19.9 us  [attention(): pl.pallas_call(attention_kernel, in_specs=[pl.BlockSpec(memory_space=pltp...]
    pallas_call x0 -> x2, Pallas kernels: none -> 4.44 us  [the longest x1 2.64 us: per_device(): pl.pallas_call(token_kernel, out_shape=jax.ShapeDtypeStruct((head_count,...]
    ppermute x3 -> x2, waiting for transfers between devices: 8.46 us -> 12.3 us  [swap_x(): return lax.ppermute(value, 'sample', [(i, i ^ 8) for i in range(16)])]
    ppermute x2 -> x1, starting transfers between devices: 8.99 us -> 5.64 us  [from_behind(): lax.ppermute(value, axis, [(source, source + steps) for source in range(i...]
    all_to_all x1, waiting for transfers between devices: 7.79 us -> 10.8 us  [per_device(): mine = lax.all_to_all(bias_local, 'seq', 0, 0, tiled=True)]
  transfers between devices with their start and end apart: 24 -> 21, of which waited for: 9 -> 8; matrix products, arithmetic and copies ran while one was open for 11% -> 2% of each run, Pallas kernels for 4% -> 2%
where the time goes in v3:
time: 157 us; the launch traced here: 156 us
  starting transfers between devices  59.5 us (38%)
  waiting for transfers between devices  48.6 us (31%)
  Pallas kernels  32 us (20%)
  local copies, waits for them, and re-layouts  13 us (8%)
  matrix products  2.56 us (2%)
    pallas_call x1, Pallas kernels, attention(): pl.pallas_call(attention_kernel, in_specs=[pl.BlockSpec(memory_space=pltp...  19.9 us
    all_to_all x1, starting transfers between devices, per_device(): lax.all_to_all(attended, 'seq', 0, 0, tiled=True).reshape(model_width, -1)  15.1 us
    ppermute x9, starting transfers between devices, swap_core(): return lax.ppermute(value, 'sample', [(i, i ^ 1) for i in range(16)])  13.5 us
    all_to_all x1, waiting for transfers between devices, per_device(): lax.all_to_all(attended, 'seq', 0, 0, tiled=True).reshape(model_width, -1)  13.3 us
    unnamed x50, local copies, waits for them, and re-layouts  12.9 us
    ppermute x2, waiting for transfers between devices, swap_x(): return lax.ppermute(value, 'sample', [(i, i ^ 8) for i in range(16)])  12.3 us
    all_to_all x1, waiting for transfers between devices, per_device(): mine = lax.all_to_all(bias_local, 'seq', 0, 0, tiled=True)  10.8 us
    ppermute x6, waiting for transfers between devices, shift_y(): lax.ppermute(value, 'sample', [(i, i & 9 | ((i >> 1) + steps & 3) << 1) f...  10.6 us
  transfers between devices with their start and end apart: 21, of which 8 were waited for; matrix products, arithmetic and copies ran while one was open for 2% of the time, Pallas kernels for 2%

profile of v3, /device:TPU:1, one launch (start us, length us, event | category | flops | bytes accessed | tf_op | source)
XLA Modules:
  0.0 156.3 jit_solution(6400724140730580210)
XLA Ops:
  0.0 6.4 %shard_map.136 = bf16[16,128,128]{2,1,0:T(8,128)(2,1)} custom-call(bf16[16,8,128,128]{3,2,1,0:T(8,128)(2,1)} %bitcast.34, bf16[16,128]{1,0:T(8,128)(2,1)} %bitcast.35), custom_call_target="tpu_custom_call" | custom-call | flops 1073741824 | bytes 5242880 | tf_op jit(solution)/shard_map/pallas_call | solution.py:87
  6.4 1.8 %shard_map.137 = (bf16[2,128,768]{2,1,0:T(8,128)(2,1)S(1)}, f32[128,128]{1,0:T(8,128)S(1)}, bf16[2,128,896]{2,1,0:T(8,128)(2,1)S(1)}) custom-call(bf16[2,1024,128]{2,1,0:T(8,128)(2,1)S(1)} %copy-done.5, s32[1,1024]{1,0:T(1,128)S(1)} %bitcast.33, bf16[128,768]{1,0:T(8,128)(2,1)S(1)} %copy-done.20), custom_call_target="tpu_custom_call" | custom-call | flops 4000000000 | bytes 3145728 | tf_op jit(solution)/shard_map/pallas_call | solution.py:343
  8.2 5.6 %collective-permute-start = (bf16[2,128,896]{2,1,0:T(8,128)(2,1)S(1)}, bf16[2,128,896]{2,1,0:T(8,128)(2,1)S(1)}, u32[]{:S(2)}, u32[]{:S(2)}) collective-permute-start(bf16[2,128,896]{2,1,0:T(8,128)(2,1)S(1)} %get-tuple-element.13), channel_id=1, source_target_pairs={{0,1},{1,2},{2,3},{3,4},{4,5},{5,6},{6,7},{7,8},{8,9},{9,10},{10,1... | collective-permute-start | bytes 1376264 | tf_op jit(solution)/shard_map/ppermute | solution.py:19
  13.9 8.7 %all-to-all-start.1 = ((bf16[16,128,128]{2,1,0:T(8,128)(2,1)}), bf16[16,128,128]{2,1,0:T(8,128)(2,1)S(1)}, u32[]{:S(2)}, u32[]{:S(2)}) async-start(bf16[16,128,128]{2,1,0:T(8,128)(2,1)} %shard_map.136), calls=%async_computation.1 | async-start | bytes 1048576 | tf_op jit(solution)/shard_map/all_to_all | solution.py:340
  25.4 2.6 %shard_map.138 = bf16[16,144,256]{2,1,0:T(8,128)(2,1)} custom-call(bf16[2,128,768]{2,1,0:T(8,128)(2,1)S(1)} %get-tuple-element.11.own_ref, f32[128,128]{1,0:T(8,128)S(1)} %get-tuple-element.12.count_ref, bf16[2,128,896]{2,1,0:T(8,128)(2,1)S(1)} %collective-permute-done.came_ref, f32[2,128,768]{2,1,0:T(8,128)S(1)} %fusion.4.gate_ref, ...), custom_call_target="tpu_custom_call" | custom-call | flops 3000000000 | bytes 6291456 | tf_op jit(solution)/shard_map/pallas_call | solution.py:361
  28.1 10.8 %all-to-all-done.1.refs_0_ = bf16[16,128,128]{2,1,0:T(8,128)(2,1)S(1)} async-done(((bf16[16,128,128]{2,1,0:T(8,128)(2,1)}), bf16[16,128,128]{2,1,0:T(8,128)(2,1)S(1)}, u32[]{:S(2)}, u32[]{:S(2)}) %all-to-all-start.1) | async-done | bytes 524320 | tf_op jit(solution)/shard_map/all_to_all | solution.py:340
  38.8 6.5 %all-to-all-start = ((bf16[16,144,256]{2,1,0:T(8,128)(2,1)}), bf16[16,144,256]{2,1,0:T(8,128)(2,1)S(1)}, u32[]{:S(2)}, u32[]{:S(2)}) async-start(bf16[16,144,256]{2,1,0:T(8,128)(2,1)} %shard_map.138), calls=%async_computation | async-start | bytes 2359296 | tf_op jit(solution)/shard_map/all_to_all | solution.py:367
  45.3 1.4 collective-permute-start.1
  46.7 1.2 collective-permute-start.4
  47.9 1.5 collective-permute-start.2
  49.4 8.6 %collective-permute-done.1.refs_1_ = bf16[16,128,128]{2,1,0:T(8,128)(2,1)S(1)} collective-permute-done((bf16[16,128,128]{2,1,0:T(8,128)(2,1)S(1)}, bf16[16,128,128]{2,1,0:T(8,128)(2,1)S(1)}, u32[]{:S(2)}, u32[]{:S(2)}) %collective-permute-start.1) | collective-permute-done | bytes 524320 | tf_op jit(solution)/shard_map/ppermute | solution.py:38
  58.0 1.2 collective-permute-start.5
  60.1 1.8 %collective-permute-start.6 = (bf16[16,128,128]{2,1,0:T(8,128)(2,1)S(1)}, bf16[16,128,128]{2,1,0:T(8,128)(2,1)S(1)}, u32[]{:S(2)}, u32[]{:S(2)}) collective-permute-start(bf16[16,128,128]{2,1,0:T(8,128)(2,1)S(1)} %collective-permute-done.4.refs_4_), channel_id=1, source_target_pairs={{0,96},{16,112},{32,0},{48,16},{64,32},{80,48},{96,64},{112,80},{1... | collective-permute-start | bytes 1572872 | tf_op jit(solution)/shard_map/ppermute | solution.py:38
  61.9 8.4 %collective-permute-start.9 = (bf16[16,128,128]{2,1,0:T(8,128)(2,1)S(1)}, bf16[16,128,128]{2,1,0:T(8,128)(2,1)S(1)}, u32[]{:S(2)}, u32[]{:S(2)}) collective-permute-start(bf16[16,128,128]{2,1,0:T(8,128)(2,1)S(1)} %all-to-all-done.1.refs_0_), channel_id=1, source_target_pairs={{0,16},{16,0},{32,48},{48,32},{64,80},{80,64},{96,112},{112,96},{1... | collective-permute-start | bytes 1572872 | tf_op jit(solution)/shard_map/ppermute | solution.py:30
  71.0 11.4 %collective-permute-done.5.refs_5_ = bf16[16,128,128]{2,1,0:T(8,128)(2,1)S(1)} collective-permute-done((bf16[16,128,128]{2,1,0:T(8,128)(2,1)S(1)}, bf16[16,128,128]{2,1,0:T(8,128)(2,1)S(1)}, u32[]{:S(2)}, u32[]{:S(2)}) %collective-permute-start.5) | collective-permute-done | bytes 524320 | tf_op jit(solution)/shard_map/ppermute | solution.py:34
  82.4 1.7 %collective-permute-start.13 = (bf16[16,128,128]{2,1,0:T(8,128)(2,1)S(1)}, bf16[16,128,128]{2,1,0:T(8,128)(2,1)S(1)}, u32[]{:S(2)}, u32[]{:S(2)}) collective-permute-start(bf16[16,128,128]{2,1,0:T(8,128)(2,1)S(1)} %collective-permute-done.4.refs_4_), channel_id=1, source_target_pairs={{0,16},{16,0},{32,48},{48,32},{64,80},{80,64},{96,112},{112,96},{1... | collective-permute-start | bytes 1572872 | tf_op jit(solution)/shard_map/ppermute | solution.py:30
  85.8 1.3 collective-permute-start.7
  87.1 1.4 collective-permute-start.8
  89.3 1.1 collective-permute-start.14
  92.5 2.0 %collective-permute-done.7.refs_7_ = bf16[8,128,128]{2,1,0:T(8,128)(2,1)} collective-permute-done((bf16[8,128,128]{2,1,0:T(8,128)(2,1)S(1)}, bf16[8,128,128]{2,1,0:T(8,128)(2,1)}, u32[]{:S(2)}, u32[]{:S(2)}) %collective-permute-start.7) | collective-permute-done | bytes 262176 | tf_op jit(solution)/shard_map/ppermute | solution.py:38
  94.5 1.4 collective-permute-start.16
  96.0 1.3 collective-permute-done.16.refs_16_
  98.8 1.0 copy-done.9
  99.8 1.0 copy-done.11
  100.9 1.0 copy-done.13
  101.9 1.0 copy-done.15
  104.0 1.0 copy-done.19
  105.0 19.9 %shard_map.139 = bf16[16,48,256]{2,1,0:T(8,128)(2,1)} custom-call(s32[16]{0:T(128)S(1)} %stack.67.order_ref, bf16[16,144,256]{2,1,0:T(8,128)(2,1)S(1)} %all-to-all-done.kv_ref, bf16[16,128,128]{2,1,0:T(8,128)(2,1)S(1)} %all-to-all-done.1.refs_0_, bf16[16,128,128]{2,1,0:T(8,128)(2,1)S(1)} %copy-done.7, bf16[16,128,128]{2,1,0:T(8,128)(2,1)S(1)} %copy-done.11, ...), custom_call_target="tpu_custom_call" | custom-call | flops 2147483648 | bytes 12582912 | tf_op jit(solution)/shard_map/pallas_call | solution.py:282
  124.9 15.1 %all-to-all-start.2 = ((bf16[16,48,256]{2,1,0:T(8,128)(2,1)}), bf16[16,48,256]{2,1,0:T(8,128)(2,1)S(1)}, u32[]{:S(2)}, u32[]{:S(2)}) async-start(bf16[16,48,256]{2,1,0:T(8,128)(2,1)} %shard_map.139), calls=%async_computation.2 | async-start | bytes 786432 | tf_op jit(solution)/shard_map/all_to_all | solution.py:386
  140.0 1.7 %fusion.6 = f32[2,128,768]{2,1,0:T(8,128)S(1)} fusion(bf16[384,768]{1,0:T(8,128)(2,1)} %param.26, f32[768]{0:T(1024)S(1)} %convert_element_type.11, bf16[2,128,384]{2,1,0:T(8,128)(2,1)S(1)} %copy-done.21, f32[2,128]{1,0:T(2,128)S(1)} %add_rsqrt_fusion, f32[2,128]{1,0:T(2,128)S(1)} %broadcast_multiply_fusion), kind=kOutput, calls=%fused_computation.8 | convolution fusion | flops 152174592 | bytes 1577984 | tf_op jit(solution)/shard_map/std,de->ste/dot_general | solution.py:356
  141.7 13.3 %all-to-all-done.2 = bf16[16,48,256]{2,1,0:T(8,128)(2,1)S(1)} async-done(((bf16[16,48,256]{2,1,0:T(8,128)(2,1)}), bf16[16,48,256]{2,1,0:T(8,128)(2,1)S(1)}, u32[]{:S(2)}, u32[]{:S(2)}) %all-to-all-start.2) | async-done | bytes 393248 | tf_op jit(solution)/shard_map/all_to_all | solution.py:386
  155.0 1.3 shard_map.140
  (77 shorter events, 11.5 us)
Async XLA Ops:
  0.0 22.9 %copy-start = (bf16[384,768]{1,0:T(8,128)(2,1)S(1)}, bf16[384,768]{1,0:T(8,128)(2,1)}, u32[]{:S(2)}) copy-start(bf16[384,768]{1,0:T(8,128)(2,1)} %param.19) | copy-start | bytes 1769476
  0.0 6.4 %copy-start.23 = (s32[1024]{0:T(1024)S(1)}, s32[1024]{0:T(1024)}, u32[]{:S(2)}) copy-start(s32[1024]{0:T(1024)} %param.15) | copy-start | bytes 12292
  0.0 6.4 %copy-start.5 = (bf16[2,1024,128]{2,1,0:T(8,128)(2,1)S(1)}, bf16[2,1024,128]{2,1,0:T(8,128)(2,1)}, u32[]{:S(2)}) copy-start(bf16[2,1024,128]{2,1,0:T(8,128)(2,1)} %feats_ref) | copy-start | bytes 1572868
  0.0 6.4 %copy-start.20 = (bf16[128,768]{1,0:T(8,128)(2,1)S(1)}, bf16[128,768]{1,0:T(8,128)(2,1)}, u32[]{:S(2)}) copy-start(bf16[128,768]{1,0:T(8,128)(2,1)} %weight_ref.2) | copy-start | bytes 589828
  8.2 14.3 %copy-start.21 = (bf16[2,128,384]{2,1,0:T(8,128)(2,1)S(1)}, bf16[2,128,384]{2,1,0:T(8,128)(2,1)}, u32[]{:S(2)}) copy-start(bf16[2,128,384]{2,1,0:T(8,128)(2,1)} %param.16) | copy-start | bytes 589828
  8.2 16.2 %collective-permute-start = (bf16[2,128,896]{2,1,0:T(8,128)(2,1)S(1)}, bf16[2,128,896]{2,1,0:T(8,128)(2,1)S(1)}, u32[]{:S(2)}, u32[]{:S(2)}) collective-permute-start(bf16[2,128,896]{2,1,0:T(8,128)(2,1)S(1)} %get-tuple-element.13), channel_id=1, source_target_pairs={{0,1},{1,2},{2,3},{3,4},{4,5},{5,6},{6,7},{7,8},{8,9},{9,10},{10,1... | collective-permute-start | bytes 1376264 | tf_op jit(solution)/shard_map/ppermute | solution.py:19
  13.9 25.0 %all-to-all-start.1 = ((bf16[16,128,128]{2,1,0:T(8,128)(2,1)}), bf16[16,128,128]{2,1,0:T(8,128)(2,1)S(1)}, u32[]{:S(2)}, u32[]{:S(2)}) async-start(bf16[16,128,128]{2,1,0:T(8,128)(2,1)} %shard_map.136), calls=%async_computation.1 | async-start | bytes 1048576 | tf_op jit(solution)/shard_map/all_to_all | solution.py:340
  22.9 1.5 copy-start.3
  22.9 1.8 %copy-start.4 = (bf16[768,768]{1,0:T(8,128)(2,1)S(1)}, bf16[768,768]{1,0:T(8,128)(2,1)}, u32[]{:S(2)}) copy-start(bf16[768,768]{1,0:T(8,128)(2,1)} %wv_ref.1) | copy-start | bytes 3538948
  38.8 58.9 %all-to-all-start = ((bf16[16,144,256]{2,1,0:T(8,128)(2,1)}), bf16[16,144,256]{2,1,0:T(8,128)(2,1)S(1)}, u32[]{:S(2)}, u32[]{:S(2)}) async-start(bf16[16,144,256]{2,1,0:T(8,128)(2,1)} %shard_map.138), calls=%async_computation | async-start | bytes 2359296 | tf_op jit(solution)/shard_map/all_to_all | solution.py:367
  45.3 12.7 %collective-permute-start.1 = (bf16[16,128,128]{2,1,0:T(8,128)(2,1)S(1)}, bf16[16,128,128]{2,1,0:T(8,128)(2,1)S(1)}, u32[]{:S(2)}, u32[]{:S(2)}) collective-permute-start(bf16[16,128,128]{2,1,0:T(8,128)(2,1)S(1)} %all-to-all-done.1.refs_0_), channel_id=1, source_target_pairs={{0,32},{16,48},{32,64},{48,80},{64,96},{80,112},{96,0},{112,16},{1... | collective-permute-start | bytes 1572872 | tf_op jit(solution)/shard_map/ppermute | solution.py:38
  46.7 13.4 %collective-permute-start.4 = (bf16[16,128,128]{2,1,0:T(8,128)(2,1)S(1)}, bf16[16,128,128]{2,1,0:T(8,128)(2,1)S(1)}, u32[]{:S(2)}, u32[]{:S(2)}) collective-permute-start(bf16[16,128,128]{2,1,0:T(8,128)(2,1)S(1)} %all-to-all-done.1.refs_0_), channel_id=1, source_target_pairs={{0,128},{16,144},{32,160},{48,176},{64,192},{80,208},{96,224},{112... | collective-permute-start | bytes 1572872 | tf_op jit(solution)/shard_map/ppermute | solution.py:34
  47.9 22.7 %collective-permute-start.2 = (bf16[16,128,128]{2,1,0:T(8,128)(2,1)S(1)}, bf16[16,128,128]{2,1,0:T(8,128)(2,1)S(1)}, u32[]{:S(2)}, u32[]{:S(2)}) collective-permute-start(bf16[16,128,128]{2,1,0:T(8,128)(2,1)S(1)} %all-to-all-done.1.refs_0_), channel_id=1, source_target_pairs={{0,96},{16,112},{32,0},{48,16},{64,32},{80,48},{96,64},{112,80},{1... | collective-permute-start | bytes 1572872 | tf_op jit(solution)/shard_map/ppermute | solution.py:38
  58.0 33.1 %copy-start.6 = (bf16[16,128,128]{2,1,0:T(8,128)(2,1)}, bf16[16,128,128]{2,1,0:T(8,128)(2,1)S(1)}, u32[]{:S(2)}) copy-start(bf16[16,128,128]{2,1,0:T(8,128)(2,1)S(1)} %collective-permute-done.1.refs_1_) | copy-start | bytes 1572868
  58.0 24.4 %collective-permute-start.5 = (bf16[16,128,128]{2,1,0:T(8,128)(2,1)S(1)}, bf16[16,128,128]{2,1,0:T(8,128)(2,1)S(1)}, u32[]{:S(2)}, u32[]{:S(2)}) collective-permute-start(bf16[16,128,128]{2,1,0:T(8,128)(2,1)S(1)} %collective-permute-done.1.refs_1_), channel_id=1, source_target_pairs={{0,128},{16,144},{32,160},{48,176},{64,192},{80,208},{96,224},{112... | collective-permute-start | bytes 1572872 | tf_op jit(solution)/shard_map/ppermute | solution.py:34
  60.1 31.1 %copy-start.8 = (bf16[16,128,128]{2,1,0:T(8,128)(2,1)}, bf16[16,128,128]{2,1,0:T(8,128)(2,1)S(1)}, u32[]{:S(2)}) copy-start(bf16[16,128,128]{2,1,0:T(8,128)(2,1)S(1)} %collective-permute-done.4.refs_4_) | copy-start | bytes 1572868
  60.1 24.0 %collective-permute-start.6 = (bf16[16,128,128]{2,1,0:T(8,128)(2,1)S(1)}, bf16[16,128,128]{2,1,0:T(8,128)(2,1)S(1)}, u32[]{:S(2)}, u32[]{:S(2)}) collective-permute-start(bf16[16,128,128]{2,1,0:T(8,128)(2,1)S(1)} %collective-permute-done.4.refs_4_), channel_id=1, source_target_pairs={{0,96},{16,112},{32,0},{48,16},{64,32},{80,48},{96,64},{112,80},{1... | collective-permute-start | bytes 1572872 | tf_op jit(solution)/shard_map/ppermute | solution.py:38
  61.9 23.1 %collective-permute-start.9 = (bf16[16,128,128]{2,1,0:T(8,128)(2,1)S(1)}, bf16[16,128,128]{2,1,0:T(8,128)(2,1)S(1)}, u32[]{:S(2)}, u32[]{:S(2)}) collective-permute-start(bf16[16,128,128]{2,1,0:T(8,128)(2,1)S(1)} %all-to-all-done.1.refs_0_), channel_id=1, source_target_pairs={{0,16},{16,0},{32,48},{48,32},{64,80},{80,64},{96,112},{112,96},{1... | collective-permute-start | bytes 1572872 | tf_op jit(solution)/shard_map/ppermute | solution.py:30
  70.3 16.8 %collective-permute-start.3 = (bf16[16,128,128]{2,1,0:T(8,128)(2,1)S(1)}, bf16[16,128,128]{2,1,0:T(8,128)(2,1)}, u32[]{:S(2)}, u32[]{:S(2)}) collective-permute-start(bf16[16,128,128]{2,1,0:T(8,128)(2,1)S(1)} %collective-permute-done.1.refs_1_), channel_id=1, source_target_pairs={{0,32},{16,48},{32,64},{48,80},{64,96},{80,112},{96,0},{112,16},{1... | collective-permute-start | bytes 1572872 | tf_op jit(solution)/shard_map/ppermute | solution.py:38
  70.6 17.9 %collective-permute-start.10 = (bf16[16,128,128]{2,1,0:T(8,128)(2,1)S(1)}, bf16[16,128,128]{2,1,0:T(8,128)(2,1)S(1)}, u32[]{:S(2)}, u32[]{:S(2)}) collective-permute-start(bf16[16,128,128]{2,1,0:T(8,128)(2,1)S(1)} %collective-permute-done.1.refs_1_), channel_id=1, source_target_pairs={{0,16},{16,0},{32,48},{48,32},{64,80},{80,64},{96,112},{112,96},{1... | collective-permute-start | bytes 1572872 | tf_op jit(solution)/shard_map/ppermute | solution.py:30
  82.4 8.0 %collective-permute-start.13 = (bf16[16,128,128]{2,1,0:T(8,128)(2,1)S(1)}, bf16[16,128,128]{2,1,0:T(8,128)(2,1)S(1)}, u32[]{:S(2)}, u32[]{:S(2)}) collective-permute-start(bf16[16,128,128]{2,1,0:T(8,128)(2,1)S(1)} %collective-permute-done.4.refs_4_), channel_id=1, source_target_pairs={{0,16},{16,0},{32,48},{48,32},{64,80},{80,64},{96,112},{112,96},{1... | collective-permute-start | bytes 1572872 | tf_op jit(solution)/shard_map/ppermute | solution.py:30
  84.1 7.0 %collective-permute-start.11 = (bf16[16,128,128]{2,1,0:T(8,128)(2,1)S(1)}, bf16[16,128,128]{2,1,0:T(8,128)(2,1)S(1)}, u32[]{:S(2)}, u32[]{:S(2)}) collective-permute-start(bf16[16,128,128]{2,1,0:T(8,128)(2,1)S(1)} %collective-permute-done.2.refs_2_), channel_id=1, source_target_pairs={{0,16},{16,0},{32,48},{48,32},{64,80},{80,64},{96,112},{112,96},{1... | collective-permute-start | bytes 1572872 | tf_op jit(solution)/shard_map/ppermute | solution.py:30
  85.8 8.7 %collective-permute-start.7 = (bf16[8,128,128]{2,1,0:T(8,128)(2,1)S(1)}, bf16[8,128,128]{2,1,0:T(8,128)(2,1)}, u32[]{:S(2)}, u32[]{:S(2)}) collective-permute-start(bf16[8,128,128]{2,1,0:T(8,128)(2,1)S(1)} %slice.8), channel_id=1, source_target_pairs={{0,32},{16,48},{32,64},{48,80},{64,96},{80,112},{96,0},{112,16},{1... | collective-permute-start | bytes 786440 | tf_op jit(solution)/shard_map/ppermute | solution.py:38
  87.1 8.7 %collective-permute-start.8 = (bf16[8,128,128]{2,1,0:T(8,128)(2,1)S(1)}, bf16[8,128,128]{2,1,0:T(8,128)(2,1)}, u32[]{:S(2)}, u32[]{:S(2)}) collective-permute-start(bf16[8,128,128]{2,1,0:T(8,128)(2,1)S(1)} %slice.9), channel_id=1, source_target_pairs={{0,96},{16,112},{32,0},{48,16},{64,32},{80,48},{96,64},{112,80},{1... | collective-permute-start | bytes 786440 | tf_op jit(solution)/shard_map/ppermute | solution.py:38
  89.3 8.4 %collective-permute-start.14 = (bf16[16,128,128]{2,1,0:T(8,128)(2,1)S(1)}, bf16[16,128,128]{2,1,0:T(8,128)(2,1)}, u32[]{:S(2)}, u32[]{:S(2)}) collective-permute-start(bf16[16,128,128]{2,1,0:T(8,128)(2,1)S(1)} %collective-permute-done.5.refs_5_), channel_id=1, source_target_pairs={{0,16},{16,0},{32,48},{48,32},{64,80},{80,64},{96,112},{112,96},{1... | collective-permute-start | bytes 1572872 | tf_op jit(solution)/shard_map/ppermute | solution.py:30
  91.2 6.6 %collective-permute-start.12 = (bf16[16,128,128]{2,1,0:T(8,128)(2,1)}, bf16[16,128,128]{2,1,0:T(8,128)(2,1)}, u32[]{:S(2)}, u32[]{:S(2)}) collective-permute-start(bf16[16,128,128]{2,1,0:T(8,128)(2,1)} %collective-permute-done.3.refs_3_), channel_id=1, source_target_pairs={{0,16},{16,0},{32,48},{48,32},{64,80},{80,64},{96,112},{112,96},{1... | collective-permute-start | bytes 1572872 | tf_op jit(solution)/shard_map/ppermute | solution.py:30
  92.0 5.7 %collective-permute-start.15 = (bf16[16,128,128]{2,1,0:T(8,128)(2,1)S(1)}, bf16[16,128,128]{2,1,0:T(8,128)(2,1)}, u32[]{:S(2)}, u32[]{:S(2)}) collective-permute-start(bf16[16,128,128]{2,1,0:T(8,128)(2,1)S(1)} %collective-permute-done.6.refs_6_), channel_id=1, source_target_pairs={{0,16},{16,0},{32,48},{48,32},{64,80},{80,64},{96,112},{112,96},{1... | collective-permute-start | bytes 1572872 | tf_op jit(solution)/shard_map/ppermute | solution.py:30
  94.5 2.9 %collective-permute-start.16 = (bf16[8,128,128]{2,1,0:T(8,128)(2,1)}, bf16[8,128,128]{2,1,0:T(8,128)(2,1)}, u32[]{:S(2)}, u32[]{:S(2)}) collective-permute-start(bf16[8,128,128]{2,1,0:T(8,128)(2,1)} %collective-permute-done.7.refs_7_), channel_id=1, source_target_pairs={{0,16},{16,0},{32,48},{48,32},{64,80},{80,64},{96,112},{112,96},{1... | collective-permute-start | bytes 786440 | tf_op jit(solution)/shard_map/ppermute | solution.py:30
  95.8 1.9 %collective-permute-start.17 = (bf16[8,128,128]{2,1,0:T(8,128)(2,1)}, bf16[8,128,128]{2,1,0:T(8,128)(2,1)}, u32[]{:S(2)}, u32[]{:S(2)}) collective-permute-start(bf16[8,128,128]{2,1,0:T(8,128)(2,1)} %collective-permute-done.8.refs_8_), channel_id=1, source_target_pairs={{0,16},{16,0},{32,48},{48,32},{64,80},{80,64},{96,112},{112,96},{1... | collective-permute-start | bytes 786440 | tf_op jit(solution)/shard_map/ppermute | solution.py:30
  95.9 44.1 %copy-start.24 = (bf16[768]{0:T(1024)(128)(2,1)S(1)}, bf16[768]{0:T(1024)(128)(2,1)}, u32[]{:S(2)}) copy-start(bf16[768]{0:T(1024)(128)(2,1)} %param.27) | copy-start | bytes 4612
  124.9 30.1 %all-to-all-start.2 = ((bf16[16,48,256]{2,1,0:T(8,128)(2,1)}), bf16[16,48,256]{2,1,0:T(8,128)(2,1)S(1)}, u32[]{:S(2)}, u32[]{:S(2)}) async-start(bf16[16,48,256]{2,1,0:T(8,128)(2,1)} %shard_map.139), calls=%async_computation.2 | async-start | bytes 786432 | tf_op jit(solution)/shard_map/all_to_all | solution.py:386
  140.0 15.0 %copy-start.1 = (bf16[768,768]{1,0:T(8,128)(2,1)S(1)}, bf16[768,768]{1,0:T(8,128)(2,1)}, u32[]{:S(2)}) copy-start(bf16[768,768]{1,0:T(8,128)(2,1)} %weight_ref.3) | copy-start | bytes 3538948
  (14 other events, 13.8 us)

commit v4 on v3

--- a/solution.py
+++ b/solution.py
@@ -147,7 +147,7 @@
             out_ref[head, kind * size : (kind + 1) * size, :] = turned[head * size : (head + 1) * size]
 
 
-def attention_kernel(order_ref, kv_ref, *refs):
+def attention_kernel(sample_ref, kv_ref, *refs):
     count = len(refs) - 11
     pieces = refs[:count]
     out_ref, q_scr, k_scr, v_scr, b_scr, s_even, s_odd, m_even, m_odd, sems, kv_scr = refs[count:]
@@ -163,8 +163,8 @@
     def copies(step):
         found = []
         for place in range(blocks):
-            first, start = place + place // 8, step * per_step
-            if place % 8 == 7:
+            first, start = place + place // 4, step * per_step
+            if place % 4 == 3:
                 found.append((pieces[first + start * 2 // blocks], start % (blocks // 2)))
             else:
                 found.append((pieces[first], start))
@@ -183,11 +183,14 @@
         for copy in copies(step):
             copy.start()
     kv_copy.wait()
+    mine = sample_ref[0]
 
     for sample in range(2):
         lanes = slice(sample * tok, (sample + 1) * tok)
         for place in range(blocks):
-            block = order_ref[place]
+            shift = (0, 3, 1, 2)[place % 4]
+            block = (mine ^ (place // 4 % 2 * 8 + place // 8)) & 9
+            block = block + ((mine // 2 + shift) % 4) * 2
             span = slice(place * tok, (place + 1) * tok)
             query = kv_scr[place, :size, lanes].astype(F32) * scale
             high = query.astype(BF16)
@@ -273,7 +276,7 @@
     run(weigh(steps - 1, 1))
 
 
-def attention(order, kv, pieces):
+def attention(sample_place, kv, pieces):
     blocks, rows3, width = kv.shape
     size = rows3 // 3
     tok = width // 2
@@ -281,7 +284,7 @@
     any_place = pl.BlockSpec(memory_space=pl.ANY)
     return pl.pallas_call(
         attention_kernel,
-        in_specs=[pl.BlockSpec(memory_space=pltpu.SMEM), any_place] + [any_place] * len(pieces),
+        in_specs=[pl.BlockSpec(memory_space=pltpu.SMEM)] + [any_place] * (1 + len(pieces)),
         out_specs=pl.BlockSpec(memory_space=pltpu.VMEM),
         out_shape=jax.ShapeDtypeStruct((blocks, size, width), BF16),
         scratch_shapes=[
@@ -296,11 +299,11 @@
             pltpu.SemaphoreType.DMA((total // ROWS + 1, blocks)),
             pltpu.VMEM(kv.shape, BF16),
         ],
-        compiler_params=pltpu.CompilerParams(vmem_limit_bytes=36 * 1024 * 1024),
+        compiler_params=pltpu.CompilerParams(vmem_limit_bytes=62 * 1024 * 1024),
         cost_estimate=pl.CostEstimate(
             flops=8 * total * total * 64, bytes_accessed=12 * 1024 * 1024, transcendentals=2 * total * total
         ),
-    )(order, kv, *pieces)
+    )(sample_place, kv, *pieces)
 
 
 def finish_kernel(attended_ref, weight_ref, gate_ref, out_ref):
@@ -337,7 +340,6 @@
 
     bias_local = pair_bias_local(pair_rep, w_pair)
     bias_local, atom_feats = lax.optimization_barrier((bias_local, atom_feats))
-    mine = lax.all_to_all(bias_local, "seq", 0, 0, tiled=True)
 
     relative = (atom_token - seq_place * tok_local)[None, :]
     own, counts, sent = pl.pallas_call(
@@ -348,9 +350,12 @@
             jax.ShapeDtypeStruct((samp_local, tok_local, model_width + 128), BF16),
         ),
         compiler_params=pltpu.CompilerParams(vmem_limit_bytes=40 * 1024 * 1024),
-        cost_estimate=pl.CostEstimate(flops=4 * 10**9, bytes_accessed=3 * 1024 * 1024, transcendentals=0),
+        cost_estimate=pl.CostEstimate(flops=10**6, bytes_accessed=64 * 1024, transcendentals=0),
     )(atom_feats, relative, w_atom)
+    bias_local, sent = lax.optimization_barrier((bias_local, sent))
     came = from_behind(sent, "seq", 1)
+    mine = lax.all_to_all(bias_local, "seq", 0, 0, tiled=True)
+
     cond = layer_norm(single_cond.astype(F32)).astype(BF16)
     out_gate = jax.nn.sigmoid(
         jnp.einsum("std,de->ste", cond, w_outgate, preferred_element_type=F32)
@@ -362,27 +367,25 @@
         token_kernel,
         out_shape=jax.ShapeDtypeStruct((head_count, 3 * head_size, samp_local * tok_local), BF16),
         compiler_params=pltpu.CompilerParams(vmem_limit_bytes=40 * 1024 * 1024),
-        cost_estimate=pl.CostEstimate(flops=3 * 10**9, bytes_accessed=6 * 1024 * 1024, transcendentals=0),
+        cost_estimate=pl.CostEstimate(flops=10**6, bytes_accessed=64 * 1024, transcendentals=0),
     )(own, counts, came, gate_ada, shift_ada, w_query, w_key, w_value)
     kv = lax.all_to_all(heads_sent, "seq", 0, 0, tiled=True)
 
     half = mine.shape[0] // 2
-    across, up, down = swap_x(mine), shift_y(mine, 1), shift_y(mine, -1)
-    far, across_up, across_down = shift_y(up, 1), swap_x(up), shift_y(across, -1)
-    across_far = [shift_y(across_up[:half], 1), shift_y(across_down[half:], -1)]
-    pieces = [mine, up, down, far, across, across_up, across_down, *across_far]
-    pieces = pieces + [swap_core(piece) for piece in pieces]
-    x_lo, y, core = sample_place // 8, sample_place // 2 % 4, sample_place % 2
-    order = jnp.stack(
-        [
-            (x_lo ^ dx) * 8 + ((y + dy) % 4) * 2 + (core ^ dc)
-            for dc in (0, 1)
-            for dx in (0, 1)
-            for dy in (0, 3, 1, 2)
-        ]
-    ).astype(jnp.int32)
-
-    attended = attention(order, kv, pieces)
+    across, up, down = lax.optimization_barrier((swap_x(mine), shift_y(mine, 1), shift_y(mine, -1)))
+    far = (shift_y(up[:half], 1), shift_y(down[half:], -1))
+    across_up, across_down = shift_y(across, 1), shift_y(across, -1)
+    near = [mine, up, down, across]
+    far, other = lax.optimization_barrier((far, [swap_core(piece) for piece in near]))
+    across_far = [swap_x(part) for part in far]
+    late = [*far, across_up, across_down, *across_far]
+
+    def in_order(close, later):
+        return [*close[:3], *later[:2], close[3], *later[2:]]
+
+    pieces = in_order(near, late) + in_order(other, [swap_core(piece) for piece in late])
+
+    attended = attention(sample_place[None], kv, pieces)
     attended = lax.all_to_all(attended, "seq", 0, 0, tiled=True).reshape(model_width, -1)
     out = pl.pallas_call(
         finish_kernel,

time: 157 us -> 135 us (0.86)
  waiting for transfers between devices: 48.6 us -> 37 us
  local copies, waits for them, and re-layouts: 13 us -> 2.36 us
  Pallas kernels: 32 us -> 25.1 us
  starting transfers between devices: 59.5 us -> 66.1 us
    unnamed x50 -> x44, local copies, waits for them, and re-layouts: 12.9 us -> 2.32 us
    ppermute x6, waiting for transfers between devices: 10.6 us -> 1.82 us  [shift_y(): lax.ppermute(value, 'sample', [(i, i & 9 | ((i >> 1) + steps & 3) << 1) f...]
    pallas_call x1, Pallas kernels: 19.9 us -> 13.1 us  [attention(): pl.pallas_call(attention_kernel, in_specs=[pl.BlockSpec(memory_space=pltp...]
    ppermute x9 -> x10, starting transfers between devices: 13.5 us -> 19.7 us  [swap_core(): return lax.ppermute(value, 'sample', [(i, i ^ 1) for i in range(16)])]
    ppermute x2 -> x3, waiting for transfers between devices: 12.3 us -> 8.92 us  [swap_x(): return lax.ppermute(value, 'sample', [(i, i ^ 8) for i in range(16)])]
  transfers between devices with their start and end apart: 21 -> 23, of which waited for: 8 -> 8; matrix products, arithmetic and copies ran while one was open for 2% -> 2% of each run, Pallas kernels for 2% -> 2%
where the time goes in v4:
time: 135 us; the launch traced here: 134 us
  starting transfers between devices  66.1 us (49%)
  waiting for transfers between devices  37 us (27%)
  Pallas kernels  25.1 us (19%)
  matrix products  2.56 us (2%)
  local copies, waits for them, and re-layouts  2.36 us (2%)
    ppermute x10, starting transfers between devices, swap_core(): return lax.ppermute(value, 'sample', [(i, i ^ 1) for i in range(16)])  19.7 us
    all_to_all x1, starting transfers between devices, per_device(): lax.all_to_all(attended, 'seq', 0, 0, tiled=True).reshape(model_width, -1)  14.5 us
    all_to_all x1, waiting for transfers between devices, per_device(): lax.all_to_all(attended, 'seq', 0, 0, tiled=True).reshape(model_width, -1)  13.5 us
    pallas_call x1, Pallas kernels, attention(): pl.pallas_call(attention_kernel, in_specs=[pl.BlockSpec(memory_space=pltp...  13.1 us
    all_to_all x1, waiting for transfers between devices, per_device(): mine = lax.all_to_all(bias_local, 'seq', 0, 0, tiled=True)  10.8 us
    ppermute x3, waiting for transfers between devices, swap_x(): return lax.ppermute(value, 'sample', [(i, i ^ 8) for i in range(16)])  8.92 us
    all_to_all x1, starting transfers between devices, per_device(): mine = lax.all_to_all(bias_local, 'seq', 0, 0, tiled=True)  8.73 us
    ppermute x6, starting transfers between devices, shift_y(): lax.ppermute(value, 'sample', [(i, i & 9 | ((i >> 1) + steps & 3) << 1) f...  8.25 us
  transfers between devices with their start and end apart: 23, of which 8 were waited for; matrix products, arithmetic and copies ran while one was open for 2% of the time, Pallas kernels for 2%

profile of v4, /device:TPU:1, one launch (start us, length us, event | category | flops | bytes accessed | tf_op | source)
XLA Modules:
  0.0 133.8 jit_solution(10903288585044332663)
XLA Ops:
  0.0 6.3 %shard_map.136 = bf16[16,128,128]{2,1,0:T(8,128)(2,1)} custom-call(bf16[16,8,128,128]{3,2,1,0:T(8,128)(2,1)} %bitcast.19, bf16[16,128]{1,0:T(8,128)(2,1)} %bitcast.20), custom_call_target="tpu_custom_call" | custom-call | flops 1073741824 | bytes 5242880 | tf_op jit(solution)/shard_map/pallas_call | solution.py:87
  6.4 1.8 %shard_map.137 = (bf16[2,128,768]{2,1,0:T(8,128)(2,1)S(1)}, f32[128,128]{1,0:T(8,128)S(1)}, bf16[2,128,896]{2,1,0:T(8,128)(2,1)S(1)}) custom-call(bf16[2,1024,128]{2,1,0:T(8,128)(2,1)S(1)} %copy-done.5, s32[1,1024]{1,0:T(1,128)S(1)} %bitcast.18, bf16[128,768]{1,0:T(8,128)(2,1)S(1)} %copy-done.6), custom_call_target="tpu_custom_call" | custom-call | flops 1000000 | bytes 65536 | tf_op jit(solution)/shard_map/pallas_call | solution.py:345
  8.2 5.5 %collective-permute-start = (bf16[2,128,896]{2,1,0:T(8,128)(2,1)S(1)}, bf16[2,128,896]{2,1,0:T(8,128)(2,1)S(1)}, u32[]{:S(2)}, u32[]{:S(2)}) collective-permute-start(bf16[2,128,896]{2,1,0:T(8,128)(2,1)S(1)} %get-tuple-element.26), channel_id=1, source_target_pairs={{0,1},{1,2},{2,3},{3,4},{4,5},{5,6},{6,7},{7,8},{8,9},{9,10},{10,1... | collective-permute-start | bytes 1376264 | tf_op jit(solution)/shard_map/ppermute | solution.py:19
  13.7 8.7 %all-to-all-start.1 = ((bf16[16,128,128]{2,1,0:T(8,128)(2,1)}), bf16[16,128,128]{2,1,0:T(8,128)(2,1)}, u32[]{:S(2)}, u32[]{:S(2)}) async-start(bf16[16,128,128]{2,1,0:T(8,128)(2,1)} %shard_map.136), calls=%async_computation.1 | async-start | bytes 1048576 | tf_op jit(solution)/shard_map/all_to_all | solution.py:357
  24.6 0.7 copy-done.1
  25.3 2.6 %shard_map.138 = bf16[16,144,256]{2,1,0:T(8,128)(2,1)} custom-call(bf16[2,128,768]{2,1,0:T(8,128)(2,1)S(1)} %get-tuple-element.22.own_ref, f32[128,128]{1,0:T(8,128)S(1)} %get-tuple-element.23.count_ref, bf16[2,128,896]{2,1,0:T(8,128)(2,1)S(1)} %collective-permute-done.came_ref, f32[2,128,768]{2,1,0:T(8,128)S(1)} %fusion.4.gate_ref, ...), custom_call_target="tpu_custom_call" | custom-call | flops 1000000 | bytes 65536 | tf_op jit(solution)/shard_map/pallas_call | solution.py:366
  27.9 10.8 %all-to-all-done.1.refs_0_ = bf16[16,128,128]{2,1,0:T(8,128)(2,1)} async-done(((bf16[16,128,128]{2,1,0:T(8,128)(2,1)}), bf16[16,128,128]{2,1,0:T(8,128)(2,1)}, u32[]{:S(2)}, u32[]{:S(2)}) %all-to-all-start.1) | async-done | bytes 524320 | tf_op jit(solution)/shard_map/all_to_all | solution.py:357
  38.8 6.5 %all-to-all-start = ((bf16[16,144,256]{2,1,0:T(8,128)(2,1)}), bf16[16,144,256]{2,1,0:T(8,128)(2,1)}, u32[]{:S(2)}, u32[]{:S(2)}) async-start(bf16[16,144,256]{2,1,0:T(8,128)(2,1)} %shard_map.138), calls=%async_computation | async-start | bytes 2359296 | tf_op jit(solution)/shard_map/all_to_all | solution.py:372
  45.3 1.3 collective-permute-start.1
  46.6 1.3 collective-permute-start.2
  47.9 1.4 %collective-permute-start.3 = (bf16[16,128,128]{2,1,0:T(8,128)(2,1)}, bf16[16,128,128]{2,1,0:T(8,128)(2,1)S(1)}, u32[]{:S(2)}, u32[]{:S(2)}) collective-permute-start(bf16[16,128,128]{2,1,0:T(8,128)(2,1)} %all-to-all-done.1.refs_0_), channel_id=1, source_target_pairs={{0,96},{16,112},{32,0},{48,16},{64,32},{80,48},{96,64},{112,80},{1... | collective-permute-start | bytes 1572872 | tf_op jit(solution)/shard_map/ppermute | solution.py:38
  49.3 2.9 %collective-permute-start.6 = (bf16[16,128,128]{2,1,0:T(8,128)(2,1)}, bf16[16,128,128]{2,1,0:T(8,128)(2,1)S(1)}, u32[]{:S(2)}, u32[]{:S(2)}) collective-permute-start(bf16[16,128,128]{2,1,0:T(8,128)(2,1)} %all-to-all-done.1.refs_0_), channel_id=1, source_target_pairs={{0,16},{16,0},{32,48},{48,32},{64,80},{80,64},{96,112},{112,96},{1... | collective-permute-start | bytes 1572872 | tf_op jit(solution)/shard_map/ppermute | solution.py:30
  52.2 6.9 %collective-permute-done.1.refs_5_ = bf16[16,128,128]{2,1,0:T(8,128)(2,1)S(1)} collective-permute-done((bf16[16,128,128]{2,1,0:T(8,128)(2,1)}, bf16[16,128,128]{2,1,0:T(8,128)(2,1)S(1)}, u32[]{:S(2)}, u32[]{:S(2)}) %collective-permute-start.1) | collective-permute-done | bytes 524320 | tf_op jit(solution)/shard_map/ppermute | solution.py:34
  59.3 1.3 collective-permute-start.4
  60.6 1.5 %collective-permute-start.5 = (bf16[8,128,128]{2,1,0:T(8,128)(2,1)S(1)}, bf16[8,128,128]{2,1,0:T(8,128)(2,1)}, u32[]{:S(2)}, u32[]{:S(2)}) collective-permute-start(bf16[8,128,128]{2,1,0:T(8,128)(2,1)S(1)} %slice.7), channel_id=1, source_target_pairs={{0,96},{16,112},{32,0},{48,16},{64,32},{80,48},{96,64},{112,80},{1... | collective-permute-start | bytes 786440 | tf_op jit(solution)/shard_map/ppermute | solution.py:38
  62.2 3.7 %collective-permute-start.7 = (bf16[16,128,128]{2,1,0:T(8,128)(2,1)S(1)}, bf16[16,128,128]{2,1,0:T(8,128)(2,1)S(1)}, u32[]{:S(2)}, u32[]{:S(2)}) collective-permute-start(bf16[16,128,128]{2,1,0:T(8,128)(2,1)S(1)} %collective-permute-done.2.refs_1_), channel_id=1, source_target_pairs={{0,16},{16,0},{32,48},{48,32},{64,80},{80,64},{96,112},{112,96},{1... | collective-permute-start | bytes 1572872 | tf_op jit(solution)/shard_map/ppermute | solution.py:30
  66.5 2.6 %collective-permute-start.11 = (bf16[16,128,128]{2,1,0:T(8,128)(2,1)S(1)}, bf16[16,128,128]{2,1,0:T(8,128)(2,1)S(1)}, u32[]{:S(2)}, u32[]{:S(2)}) collective-permute-start(bf16[16,128,128]{2,1,0:T(8,128)(2,1)S(1)} %collective-permute-done.1.refs_5_), channel_id=1, source_target_pairs={{0,96},{16,112},{32,0},{48,16},{64,32},{80,48},{96,64},{112,80},{1... | collective-permute-start | bytes 1572872 | tf_op jit(solution)/shard_map/ppermute | solution.py:38
  69.1 1.6 %collective-permute-start.12 = (bf16[8,128,128]{2,1,0:T(8,128)(2,1)S(1)}, bf16[8,128,128]{2,1,0:T(8,128)(2,1)}, u32[]{:S(2)}, u32[]{:S(2)}) collective-permute-start(bf16[8,128,128]{2,1,0:T(8,128)(2,1)S(1)} %collective-permute-done.4.refs_3_), channel_id=1, source_target_pairs={{0,128},{16,144},{32,160},{48,176},{64,192},{80,208},{96,224},{112... | collective-permute-start | bytes 786440 | tf_op jit(solution)/shard_map/ppermute | solution.py:34
  70.8 4.9 %collective-permute-start.14 = (bf16[8,128,128]{2,1,0:T(8,128)(2,1)S(1)}, bf16[8,128,128]{2,1,0:T(8,128)(2,1)S(1)}, u32[]{:S(2)}, u32[]{:S(2)}) collective-permute-start(bf16[8,128,128]{2,1,0:T(8,128)(2,1)S(1)} %collective-permute-done.4.refs_3_), channel_id=1, source_target_pairs={{0,16},{16,0},{32,48},{48,32},{64,80},{80,64},{96,112},{112,96},{1... | collective-permute-start | bytes 786440 | tf_op jit(solution)/shard_map/ppermute | solution.py:30
  75.7 1.7 %collective-permute-done.10.refs_6_ = bf16[16,128,128]{2,1,0:T(8,128)(2,1)S(1)} collective-permute-done((bf16[16,128,128]{2,1,0:T(8,128)(2,1)S(1)}, bf16[16,128,128]{2,1,0:T(8,128)(2,1)S(1)}, u32[]{:S(2)}, u32[]{:S(2)}) %collective-permute-start.10) | collective-permute-done | bytes 524320 | tf_op jit(solution)/shard_map/ppermute | solution.py:38
  77.4 4.5 %collective-permute-start.16 = (bf16[16,128,128]{2,1,0:T(8,128)(2,1)S(1)}, bf16[16,128,128]{2,1,0:T(8,128)(2,1)}, u32[]{:S(2)}, u32[]{:S(2)}) collective-permute-start(bf16[16,128,128]{2,1,0:T(8,128)(2,1)S(1)} %collective-permute-done.10.refs_6_), channel_id=1, source_target_pairs={{0,16},{16,0},{32,48},{48,32},{64,80},{80,64},{96,112},{112,96},{1... | collective-permute-start | bytes 1572872 | tf_op jit(solution)/shard_map/ppermute | solution.py:30
  82.1 1.0 collective-permute-start.15
  83.1 2.0 %collective-permute-done.13.refs_9_ = bf16[8,128,128]{2,1,0:T(8,128)(2,1)} collective-permute-done((bf16[8,128,128]{2,1,0:T(8,128)(2,1)}, bf16[8,128,128]{2,1,0:T(8,128)(2,1)}, u32[]{:S(2)}, u32[]{:S(2)}) %collective-permute-start.13) | collective-permute-done | bytes 262176 | tf_op jit(solution)/shard_map/ppermute | solution.py:34
  85.0 2.0 %collective-permute-start.18 = (bf16[8,128,128]{2,1,0:T(8,128)(2,1)}, bf16[8,128,128]{2,1,0:T(8,128)(2,1)}, u32[]{:S(2)}, u32[]{:S(2)}) collective-permute-start(bf16[8,128,128]{2,1,0:T(8,128)(2,1)} %collective-permute-done.12.refs_8_), channel_id=1, source_target_pairs={{0,16},{16,0},{32,48},{48,32},{64,80},{80,64},{96,112},{112,96},{1... | collective-permute-start | bytes 786440 | tf_op jit(solution)/shard_map/ppermute | solution.py:30
  87.1 0.7 copy-done.21
  87.8 0.8 collective-permute-done.18.refs_18_
  88.6 1.1 collective-permute-done.19.refs_19_
  89.7 13.1 %shard_map.139 = bf16[16,48,256]{2,1,0:T(8,128)(2,1)} custom-call(s32[1]{0:T(128)} %bitcast.sample_ref, bf16[16,144,256]{2,1,0:T(8,128)(2,1)} %all-to-all-done.kv_ref, bf16[16,128,128]{2,1,0:T(8,128)(2,1)} %all-to-all-done.1.refs_0_, bf16[16,128,128]{2,1,0:T(8,128)(2,1)} %copy-done.9, bf16[16,128,128]{2,1,0:T(8,128)(2,1)} %copy-done.10, ...), custom_call_target="tpu_custom_call" | custom-call | flops 2147483648 | bytes 12582912 | tf_op jit(solution)/shard_map/pallas_call | solution.py:285
  102.8 14.5 %all-to-all-start.2 = ((bf16[16,48,256]{2,1,0:T(8,128)(2,1)}), bf16[16,48,256]{2,1,0:T(8,128)(2,1)S(1)}, u32[]{:S(2)}, u32[]{:S(2)}) async-start(bf16[16,48,256]{2,1,0:T(8,128)(2,1)} %shard_map.139), calls=%async_computation.2 | async-start | bytes 786432 | tf_op jit(solution)/shard_map/all_to_all | solution.py:389
  117.3 1.7 %fusion.6 = f32[2,128,768]{2,1,0:T(8,128)S(1)} fusion(bf16[384,768]{1,0:T(8,128)(2,1)} %param.26, f32[768]{0:T(1024)S(1)} %convert_element_type.11, bf16[2,128,384]{2,1,0:T(8,128)(2,1)S(1)} %copy-done.7, f32[2,128]{1,0:T(2,128)S(1)} %add_rsqrt_fusion, f32[2,128]{1,0:T(2,128)S(1)} %broadcast_multiply_fusion), kind=kOutput, calls=%fused_computation.8 | convolution fusion | flops 152174592 | bytes 1577984 | tf_op jit(solution)/shard_map/std,de->ste/dot_general | solution.py:361
  119.0 13.5 %all-to-all-done.2 = bf16[16,48,256]{2,1,0:T(8,128)(2,1)S(1)} async-done(((bf16[16,48,256]{2,1,0:T(8,128)(2,1)}), bf16[16,48,256]{2,1,0:T(8,128)(2,1)S(1)}, u32[]{:S(2)}, u32[]{:S(2)}) %all-to-all-start.2) | async-done | bytes 393248 | tf_op jit(solution)/shard_map/all_to_all | solution.py:389
  132.5 1.3 shard_map.140
  (74 shorter events, 3.2 us)
Async XLA Ops:
  0.0 22.8 %copy-start = (bf16[384,768]{1,0:T(8,128)(2,1)S(1)}, bf16[384,768]{1,0:T(8,128)(2,1)}, u32[]{:S(2)}) copy-start(bf16[384,768]{1,0:T(8,128)(2,1)} %param.19) | copy-start | bytes 1769476
  6.3 16.1 %copy-start.7 = (bf16[2,128,384]{2,1,0:T(8,128)(2,1)S(1)}, bf16[2,128,384]{2,1,0:T(8,128)(2,1)}, u32[]{:S(2)}) copy-start(bf16[2,128,384]{2,1,0:T(8,128)(2,1)} %param.16) | copy-start | bytes 589828
  8.2 16.1 %collective-permute-start = (bf16[2,128,896]{2,1,0:T(8,128)(2,1)S(1)}, bf16[2,128,896]{2,1,0:T(8,128)(2,1)S(1)}, u32[]{:S(2)}, u32[]{:S(2)}) collective-permute-start(bf16[2,128,896]{2,1,0:T(8,128)(2,1)S(1)} %get-tuple-element.26), channel_id=1, source_target_pairs={{0,1},{1,2},{2,3},{3,4},{4,5},{5,6},{6,7},{7,8},{8,9},{9,10},{10,1... | collective-permute-start | bytes 1376264 | tf_op jit(solution)/shard_map/ppermute | solution.py:19
  13.7 25.1 %all-to-all-start.1 = ((bf16[16,128,128]{2,1,0:T(8,128)(2,1)}), bf16[16,128,128]{2,1,0:T(8,128)(2,1)}, u32[]{:S(2)}, u32[]{:S(2)}) async-start(bf16[16,128,128]{2,1,0:T(8,128)(2,1)} %shard_map.136), calls=%async_computation.1 | async-start | bytes 1048576 | tf_op jit(solution)/shard_map/all_to_all | solution.py:357
  38.8 50.9 %all-to-all-start = ((bf16[16,144,256]{2,1,0:T(8,128)(2,1)}), bf16[16,144,256]{2,1,0:T(8,128)(2,1)}, u32[]{:S(2)}, u32[]{:S(2)}) async-start(bf16[16,144,256]{2,1,0:T(8,128)(2,1)} %shard_map.138), calls=%async_computation | async-start | bytes 2359296 | tf_op jit(solution)/shard_map/all_to_all | solution.py:372
  45.3 13.9 %collective-permute-start.1 = (bf16[16,128,128]{2,1,0:T(8,128)(2,1)}, bf16[16,128,128]{2,1,0:T(8,128)(2,1)S(1)}, u32[]{:S(2)}, u32[]{:S(2)}) collective-permute-start(bf16[16,128,128]{2,1,0:T(8,128)(2,1)} %all-to-all-done.1.refs_0_), channel_id=1, source_target_pairs={{0,128},{16,144},{32,160},{48,176},{64,192},{80,208},{96,224},{112... | collective-permute-start | bytes 1572872 | tf_op jit(solution)/shard_map/ppermute | solution.py:34
  46.6 12.7 %collective-permute-start.2 = (bf16[16,128,128]{2,1,0:T(8,128)(2,1)}, bf16[16,128,128]{2,1,0:T(8,128)(2,1)S(1)}, u32[]{:S(2)}, u32[]{:S(2)}) collective-permute-start(bf16[16,128,128]{2,1,0:T(8,128)(2,1)} %all-to-all-done.1.refs_0_), channel_id=1, source_target_pairs={{0,32},{16,48},{32,64},{48,80},{64,96},{80,112},{96,0},{112,16},{1... | collective-permute-start | bytes 1572872 | tf_op jit(solution)/shard_map/ppermute | solution.py:38
  47.9 11.4 %collective-permute-start.3 = (bf16[16,128,128]{2,1,0:T(8,128)(2,1)}, bf16[16,128,128]{2,1,0:T(8,128)(2,1)S(1)}, u32[]{:S(2)}, u32[]{:S(2)}) collective-permute-start(bf16[16,128,128]{2,1,0:T(8,128)(2,1)} %all-to-all-done.1.refs_0_), channel_id=1, source_target_pairs={{0,96},{16,112},{32,0},{48,16},{64,32},{80,48},{96,64},{112,80},{1... | collective-permute-start | bytes 1572872 | tf_op jit(solution)/shard_map/ppermute | solution.py:38
  49.3 16.6 %collective-permute-start.6 = (bf16[16,128,128]{2,1,0:T(8,128)(2,1)}, bf16[16,128,128]{2,1,0:T(8,128)(2,1)S(1)}, u32[]{:S(2)}, u32[]{:S(2)}) collective-permute-start(bf16[16,128,128]{2,1,0:T(8,128)(2,1)} %all-to-all-done.1.refs_0_), channel_id=1, source_target_pairs={{0,16},{16,0},{32,48},{48,32},{64,80},{80,64},{96,112},{112,96},{1... | collective-permute-start | bytes 1572872 | tf_op jit(solution)/shard_map/ppermute | solution.py:30
  59.3 30.4 %copy-start.9 = (bf16[16,128,128]{2,1,0:T(8,128)(2,1)}, bf16[16,128,128]{2,1,0:T(8,128)(2,1)S(1)}, u32[]{:S(2)}) copy-start(bf16[16,128,128]{2,1,0:T(8,128)(2,1)S(1)} %collective-permute-done.2.refs_1_) | copy-start | bytes 1572868
  59.3 30.4 %copy-start.10 = (bf16[16,128,128]{2,1,0:T(8,128)(2,1)}, bf16[16,128,128]{2,1,0:T(8,128)(2,1)S(1)}, u32[]{:S(2)}) copy-start(bf16[16,128,128]{2,1,0:T(8,128)(2,1)S(1)} %collective-permute-done.3.refs_2_) | copy-start | bytes 1572868
  59.3 7.1 %collective-permute-start.4 = (bf16[8,128,128]{2,1,0:T(8,128)(2,1)S(1)}, bf16[8,128,128]{2,1,0:T(8,128)(2,1)S(1)}, u32[]{:S(2)}, u32[]{:S(2)}) collective-permute-start(bf16[8,128,128]{2,1,0:T(8,128)(2,1)S(1)} %slice.6), channel_id=1, source_target_pairs={{0,32},{16,48},{32,64},{48,80},{64,96},{80,112},{96,0},{112,16},{1... | collective-permute-start | bytes 786440 | tf_op jit(solution)/shard_map/ppermute | solution.py:38
  60.6 5.8 %collective-permute-start.5 = (bf16[8,128,128]{2,1,0:T(8,128)(2,1)S(1)}, bf16[8,128,128]{2,1,0:T(8,128)(2,1)}, u32[]{:S(2)}, u32[]{:S(2)}) collective-permute-start(bf16[8,128,128]{2,1,0:T(8,128)(2,1)S(1)} %slice.7), channel_id=1, source_target_pairs={{0,96},{16,112},{32,0},{48,16},{64,32},{80,48},{96,64},{112,80},{1... | collective-permute-start | bytes 786440 | tf_op jit(solution)/shard_map/ppermute | solution.py:38
  62.2 6.9 %collective-permute-start.7 = (bf16[16,128,128]{2,1,0:T(8,128)(2,1)S(1)}, bf16[16,128,128]{2,1,0:T(8,128)(2,1)S(1)}, u32[]{:S(2)}, u32[]{:S(2)}) collective-permute-start(bf16[16,128,128]{2,1,0:T(8,128)(2,1)S(1)} %collective-permute-done.2.refs_1_), channel_id=1, source_target_pairs={{0,16},{16,0},{32,48},{48,32},{64,80},{80,64},{96,112},{112,96},{1... | collective-permute-start | bytes 1572872 | tf_op jit(solution)/shard_map/ppermute | solution.py:30
  65.9 3.2 %collective-permute-start.8 = (bf16[16,128,128]{2,1,0:T(8,128)(2,1)S(1)}, bf16[16,128,128]{2,1,0:T(8,128)(2,1)S(1)}, u32[]{:S(2)}, u32[]{:S(2)}) collective-permute-start(bf16[16,128,128]{2,1,0:T(8,128)(2,1)S(1)} %collective-permute-done.3.refs_2_), channel_id=1, source_target_pairs={{0,16},{16,0},{32,48},{48,32},{64,80},{80,64},{96,112},{112,96},{1... | collective-permute-start | bytes 1572872 | tf_op jit(solution)/shard_map/ppermute | solution.py:30
  65.9 16.1 %copy-start.14 = (bf16[16,128,128]{2,1,0:T(8,128)(2,1)}, bf16[16,128,128]{2,1,0:T(8,128)(2,1)S(1)}, u32[]{:S(2)}) copy-start(bf16[16,128,128]{2,1,0:T(8,128)(2,1)S(1)} %collective-permute-done.6.refs_10_) | copy-start | bytes 1572868
  65.9 3.2 %collective-permute-start.9 = (bf16[16,128,128]{2,1,0:T(8,128)(2,1)S(1)}, bf16[16,128,128]{2,1,0:T(8,128)(2,1)S(1)}, u32[]{:S(2)}, u32[]{:S(2)}) collective-permute-start(bf16[16,128,128]{2,1,0:T(8,128)(2,1)S(1)} %collective-permute-done.1.refs_5_), channel_id=1, source_target_pairs={{0,16},{16,0},{32,48},{48,32},{64,80},{80,64},{96,112},{112,96},{1... | collective-permute-start | bytes 1572872 | tf_op jit(solution)/shard_map/ppermute | solution.py:30
  66.4 23.3 %copy-start.20 = (bf16[8,128,128]{2,1,0:T(8,128)(2,1)}, bf16[8,128,128]{2,1,0:T(8,128)(2,1)S(1)}, u32[]{:S(2)}) copy-start(bf16[8,128,128]{2,1,0:T(8,128)(2,1)S(1)} %collective-permute-done.4.refs_3_) | copy-start | bytes 786436
  66.4 11.0 %collective-permute-start.10 = (bf16[16,128,128]{2,1,0:T(8,128)(2,1)S(1)}, bf16[16,128,128]{2,1,0:T(8,128)(2,1)S(1)}, u32[]{:S(2)}, u32[]{:S(2)}) collective-permute-start(bf16[16,128,128]{2,1,0:T(8,128)(2,1)S(1)} %collective-permute-done.1.refs_5_), channel_id=1, source_target_pairs={{0,32},{16,48},{32,64},{48,80},{64,96},{80,112},{96,0},{112,16},{1... | collective-permute-start | bytes 1572872 | tf_op jit(solution)/shard_map/ppermute | solution.py:38
  66.5 15.5 %collective-permute-start.11 = (bf16[16,128,128]{2,1,0:T(8,128)(2,1)S(1)}, bf16[16,128,128]{2,1,0:T(8,128)(2,1)S(1)}, u32[]{:S(2)}, u32[]{:S(2)}) collective-permute-start(bf16[16,128,128]{2,1,0:T(8,128)(2,1)S(1)} %collective-permute-done.1.refs_5_), channel_id=1, source_target_pairs={{0,96},{16,112},{32,0},{48,16},{64,32},{80,48},{96,64},{112,80},{1... | collective-permute-start | bytes 1572872 | tf_op jit(solution)/shard_map/ppermute | solution.py:38
  69.1 13.9 %copy-start.17 = (bf16[16,128,128]{2,1,0:T(8,128)(2,1)}, bf16[16,128,128]{2,1,0:T(8,128)(2,1)S(1)}, u32[]{:S(2)}) copy-start(bf16[16,128,128]{2,1,0:T(8,128)(2,1)S(1)} %collective-permute-done.9.refs_15_) | copy-start | bytes 1572868
  69.1 12.9 %collective-permute-start.12 = (bf16[8,128,128]{2,1,0:T(8,128)(2,1)S(1)}, bf16[8,128,128]{2,1,0:T(8,128)(2,1)}, u32[]{:S(2)}, u32[]{:S(2)}) collective-permute-start(bf16[8,128,128]{2,1,0:T(8,128)(2,1)S(1)} %collective-permute-done.4.refs_3_), channel_id=1, source_target_pairs={{0,128},{16,144},{32,160},{48,176},{64,192},{80,208},{96,224},{112... | collective-permute-start | bytes 786440 | tf_op jit(solution)/shard_map/ppermute | solution.py:34
  70.7 14.3 %collective-permute-start.13 = (bf16[8,128,128]{2,1,0:T(8,128)(2,1)}, bf16[8,128,128]{2,1,0:T(8,128)(2,1)}, u32[]{:S(2)}, u32[]{:S(2)}) collective-permute-start(bf16[8,128,128]{2,1,0:T(8,128)(2,1)} %collective-permute-done.5.refs_4_), channel_id=1, source_target_pairs={{0,128},{16,144},{32,160},{48,176},{64,192},{80,208},{96,224},{112... | collective-permute-start | bytes 786440 | tf_op jit(solution)/shard_map/ppermute | solution.py:34
  70.8 16.3 %collective-permute-start.14 = (bf16[8,128,128]{2,1,0:T(8,128)(2,1)S(1)}, bf16[8,128,128]{2,1,0:T(8,128)(2,1)S(1)}, u32[]{:S(2)}, u32[]{:S(2)}) collective-permute-start(bf16[8,128,128]{2,1,0:T(8,128)(2,1)S(1)} %collective-permute-done.4.refs_3_), channel_id=1, source_target_pairs={{0,16},{16,0},{32,48},{48,32},{64,80},{80,64},{96,112},{112,96},{1... | collective-permute-start | bytes 786440 | tf_op jit(solution)/shard_map/ppermute | solution.py:30
  77.4 12.2 %collective-permute-start.16 = (bf16[16,128,128]{2,1,0:T(8,128)(2,1)S(1)}, bf16[16,128,128]{2,1,0:T(8,128)(2,1)}, u32[]{:S(2)}, u32[]{:S(2)}) collective-permute-start(bf16[16,128,128]{2,1,0:T(8,128)(2,1)S(1)} %collective-permute-done.10.refs_6_), channel_id=1, source_target_pairs={{0,16},{16,0},{32,48},{48,32},{64,80},{80,64},{96,112},{112,96},{1... | collective-permute-start | bytes 1572872 | tf_op jit(solution)/shard_map/ppermute | solution.py:30
  82.0 7.7 %collective-permute-start.17 = (bf16[16,128,128]{2,1,0:T(8,128)(2,1)S(1)}, bf16[16,128,128]{2,1,0:T(8,128)(2,1)}, u32[]{:S(2)}, u32[]{:S(2)}) collective-permute-start(bf16[16,128,128]{2,1,0:T(8,128)(2,1)S(1)} %collective-permute-done.11.refs_7_), channel_id=1, source_target_pairs={{0,16},{16,0},{32,48},{48,32},{64,80},{80,64},{96,112},{112,96},{1... | collective-permute-start | bytes 1572872 | tf_op jit(solution)/shard_map/ppermute | solution.py:30
  82.1 5.7 %collective-permute-start.15 = (bf16[8,128,128]{2,1,0:T(8,128)(2,1)}, bf16[8,128,128]{2,1,0:T(8,128)(2,1)}, u32[]{:S(2)}, u32[]{:S(2)}) collective-permute-start(bf16[8,128,128]{2,1,0:T(8,128)(2,1)} %collective-permute-done.5.refs_4_), channel_id=1, source_target_pairs={{0,16},{16,0},{32,48},{48,32},{64,80},{80,64},{96,112},{112,96},{1... | collective-permute-start | bytes 786440 | tf_op jit(solution)/shard_map/ppermute | solution.py:30
  85.0 3.5 %collective-permute-start.18 = (bf16[8,128,128]{2,1,0:T(8,128)(2,1)}, bf16[8,128,128]{2,1,0:T(8,128)(2,1)}, u32[]{:S(2)}, u32[]{:S(2)}) collective-permute-start(bf16[8,128,128]{2,1,0:T(8,128)(2,1)} %collective-permute-done.12.refs_8_), channel_id=1, source_target_pairs={{0,16},{16,0},{32,48},{48,32},{64,80},{80,64},{96,112},{112,96},{1... | collective-permute-start | bytes 786440 | tf_op jit(solution)/shard_map/ppermute | solution.py:30
  87.8 1.9 %collective-permute-start.19 = (bf16[8,128,128]{2,1,0:T(8,128)(2,1)}, bf16[8,128,128]{2,1,0:T(8,128)(2,1)}, u32[]{:S(2)}, u32[]{:S(2)}) collective-permute-start(bf16[8,128,128]{2,1,0:T(8,128)(2,1)} %collective-permute-done.13.refs_9_), channel_id=1, source_target_pairs={{0,16},{16,0},{32,48},{48,32},{64,80},{80,64},{96,112},{112,96},{1... | collective-permute-start | bytes 786440 | tf_op jit(solution)/shard_map/ppermute | solution.py:30
  89.7 27.6 %copy-start.12 = (bf16[768]{0:T(1024)(128)(2,1)S(1)}, bf16[768]{0:T(1024)(128)(2,1)}, u32[]{:S(2)}) copy-start(bf16[768]{0:T(1024)(128)(2,1)} %param.27) | copy-start | bytes 4612
  102.8 29.7 %all-to-all-start.2 = ((bf16[16,48,256]{2,1,0:T(8,128)(2,1)}), bf16[16,48,256]{2,1,0:T(8,128)(2,1)S(1)}, u32[]{:S(2)}, u32[]{:S(2)}) async-start(bf16[16,48,256]{2,1,0:T(8,128)(2,1)} %shard_map.139), calls=%async_computation.2 | async-start | bytes 786432 | tf_op jit(solution)/shard_map/all_to_all | solution.py:389
  117.3 15.2 %copy-start.4 = (bf16[768,768]{1,0:T(8,128)(2,1)S(1)}, bf16[768,768]{1,0:T(8,128)(2,1)}, u32[]{:S(2)}) copy-start(bf16[768,768]{1,0:T(8,128)(2,1)} %weight_ref.3) | copy-start | bytes 3538948
  (13 other events, 81.4 us)

commit v5 on v4

--- a/solution.py
+++ b/solution.py
@@ -161,13 +161,7 @@
     scale = LOG2E / math.sqrt(size)
 
     def copies(step):
-        found = []
-        for place in range(blocks):
-            first, start = place + place // 4, step * per_step
-            if place % 4 == 3:
-                found.append((pieces[first + start * 2 // blocks], start % (blocks // 2)))
-            else:
-                found.append((pieces[first], start))
+        found = [(piece, step * per_step) for piece in pieces]
         return [
             pltpu.make_async_copy(
                 piece.at[pl.ds(start, per_step)],
@@ -377,11 +371,11 @@
     across_up, across_down = shift_y(across, 1), shift_y(across, -1)
     near = [mine, up, down, across]
     far, other = lax.optimization_barrier((far, [swap_core(piece) for piece in near]))
-    across_far = [swap_x(part) for part in far]
-    late = [*far, across_up, across_down, *across_far]
+    far = jnp.concatenate(far, axis=0)
+    late = [far, across_up, across_down, swap_x(far)]
 
     def in_order(close, later):
-        return [*close[:3], *later[:2], close[3], *later[2:]]
+        return [*close[:3], later[0], close[3], *later[1:]]
 
     pieces = in_order(near, late) + in_order(other, [swap_core(piece) for piece in late])
 

time: 135 us -> 138 us (1.022)
  starting transfers between devices: 66.1 us -> 52.1 us
  waiting for transfers between devices: 37 us -> 48.2 us
  local copies, waits for them, and re-layouts: 2.36 us -> 5.21 us
  matrix products: 2.56 us -> 4.51 us
  Pallas kernels: 25.1 us -> 26.9 us
    ppermute x6, waiting for transfers between devices: 1.82 us -> 14.6 us  [shift_y(): lax.ppermute(value, 'sample', [(i, i & 9 | ((i >> 1) + steps & 3) << 1) f...]
    ppermute x10 -> x8, starting transfers between devices: 19.7 us -> 6.95 us  [swap_core(): return lax.ppermute(value, 'sample', [(i, i ^ 1) for i in range(16)])]
    all_to_all x1, starting transfers between devices: 14.5 us -> 8.83 us  [per_device(): lax.all_to_all(attended, 'seq', 0, 0, tiled=True).reshape(model_width, -1)]
    all_to_all x1, starting transfers between devices: 6.53 us -> 9.74 us  [per_device(): kv = lax.all_to_all(heads_sent, 'seq', 0, 0, tiled=True)]
    all_to_all x1, starting transfers between devices: 8.73 us -> 11.6 us  [per_device(): mine = lax.all_to_all(bias_local, 'seq', 0, 0, tiled=True)]
    ppermute x3 -> x2, starting transfers between devices: 2.95 us -> 0.71 us  [swap_x(): return lax.ppermute(value, 'sample', [(i, i ^ 8) for i in range(16)])]
    slice x2, local copies, waits for them, and re-layouts: 0.04 us -> 1.94 us  [per_device(): far = (shift_y(up[:half], 1), shift_y(down[half:], -1))]
    unnamed x44 -> x41, local copies, waits for them, and re-layouts: 2.32 us -> 3.24 us
  transfers between devices with their start and end apart: 23 -> 20, of which waited for: 8 -> 6; matrix products, arithmetic and copies ran while one was open for 2% -> 5% of each run, Pallas kernels for 2% -> 3%
where the time goes in v5:
time: 138 us
  starting transfers between devices  52.1 us (38%)
  waiting for transfers between devices  48.2 us (35%)
  Pallas kernels  26.9 us (19%)
  local copies, waits for them, and re-layouts  5.21 us (4%)
  matrix products  4.51 us (3%)
    ppermute x6, waiting for transfers between devices, shift_y(): lax.ppermute(value, 'sample', [(i, i & 9 | ((i >> 1) + steps & 3) << 1) f...  14.6 us
    all_to_all x1, waiting for transfers between devices, per_device(): lax.all_to_all(attended, 'seq', 0, 0, tiled=True).reshape(model_width, -1)  13.3 us
    pallas_call x1, Pallas kernels, attention(): pl.pallas_call(attention_kernel, in_specs=[pl.BlockSpec(memory_space=pltp...  13.1 us
    all_to_all x1, starting transfers between devices, per_device(): mine = lax.all_to_all(bias_local, 'seq', 0, 0, tiled=True)  11.6 us
    all_to_all x1, waiting for transfers between devices, per_device(): mine = lax.all_to_all(bias_local, 'seq', 0, 0, tiled=True)  9.77 us
    all_to_all x1, starting transfers between devices, per_device(): kv = lax.all_to_all(heads_sent, 'seq', 0, 0, tiled=True)  9.74 us
    all_to_all x1, starting transfers between devices, per_device(): lax.all_to_all(attended, 'seq', 0, 0, tiled=True).reshape(model_width, -1)  8.83 us
    ppermute x6, starting transfers between devices, shift_y(): lax.ppermute(value, 'sample', [(i, i & 9 | ((i >> 1) + steps & 3) << 1) f...  8.73 us
  transfers between devices with their start and end apart: 20, of which 6 were waited for; matrix products, arithmetic and copies ran while one was open for 5% of the time, Pallas kernels for 3%

profile of v5, /device:TPU:1, one launch (start us, length us, event | category | flops | bytes accessed | tf_op | source)
XLA Modules:
  0.0 137.6 jit_solution(8504010803705512079)
XLA Ops:
  0.0 6.3 %shard_map.136 = bf16[16,128,128]{2,1,0:T(8,128)(2,1)} custom-call(bf16[16,8,128,128]{3,2,1,0:T(8,128)(2,1)} %bitcast.19, bf16[16,128]{1,0:T(8,128)(2,1)} %bitcast.20), custom_call_target="tpu_custom_call" | custom-call | flops 1073741824 | bytes 5242880 | tf_op jit(solution)/shard_map/pallas_call | solution.py:87
  6.4 2.6 %shard_map.137 = (bf16[2,128,768]{2,1,0:T(8,128)(2,1)S(1)}, f32[128,128]{1,0:T(8,128)S(1)}, bf16[2,128,896]{2,1,0:T(8,128)(2,1)}) custom-call(bf16[2,1024,128]{2,1,0:T(8,128)(2,1)S(1)} %copy-done.6, s32[1,1024]{1,0:T(1,128)S(1)} %bitcast.18, bf16[128,768]{1,0:T(8,128)(2,1)S(1)} %copy-done.9), custom_call_target="tpu_custom_call" | custom-call | flops 1000000 | bytes 65536 | tf_op jit(solution)/shard_map/pallas_call | solution.py:339
  9.0 0.7 copy-done.7
  9.7 11.6 %all-to-all-start.1 = ((bf16[16,128,128]{2,1,0:T(8,128)(2,1)}), bf16[16,128,128]{2,1,0:T(8,128)(2,1)}, u32[]{:S(2)}, u32[]{:S(2)}) async-start(bf16[16,128,128]{2,1,0:T(8,128)(2,1)} %shard_map.136), calls=%async_computation.1 | async-start | bytes 1048576 | tf_op jit(solution)/shard_map/all_to_all | solution.py:351
  21.4 5.5 %collective-permute-start = (bf16[2,128,896]{2,1,0:T(8,128)(2,1)}, bf16[2,128,896]{2,1,0:T(8,128)(2,1)}, u32[]{:S(2)}, u32[]{:S(2)}) collective-permute-start(bf16[2,128,896]{2,1,0:T(8,128)(2,1)} %get-tuple-element.26), channel_id=1, source_target_pairs={{0,1},{1,2},{2,3},{3,4},{4,5},{5,6},{6,7},{7,8},{8,9},{9,10},{10,1... | collective-permute-start | bytes 1376264 | tf_op jit(solution)/shard_map/ppermute | solution.py:19
  27.2 1.4 %fusion.4.gate_ref = f32[2,128,768]{2,1,0:T(8,128)} fusion(bf16[384,768]{1,0:T(8,128)(2,1)S(1)} %copy-done, bf16[2,128,384]{2,1,0:T(8,128)(2,1)S(1)} %copy-done.10, f32[2,128]{1,0:T(2,128)S(1)} %add_rsqrt_fusion, f32[2,128]{1,0:T(2,128)S(1)} %broadcast_multiply_fusion), kind=kOutput, calls=%fused_computation.6 | convolution fusion | flops 151977984 | bytes 1574912 | tf_op jit(solution)/shard_map/stc,cd->std/dot_general | solution.py:358
  28.6 9.8 %all-to-all-done.1.refs_0_ = bf16[16,128,128]{2,1,0:T(8,128)(2,1)} async-done(((bf16[16,128,128]{2,1,0:T(8,128)(2,1)}), bf16[16,128,128]{2,1,0:T(8,128)(2,1)}, u32[]{:S(2)}, u32[]{:S(2)}) %all-to-all-start.1) | async-done | bytes 524320 | tf_op jit(solution)/shard_map/all_to_all | solution.py:351
  38.7 1.3 collective-permute-start.2
  40.0 1.4 %collective-permute-start.3 = (bf16[16,128,128]{2,1,0:T(8,128)(2,1)}, bf16[16,128,128]{2,1,0:T(8,128)(2,1)}, u32[]{:S(2)}, u32[]{:S(2)}) collective-permute-start(bf16[16,128,128]{2,1,0:T(8,128)(2,1)} %all-to-all-done.1.refs_0_), channel_id=1, source_target_pairs={{0,96},{16,112},{32,0},{48,16},{64,32},{80,48},{96,64},{112,80},{1... | collective-permute-start | bytes 1572872 | tf_op jit(solution)/shard_map/ppermute | solution.py:38
  41.5 1.5 %fusion.8.shift_ref = f32[2,128,768]{2,1,0:T(8,128)S(1)} fusion(bf16[384,768]{1,0:T(8,128)(2,1)} %param.20, bf16[2,128,384]{2,1,0:T(8,128)(2,1)S(1)} %copy-done.10, f32[2,128]{1,0:T(2,128)S(1)} %add_rsqrt_fusion, f32[2,128]{1,0:T(2,128)S(1)} %broadcast_multiply_fusion), kind=kOutput, calls=%fused_computation.10 | convolution fusion | flops 151388160 | bytes 1574912 | tf_op jit(solution)/shard_map/stc,cd->std/dot_general | solution.py:359
  43.0 1.3 copy-done.3
  44.3 1.1 copy-done.5
  45.4 3.6 %shard_map.138 = bf16[16,144,256]{2,1,0:T(8,128)(2,1)} custom-call(bf16[2,128,768]{2,1,0:T(8,128)(2,1)S(1)} %copy-done.8, f32[128,128]{1,0:T(8,128)S(1)} %get-tuple-element.23.count_ref, bf16[2,128,896]{2,1,0:T(8,128)(2,1)} %collective-permute-done.came_ref, f32[2,128,768]{2,1,0:T(8,128)S(1)} %copy-done.5, f32[2,128,768]{2,1,0:T(8,128)S(1)} %fusion.8.shift_ref, ...), custom_call_target="tpu_custom_call" | custom-call | flops 1000000 | bytes 65536 | tf_op jit(solution)/shard_map/pallas_call | solution.py:360
  49.0 9.7 %all-to-all-start = ((bf16[16,144,256]{2,1,0:T(8,128)(2,1)}), bf16[16,144,256]{2,1,0:T(8,128)(2,1)}, u32[]{:S(2)}, u32[]{:S(2)}) async-start(bf16[16,144,256]{2,1,0:T(8,128)(2,1)} %shard_map.138), calls=%async_computation | async-start | bytes 2359296 | tf_op jit(solution)/shard_map/all_to_all | solution.py:366
  58.8 1.5 %collective-permute-start.6 = (bf16[16,128,128]{2,1,0:T(8,128)(2,1)}, bf16[16,128,128]{2,1,0:T(8,128)(2,1)S(1)}, u32[]{:S(2)}, u32[]{:S(2)}) collective-permute-start(bf16[16,128,128]{2,1,0:T(8,128)(2,1)} %all-to-all-done.1.refs_0_), channel_id=1, source_target_pairs={{0,16},{16,0},{32,48},{48,32},{64,80},{80,64},{96,112},{112,96},{1... | collective-permute-start | bytes 1572872 | tf_op jit(solution)/shard_map/ppermute | solution.py:30
  61.0 1.0 slice.6
  61.9 1.0 slice.7
  62.9 1.4 collective-permute-start.4
  64.3 1.7 %collective-permute-start.5 = (bf16[8,128,128]{2,1,0:T(8,128)(2,1)S(1)}, bf16[8,128,128]{2,1,0:T(8,128)(2,1)S(1)}, u32[]{:S(2)}, u32[]{:S(2)}) collective-permute-start(bf16[8,128,128]{2,1,0:T(8,128)(2,1)S(1)} %slice.7), channel_id=1, source_target_pairs={{0,96},{16,112},{32,0},{48,16},{64,32},{80,48},{96,64},{112,80},{1... | collective-permute-start | bytes 786440 | tf_op jit(solution)/shard_map/ppermute | solution.py:38
  66.0 5.9 %collective-permute-done.4 = bf16[8,128,128]{2,1,0:T(8,128)(2,1)S(1)} collective-permute-done((bf16[8,128,128]{2,1,0:T(8,128)(2,1)S(1)}, bf16[8,128,128]{2,1,0:T(8,128)(2,1)S(1)}, u32[]{:S(2)}, u32[]{:S(2)}) %collective-permute-start.4) | collective-permute-done | bytes 262176 | tf_op jit(solution)/shard_map/ppermute | solution.py:38
  71.9 2.9 %collective-permute-start.11 = (bf16[16,128,128]{2,1,0:T(8,128)(2,1)}, bf16[16,128,128]{2,1,0:T(8,128)(2,1)S(1)}, u32[]{:S(2)}, u32[]{:S(2)}) collective-permute-start(bf16[16,128,128]{2,1,0:T(8,128)(2,1)} %collective-permute-done.1.refs_4_), channel_id=1, source_target_pairs={{0,96},{16,112},{32,0},{48,16},{64,32},{80,48},{96,64},{112,80},{1... | collective-permute-start | bytes 1572872 | tf_op jit(solution)/shard_map/ppermute | solution.py:38
  75.3 1.7 %collective-permute-start.13 = (bf16[16,128,128]{2,1,0:T(8,128)(2,1)S(1)}, bf16[16,128,128]{2,1,0:T(8,128)(2,1)}, u32[]{:S(2)}, u32[]{:S(2)}) collective-permute-start(bf16[16,128,128]{2,1,0:T(8,128)(2,1)S(1)} %constant_dynamic-update-slice_fusion.refs_3_), channel_id=1, source_target_pairs={{0,16},{16,0},{32,48},{48,32},{64,80},{80,64},{96,112},{112,96},{1... | collective-permute-start | bytes 1572872 | tf_op jit(solution)/shard_map/ppermute | solution.py:30
  77.0 8.7 %collective-permute-done.10.refs_5_ = bf16[16,128,128]{2,1,0:T(8,128)(2,1)S(1)} collective-permute-done((bf16[16,128,128]{2,1,0:T(8,128)(2,1)}, bf16[16,128,128]{2,1,0:T(8,128)(2,1)S(1)}, u32[]{:S(2)}, u32[]{:S(2)}) %collective-permute-start.10) | collective-permute-done | bytes 524320 | tf_op jit(solution)/shard_map/ppermute | solution.py:38
  85.8 1.9 %collective-permute-start.14 = (bf16[16,128,128]{2,1,0:T(8,128)(2,1)S(1)}, bf16[16,128,128]{2,1,0:T(8,128)(2,1)}, u32[]{:S(2)}, u32[]{:S(2)}) collective-permute-start(bf16[16,128,128]{2,1,0:T(8,128)(2,1)S(1)} %collective-permute-done.10.refs_5_), channel_id=1, source_target_pairs={{0,16},{16,0},{32,48},{48,32},{64,80},{80,64},{96,112},{112,96},{1... | collective-permute-start | bytes 1572872 | tf_op jit(solution)/shard_map/ppermute | solution.py:30
  87.8 8.6 %collective-permute-done.12.refs_7_ = bf16[16,128,128]{2,1,0:T(8,128)(2,1)} collective-permute-done((bf16[16,128,128]{2,1,0:T(8,128)(2,1)S(1)}, bf16[16,128,128]{2,1,0:T(8,128)(2,1)}, u32[]{:S(2)}, u32[]{:S(2)}) %collective-permute-start.12) | collective-permute-done | bytes 524320 | tf_op jit(solution)/shard_map/ppermute | solution.py:34
  96.4 1.1 collective-permute-start.16
  97.5 1.9 %collective-permute-done.16.refs_15_ = bf16[16,128,128]{2,1,0:T(8,128)(2,1)} collective-permute-done((bf16[16,128,128]{2,1,0:T(8,128)(2,1)}, bf16[16,128,128]{2,1,0:T(8,128)(2,1)}, u32[]{:S(2)}, u32[]{:S(2)}) %collective-permute-start.16) | collective-permute-done | bytes 524320 | tf_op jit(solution)/shard_map/ppermute | solution.py:30
  99.4 13.1 %shard_map.139 = bf16[16,48,256]{2,1,0:T(8,128)(2,1)} custom-call(s32[1]{0:T(128)} %bitcast.sample_ref, bf16[16,144,256]{2,1,0:T(8,128)(2,1)} %all-to-all-done.kv_ref, bf16[16,128,128]{2,1,0:T(8,128)(2,1)} %all-to-all-done.1.refs_0_, bf16[16,128,128]{2,1,0:T(8,128)(2,1)} %collective-permute-done.2.refs_1_, ...), custom_call_target="tpu_custom_call" | custom-call | flops 2147483648 | bytes 12582912 | tf_op jit(solution)/shard_map/pallas_call | solution.py:279
  112.5 8.8 %all-to-all-start.2 = ((bf16[16,48,256]{2,1,0:T(8,128)(2,1)}), bf16[16,48,256]{2,1,0:T(8,128)(2,1)S(1)}, u32[]{:S(2)}, u32[]{:S(2)}) async-start(bf16[16,48,256]{2,1,0:T(8,128)(2,1)} %shard_map.139), calls=%async_computation.2 | async-start | bytes 786432 | tf_op jit(solution)/shard_map/all_to_all | solution.py:383
  121.4 1.7 %fusion.6 = f32[2,128,768]{2,1,0:T(8,128)S(1)} fusion(bf16[384,768]{1,0:T(8,128)(2,1)} %param.26, f32[768]{0:T(1024)S(1)} %convert_element_type.11, bf16[2,128,384]{2,1,0:T(8,128)(2,1)S(1)} %copy-done.10, f32[2,128]{1,0:T(2,128)S(1)} %add_rsqrt_fusion, f32[2,128]{1,0:T(2,128)S(1)} %broadcast_multiply_fusion), kind=kOutput, calls=%fused_computation.8 | convolution fusion | flops 152174592 | bytes 1577984 | tf_op jit(solution)/shard_map/std,de->ste/dot_general | solution.py:355
  123.0 13.3 %all-to-all-done.2 = bf16[16,48,256]{2,1,0:T(8,128)(2,1)S(1)} async-done(((bf16[16,48,256]{2,1,0:T(8,128)(2,1)}), bf16[16,48,256]{2,1,0:T(8,128)(2,1)S(1)}, u32[]{:S(2)}, u32[]{:S(2)}) %all-to-all-start.2) | async-done | bytes 393248 | tf_op jit(solution)/shard_map/all_to_all | solution.py:383
  136.3 1.3 shard_map.140
  (66 shorter events, 2.0 us)
Async XLA Ops:
  0.0 27.2 %copy-start = (bf16[384,768]{1,0:T(8,128)(2,1)S(1)}, bf16[384,768]{1,0:T(8,128)(2,1)}, u32[]{:S(2)}) copy-start(bf16[384,768]{1,0:T(8,128)(2,1)} %param.19) | copy-start | bytes 1769476
  6.4 20.5 %copy-start.10 = (bf16[2,128,384]{2,1,0:T(8,128)(2,1)S(1)}, bf16[2,128,384]{2,1,0:T(8,128)(2,1)}, u32[]{:S(2)}) copy-start(bf16[2,128,384]{2,1,0:T(8,128)(2,1)} %param.16) | copy-start | bytes 589828
  9.7 28.7 %all-to-all-start.1 = ((bf16[16,128,128]{2,1,0:T(8,128)(2,1)}), bf16[16,128,128]{2,1,0:T(8,128)(2,1)}, u32[]{:S(2)}, u32[]{:S(2)}) async-start(bf16[16,128,128]{2,1,0:T(8,128)(2,1)} %shard_map.136), calls=%async_computation.1 | async-start | bytes 1048576 | tf_op jit(solution)/shard_map/all_to_all | solution.py:351
  21.4 21.6 %collective-permute-start = (bf16[2,128,896]{2,1,0:T(8,128)(2,1)}, bf16[2,128,896]{2,1,0:T(8,128)(2,1)}, u32[]{:S(2)}, u32[]{:S(2)}) collective-permute-start(bf16[2,128,896]{2,1,0:T(8,128)(2,1)} %get-tuple-element.26), channel_id=1, source_target_pairs={{0,1},{1,2},{2,3},{3,4},{4,5},{5,6},{6,7},{7,8},{8,9},{9,10},{10,1... | collective-permute-start | bytes 1376264 | tf_op jit(solution)/shard_map/ppermute | solution.py:19
  27.2 15.7 %copy-start.2 = (bf16[768,768]{1,0:T(8,128)(2,1)S(1)}, bf16[768,768]{1,0:T(8,128)(2,1)}, u32[]{:S(2)}) copy-start(bf16[768,768]{1,0:T(8,128)(2,1)} %wk_ref.1) | copy-start | bytes 3538948
  28.6 14.3 %copy-start.1 = (bf16[768,768]{1,0:T(8,128)(2,1)S(1)}, bf16[768,768]{1,0:T(8,128)(2,1)}, u32[]{:S(2)}) copy-start(bf16[768,768]{1,0:T(8,128)(2,1)} %wq_ref.1) | copy-start | bytes 3538948
  38.4 21.9 %collective-permute-start.1 = (bf16[16,128,128]{2,1,0:T(8,128)(2,1)}, bf16[16,128,128]{2,1,0:T(8,128)(2,1)}, u32[]{:S(2)}, u32[]{:S(2)}) collective-permute-start(bf16[16,128,128]{2,1,0:T(8,128)(2,1)} %all-to-all-done.1.refs_0_), channel_id=1, source_target_pairs={{0,128},{16,144},{32,160},{48,176},{64,192},{80,208},{96,224},{112... | collective-permute-start | bytes 1572872 | tf_op jit(solution)/shard_map/ppermute | solution.py:34
  38.7 21.6 %collective-permute-start.2 = (bf16[16,128,128]{2,1,0:T(8,128)(2,1)}, bf16[16,128,128]{2,1,0:T(8,128)(2,1)}, u32[]{:S(2)}, u32[]{:S(2)}) collective-permute-start(bf16[16,128,128]{2,1,0:T(8,128)(2,1)} %all-to-all-done.1.refs_0_), channel_id=1, source_target_pairs={{0,32},{16,48},{32,64},{48,80},{64,96},{80,112},{96,0},{112,16},{1... | collective-permute-start | bytes 1572872 | tf_op jit(solution)/shard_map/ppermute | solution.py:38
  40.0 20.3 %collective-permute-start.3 = (bf16[16,128,128]{2,1,0:T(8,128)(2,1)}, bf16[16,128,128]{2,1,0:T(8,128)(2,1)}, u32[]{:S(2)}, u32[]{:S(2)}) collective-permute-start(bf16[16,128,128]{2,1,0:T(8,128)(2,1)} %all-to-all-done.1.refs_0_), channel_id=1, source_target_pairs={{0,96},{16,112},{32,0},{48,16},{64,32},{80,48},{96,64},{112,80},{1... | collective-permute-start | bytes 1572872 | tf_op jit(solution)/shard_map/ppermute | solution.py:38
  49.0 48.5 %all-to-all-start = ((bf16[16,144,256]{2,1,0:T(8,128)(2,1)}), bf16[16,144,256]{2,1,0:T(8,128)(2,1)}, u32[]{:S(2)}, u32[]{:S(2)}) async-start(bf16[16,144,256]{2,1,0:T(8,128)(2,1)} %shard_map.138), calls=%async_computation | async-start | bytes 2359296 | tf_op jit(solution)/shard_map/all_to_all | solution.py:366
  58.8 5.5 %collective-permute-start.6 = (bf16[16,128,128]{2,1,0:T(8,128)(2,1)}, bf16[16,128,128]{2,1,0:T(8,128)(2,1)S(1)}, u32[]{:S(2)}, u32[]{:S(2)}) collective-permute-start(bf16[16,128,128]{2,1,0:T(8,128)(2,1)} %all-to-all-done.1.refs_0_), channel_id=1, source_target_pairs={{0,16},{16,0},{32,48},{48,32},{64,80},{80,64},{96,112},{112,96},{1... | collective-permute-start | bytes 1572872 | tf_op jit(solution)/shard_map/ppermute | solution.py:30
  60.3 14.5 %collective-permute-start.7 = (bf16[16,128,128]{2,1,0:T(8,128)(2,1)}, bf16[16,128,128]{2,1,0:T(8,128)(2,1)S(1)}, u32[]{:S(2)}, u32[]{:S(2)}) collective-permute-start(bf16[16,128,128]{2,1,0:T(8,128)(2,1)} %collective-permute-done.2.refs_1_), channel_id=1, source_target_pairs={{0,16},{16,0},{32,48},{48,32},{64,80},{80,64},{96,112},{112,96},{1... | collective-permute-start | bytes 1572872 | tf_op jit(solution)/shard_map/ppermute | solution.py:30
  60.4 14.4 %collective-permute-start.8 = (bf16[16,128,128]{2,1,0:T(8,128)(2,1)}, bf16[16,128,128]{2,1,0:T(8,128)(2,1)S(1)}, u32[]{:S(2)}, u32[]{:S(2)}) collective-permute-start(bf16[16,128,128]{2,1,0:T(8,128)(2,1)} %collective-permute-done.3.refs_2_), channel_id=1, source_target_pairs={{0,16},{16,0},{32,48},{48,32},{64,80},{80,64},{96,112},{112,96},{1... | collective-permute-start | bytes 1572872 | tf_op jit(solution)/shard_map/ppermute | solution.py:30
  60.9 14.0 %collective-permute-start.9 = (bf16[16,128,128]{2,1,0:T(8,128)(2,1)}, bf16[16,128,128]{2,1,0:T(8,128)(2,1)S(1)}, u32[]{:S(2)}, u32[]{:S(2)}) collective-permute-start(bf16[16,128,128]{2,1,0:T(8,128)(2,1)} %collective-permute-done.1.refs_4_), channel_id=1, source_target_pairs={{0,16},{16,0},{32,48},{48,32},{64,80},{80,64},{96,112},{112,96},{1... | collective-permute-start | bytes 1572872 | tf_op jit(solution)/shard_map/ppermute | solution.py:30
  62.9 9.0 %collective-permute-start.4 = (bf16[8,128,128]{2,1,0:T(8,128)(2,1)S(1)}, bf16[8,128,128]{2,1,0:T(8,128)(2,1)S(1)}, u32[]{:S(2)}, u32[]{:S(2)}) collective-permute-start(bf16[8,128,128]{2,1,0:T(8,128)(2,1)S(1)} %slice.6), channel_id=1, source_target_pairs={{0,32},{16,48},{32,64},{48,80},{64,96},{80,112},{96,0},{112,16},{1... | collective-permute-start | bytes 786440 | tf_op jit(solution)/shard_map/ppermute | solution.py:38
  64.3 35.1 %copy-start.14 = (bf16[16,128,128]{2,1,0:T(8,128)(2,1)}, bf16[16,128,128]{2,1,0:T(8,128)(2,1)S(1)}, u32[]{:S(2)}) copy-start(bf16[16,128,128]{2,1,0:T(8,128)(2,1)S(1)} %collective-permute-done.6.refs_8_) | copy-start | bytes 1572868
  64.3 7.6 %collective-permute-start.5 = (bf16[8,128,128]{2,1,0:T(8,128)(2,1)S(1)}, bf16[8,128,128]{2,1,0:T(8,128)(2,1)S(1)}, u32[]{:S(2)}, u32[]{:S(2)}) collective-permute-start(bf16[8,128,128]{2,1,0:T(8,128)(2,1)S(1)} %slice.7), channel_id=1, source_target_pairs={{0,96},{16,112},{32,0},{48,16},{64,32},{80,48},{96,64},{112,80},{1... | collective-permute-start | bytes 786440 | tf_op jit(solution)/shard_map/ppermute | solution.py:38
  71.9 13.9 %collective-permute-start.10 = (bf16[16,128,128]{2,1,0:T(8,128)(2,1)}, bf16[16,128,128]{2,1,0:T(8,128)(2,1)S(1)}, u32[]{:S(2)}, u32[]{:S(2)}) collective-permute-start(bf16[16,128,128]{2,1,0:T(8,128)(2,1)} %collective-permute-done.1.refs_4_), channel_id=1, source_target_pairs={{0,32},{16,48},{32,64},{48,80},{64,96},{80,112},{96,0},{112,16},{1... | collective-permute-start | bytes 1572872 | tf_op jit(solution)/shard_map/ppermute | solution.py:38
  71.9 15.8 %collective-permute-start.11 = (bf16[16,128,128]{2,1,0:T(8,128)(2,1)}, bf16[16,128,128]{2,1,0:T(8,128)(2,1)S(1)}, u32[]{:S(2)}, u32[]{:S(2)}) collective-permute-start(bf16[16,128,128]{2,1,0:T(8,128)(2,1)} %collective-permute-done.1.refs_4_), channel_id=1, source_target_pairs={{0,96},{16,112},{32,0},{48,16},{64,32},{80,48},{96,64},{112,80},{1... | collective-permute-start | bytes 1572872 | tf_op jit(solution)/shard_map/ppermute | solution.py:38
  74.8 21.6 %copy-start.15 = (bf16[16,128,128]{2,1,0:T(8,128)(2,1)}, bf16[16,128,128]{2,1,0:T(8,128)(2,1)S(1)}, u32[]{:S(2)}) copy-start(bf16[16,128,128]{2,1,0:T(8,128)(2,1)S(1)} %collective-permute-done.7.refs_9_) | copy-start | bytes 1572868
  74.8 21.6 %copy-start.16 = (bf16[16,128,128]{2,1,0:T(8,128)(2,1)}, bf16[16,128,128]{2,1,0:T(8,128)(2,1)S(1)}, u32[]{:S(2)}) copy-start(bf16[16,128,128]{2,1,0:T(8,128)(2,1)S(1)} %collective-permute-done.8.refs_10_) | copy-start | bytes 1572868
  74.8 21.6 %copy-start.17 = (bf16[16,128,128]{2,1,0:T(8,128)(2,1)}, bf16[16,128,128]{2,1,0:T(8,128)(2,1)S(1)}, u32[]{:S(2)}) copy-start(bf16[16,128,128]{2,1,0:T(8,128)(2,1)S(1)} %collective-permute-done.9.refs_12_) | copy-start | bytes 1572868
  74.9 24.5 %copy-start.11 = (bf16[16,128,128]{2,1,0:T(8,128)(2,1)}, bf16[16,128,128]{2,1,0:T(8,128)(2,1)S(1)}, u32[]{:S(2)}) copy-start(bf16[16,128,128]{2,1,0:T(8,128)(2,1)S(1)} %constant_dynamic-update-slice_fusion.refs_3_) | copy-start | bytes 1572868
  74.9 21.5 %collective-permute-start.12 = (bf16[16,128,128]{2,1,0:T(8,128)(2,1)S(1)}, bf16[16,128,128]{2,1,0:T(8,128)(2,1)}, u32[]{:S(2)}, u32[]{:S(2)}) collective-permute-start(bf16[16,128,128]{2,1,0:T(8,128)(2,1)S(1)} %constant_dynamic-update-slice_fusion.refs_3_), channel_id=1, source_target_pairs={{0,128},{16,144},{32,160},{48,176},{64,192},{80,208},{96,224},{112... | collective-permute-start | bytes 1572872 | tf_op jit(solution)/shard_map/ppermute | solution.py:34
  75.3 22.2 %collective-permute-start.13 = (bf16[16,128,128]{2,1,0:T(8,128)(2,1)S(1)}, bf16[16,128,128]{2,1,0:T(8,128)(2,1)}, u32[]{:S(2)}, u32[]{:S(2)}) collective-permute-start(bf16[16,128,128]{2,1,0:T(8,128)(2,1)S(1)} %constant_dynamic-update-slice_fusion.refs_3_), channel_id=1, source_target_pairs={{0,16},{16,0},{32,48},{48,32},{64,80},{80,64},{96,112},{112,96},{1... | collective-permute-start | bytes 1572872 | tf_op jit(solution)/shard_map/ppermute | solution.py:30
  85.8 13.6 %copy-start.18 = (bf16[16,128,128]{2,1,0:T(8,128)(2,1)}, bf16[16,128,128]{2,1,0:T(8,128)(2,1)S(1)}, u32[]{:S(2)}) copy-start(bf16[16,128,128]{2,1,0:T(8,128)(2,1)S(1)} %collective-permute-done.10.refs_5_) | copy-start | bytes 1572868
  85.8 11.7 %collective-permute-start.14 = (bf16[16,128,128]{2,1,0:T(8,128)(2,1)S(1)}, bf16[16,128,128]{2,1,0:T(8,128)(2,1)}, u32[]{:S(2)}, u32[]{:S(2)}) collective-permute-start(bf16[16,128,128]{2,1,0:T(8,128)(2,1)S(1)} %collective-permute-done.10.refs_5_), channel_id=1, source_target_pairs={{0,16},{16,0},{32,48},{48,32},{64,80},{80,64},{96,112},{112,96},{1... | collective-permute-start | bytes 1572872 | tf_op jit(solution)/shard_map/ppermute | solution.py:30
  87.7 9.8 %collective-permute-start.15 = (bf16[16,128,128]{2,1,0:T(8,128)(2,1)S(1)}, bf16[16,128,128]{2,1,0:T(8,128)(2,1)}, u32[]{:S(2)}, u32[]{:S(2)}) collective-permute-start(bf16[16,128,128]{2,1,0:T(8,128)(2,1)S(1)} %collective-permute-done.11.refs_6_), channel_id=1, source_target_pairs={{0,16},{16,0},{32,48},{48,32},{64,80},{80,64},{96,112},{112,96},{1... | collective-permute-start | bytes 1572872 | tf_op jit(solution)/shard_map/ppermute | solution.py:30
  96.4 2.9 %collective-permute-start.16 = (bf16[16,128,128]{2,1,0:T(8,128)(2,1)}, bf16[16,128,128]{2,1,0:T(8,128)(2,1)}, u32[]{:S(2)}, u32[]{:S(2)}) collective-permute-start(bf16[16,128,128]{2,1,0:T(8,128)(2,1)} %collective-permute-done.12.refs_7_), channel_id=1, source_target_pairs={{0,16},{16,0},{32,48},{48,32},{64,80},{80,64},{96,112},{112,96},{1... | collective-permute-start | bytes 1572872 | tf_op jit(solution)/shard_map/ppermute | solution.py:30
  99.4 22.0 %copy-start.13 = (bf16[768]{0:T(1024)(128)(2,1)S(1)}, bf16[768]{0:T(1024)(128)(2,1)}, u32[]{:S(2)}) copy-start(bf16[768]{0:T(1024)(128)(2,1)} %param.27) | copy-start | bytes 4612
  112.5 23.8 %all-to-all-start.2 = ((bf16[16,48,256]{2,1,0:T(8,128)(2,1)}), bf16[16,48,256]{2,1,0:T(8,128)(2,1)S(1)}, u32[]{:S(2)}, u32[]{:S(2)}) async-start(bf16[16,48,256]{2,1,0:T(8,128)(2,1)} %shard_map.139), calls=%async_computation.2 | async-start | bytes 786432 | tf_op jit(solution)/shard_map/all_to_all | solution.py:383
  121.4 15.0 %copy-start.4 = (bf16[768,768]{1,0:T(8,128)(2,1)S(1)}, bf16[768,768]{1,0:T(8,128)(2,1)}, u32[]{:S(2)}) copy-start(bf16[768,768]{1,0:T(8,128)(2,1)} %weight_ref.3) | copy-start | bytes 3538948
  (8 other events, 38.5 us)
